TPU v7x, 32 devices: a whole 2x2x4 slice. The times are simulated.
32 devices in a mesh: dp: 8 (over z, x), psg: 4 (over y, core).
Axes of the slice: x: 2, y: 2, z: 4, core: 2. Of those that a mesh axis runs over, the one named last changes fastest.
Arguments:
- decoder_input: bfloat16 [64, 512, 768], P(('dp', 'psg')), may hold values from -6 to 6
- encoder_out: bfloat16 [64, 8, 384, 768], P('dp', 'psg'), may hold values from -6 to 6
- cotangent: bfloat16 [64, 512, 768], P(('dp', 'psg')), may hold values from -12 to 12
- task_ids: int32 [64], P(('dp', 'psg')), may hold values from 0 to 2
- passage_ids: int32 [64, 8], P('dp', 'psg'), may hold values from 0 to 2047
- target_lengths: int32 [64], P(('dp', 'psg')), may hold values from 128 to 512, as said below
- query_embed: float32 [64, 768], P('dp'), may hold values from -0.21875 to 0.21875
- passage_bank: bfloat16 [2048, 768], replicated, may hold values from -6 to 6
- self_in: bfloat16 [768, 2304], P(('dp', 'psg')), may hold values from -0.21875 to 0.21875
- self_out: bfloat16 [768, 768], P(('dp', 'psg')), may hold values from -1.75 to 1.75
- cross_query: bfloat16 [768, 768], P(('dp', 'psg')), may hold values from -0.21875 to 0.21875
- cross_keyval: bfloat16 [768, 1536], P(('dp', 'psg')), may hold values from -0.21875 to 0.21875
- cross_out: bfloat16 [768, 768], P(('dp', 'psg')), may hold values from -7 to 7
- hidden_in: bfloat16 [768, 3072], P(('dp', 'psg')), may hold values from -0.21875 to 0.21875
- hidden_output_weight: bfloat16 [3072, 768], P(('dp', 'psg')), may hold values from -0.109375 to 0.109375
- norm_gains: bfloat16 [3, 768], P(None, ('dp', 'psg')), may hold values from 0.5 to 1.5
- task_table: bfloat16 [3, 768], P(None, ('dp', 'psg')), may hold values from -6 to 6
Outputs:
- output: bfloat16 [64, 512, 768], P(('dp', 'psg'))
- input_grad: float32 [64, 512, 768], P(('dp', 'psg'))
- encoder_grad: float32 [64, 8, 384, 768], P('dp', 'psg')
- grad_self_in: float32 [768, 2304], P(('dp', 'psg'))
- grad_self_out: float32 [768, 768], P(('dp', 'psg'))
- grad_cross_query: float32 [768, 768], P(('dp', 'psg'))
- grad_cross_keyval: float32 [768, 1536], P(('dp', 'psg'))
- grad_cross_out: float32 [768, 768], P(('dp', 'psg'))
- grad_hidden_in: float32 [768, 3072], P(('dp', 'psg'))
- grad_hidden_out: float32 [3072, 768], P(('dp', 'psg'))
- grad_norm_gains: float32 [3, 768], P(None, ('dp', 'psg'))
- grad_task_table: float32 [3, 768], P(None, ('dp', 'psg'))
- query_grad: float32 [64, 768], P('dp')
Inputs may be any that keep to these rules, and one draw needn't show every extreme that they name: `target_lengths`: in each aligned block of 8 queries one query uses all 512 decoder tokens.
All inputs are finite; a program needn't handle non-finite values.
Results may differ from a plain program's by a relative error of at most 0.02.
Values may be sent and summed in bfloat16 or wider, within the bound.
A program may use at most 384 MiB of HBM per device.

v0:
```python
import jax
import jax.numpy as jnp
from jax import lax
from jax.sharding import PartitionSpec as P

H = 12
DH = 64


def gelu_tanh(tensor):
    return (
        0.5
        * tensor
        * (1.0 + jnp.tanh(0.7978845608028654 * (tensor + 0.044715 * tensor * tensor * tensor)))
    )


def rms_norm(tensor, gain_row):
    return tensor * lax.rsqrt(jnp.mean(tensor * tensor, axis=-1, keepdims=True) + 1e-06) * gain_row


def norm_back(tensor, gain_row, upstream):
    unused_value, pullback = jax.vjp(rms_norm, tensor, gain_row)
    return pullback(upstream)


def merge_softmax(earlier, later):
    biggest = jnp.maximum(earlier[0], later[0])
    return (
        biggest,
        earlier[1] * jnp.exp(earlier[0] - biggest) + later[1] * jnp.exp(later[0] - biggest),
    )


def cross_scores(queries_one, keys_one):
    return (
        jnp.einsum("ihd,jhd->hij", queries_one, keys_one, preferred_element_type=jnp.float32)
        * 0.125
    )


def softmax_weights(scores_row):
    biggest = jnp.max(scores_row, axis=-1, keepdims=True)
    exponent = jnp.exp(scores_row - biggest)
    return exponent / jnp.sum(exponent, axis=-1, keepdims=True)


def on_device(
    decoder_input,
    encoder_out,
    cotangent,
    task_ids,
    passage_ids,
    target_lengths,
    query_embed,
    passage_bank,
    self_in,
    self_out,
    cross_query,
    cross_keyval,
    cross_out,
    hidden_in,
    hidden_output_weight,
    norm_gains,
    task_table,
):
    shards = (
        self_in,
        self_out,
        cross_query,
        cross_keyval,
        cross_out,
        hidden_in,
        hidden_output_weight,
        norm_gains,
        task_table,
    )
    gathered = (
        lax.all_gather(shards[0], ("dp", "psg"), axis=0, tiled=True),
        lax.all_gather(shards[1], ("dp", "psg"), axis=0, tiled=True),
        lax.all_gather(shards[2], ("dp", "psg"), axis=0, tiled=True),
        lax.all_gather(shards[3], ("dp", "psg"), axis=0, tiled=True),
        lax.all_gather(shards[4], ("dp", "psg"), axis=0, tiled=True),
        lax.all_gather(shards[5], ("dp", "psg"), axis=0, tiled=True),
        lax.all_gather(shards[6], ("dp", "psg"), axis=0, tiled=True),
        lax.all_gather(shards[7], ("dp", "psg"), axis=1, tiled=True),
        lax.all_gather(shards[8], ("dp", "psg"), axis=1, tiled=True),
    )
    (
        w_self_in,
        w_self_out,
        w_cross_query,
        w_cross_keyval,
        w_cross_out,
        w_hidden_in,
        w_hidden_out,
        gains,
        table,
    ) = gathered
    local_count, seq_len, model_width = decoder_input.shape
    group_count = encoder_out.shape[0]
    passages_here = encoder_out.shape[1]
    tokens_each = encoder_out.shape[2]
    key_count = passages_here * tokens_each
    group_size = lax.axis_size("psg")
    gain_rows = gains.astype(jnp.float32)
    choose = (task_ids[:, None] == jnp.arange(table.shape[0], dtype=jnp.int32)[None, :]).astype(
        jnp.bfloat16
    )
    task_rows = jnp.dot(choose, table, preferred_element_type=jnp.float32)
    stream = decoder_input.astype(jnp.float32) + task_rows[:, None, :]
    normed_one = rms_norm(stream, gain_rows[0]).astype(jnp.bfloat16)
    qkv_rows = jnp.einsum(
        "qrd,de->qre", normed_one, w_self_in, preferred_element_type=jnp.float32
    ).astype(jnp.bfloat16)
    qkv_heads = qkv_rows.reshape(local_count, seq_len, 3, H, DH)
    self_queries = qkv_heads[:, :, 0]
    self_keys = qkv_heads[:, :, 1]
    self_values = qkv_heads[:, :, 2]
    row_pos = lax.broadcasted_iota(jnp.int32, (seq_len, seq_len), 0)
    col_pos = lax.broadcasted_iota(jnp.int32, (seq_len, seq_len), 1)
    allowed = (col_pos[None] <= row_pos[None]) & (col_pos[None] < target_lengths[:, None, None])

    def self_scores_of():
        raw_scores = (
            jnp.einsum(
                "qihd,qjhd->qhij", self_queries, self_keys, preferred_element_type=jnp.float32
            )
            * 0.125
        )
        return jnp.where(allowed[:, None], raw_scores, -1e30)

    self_scores = self_scores_of()
    self_max = jnp.max(self_scores, axis=-1, keepdims=True)
    self_exp = jnp.exp(self_scores - self_max)
    self_sum = jnp.sum(self_exp, axis=-1, keepdims=True)
    self_probs = self_exp / self_sum
    self_att = jnp.einsum(
        "qhij,qjhd->qihd",
        self_probs.astype(jnp.bfloat16),
        self_values,
        preferred_element_type=jnp.float32,
    )
    self_att = self_att.reshape(local_count, seq_len, model_width).astype(jnp.bfloat16)
    middle = stream + jnp.einsum(
        "qrd,de->qre", self_att, w_self_out, preferred_element_type=jnp.float32
    )
    normed_two = rms_norm(middle, gain_rows[1]).astype(jnp.bfloat16)
    cross_local = jnp.einsum(
        "qrd,de->qre", normed_two, w_cross_query, preferred_element_type=jnp.float32
    ).astype(jnp.bfloat16)
    enc_rows = encoder_out.reshape(group_count, key_count, model_width)
    cross_kv = jnp.einsum(
        "qkd,de->qke", enc_rows, w_cross_keyval, preferred_element_type=jnp.float32
    ).astype(jnp.bfloat16)
    owner_kv = lax.all_to_all(cross_kv, "psg", split_axis=0, concat_axis=1, tiled=True)
    owner_heads = owner_kv.reshape(local_count, group_size, key_count, 2, H, DH)
    own_queries = cross_local.reshape(local_count, seq_len, H, DH)

    def owner_forward(packed):
        queries_one, blocks_one = packed

        def stat_step(carry, block):
            scores = cross_scores(queries_one, block[:, 0])
            biggest = jnp.max(scores, axis=-1)
            summed = jnp.sum(jnp.exp(scores - biggest[..., None]), axis=-1)
            return (merge_softmax(carry, (biggest, summed)), None)

        start = (jnp.full((H, seq_len), -1e30, jnp.float32), jnp.zeros((H, seq_len), jnp.float32))
        (row_max, row_sum), unused_stat = lax.scan(stat_step, start, blocks_one)

        def value_step(carry, block):
            weights_one = (
                jnp.exp(cross_scores(queries_one, block[:, 0]) - row_max[..., None])
                / row_sum[..., None]
            )
            carry = carry + jnp.einsum(
                "hij,jhd->ihd",
                weights_one.astype(jnp.bfloat16),
                block[:, 1],
                preferred_element_type=jnp.float32,
            )
            shares = jnp.sum(
                weights_one.reshape(H, seq_len, passages_here, tokens_each), axis=(0, 1, 3)
            ) / (H * seq_len)
            return (carry, shares)

        numer, shares = lax.scan(value_step, jnp.zeros((seq_len, H, DH), jnp.float32), blocks_one)
        return (numer.reshape(seq_len, model_width), shares.reshape(-1), row_max, row_sum)

    cross_sum, mass_rows, own_max, own_sum = lax.map(owner_forward, (own_queries, owner_heads))
    cross_att = cross_sum.astype(jnp.bfloat16)
    latter = middle + jnp.einsum(
        "qrd,de->qre", cross_att, w_cross_out, preferred_element_type=jnp.float32
    )
    normed_three = rms_norm(latter, gain_rows[2]).astype(jnp.bfloat16)
    hidden_pre = jnp.einsum(
        "qrd,df->qrf", normed_three, w_hidden_in, preferred_element_type=jnp.float32
    )
    activated = gelu_tanh(hidden_pre).astype(jnp.bfloat16)
    output = (
        latter
        + jnp.einsum("qrf,fd->qrd", activated, w_hidden_out, preferred_element_type=jnp.float32)
    ).astype(jnp.bfloat16)
    regathered = (
        lax.all_gather(shards[0], ("dp", "psg"), axis=0, tiled=True),
        lax.all_gather(shards[1], ("dp", "psg"), axis=0, tiled=True),
        lax.all_gather(shards[2], ("dp", "psg"), axis=0, tiled=True),
        lax.all_gather(shards[3], ("dp", "psg"), axis=0, tiled=True),
        lax.all_gather(shards[4], ("dp", "psg"), axis=0, tiled=True),
        lax.all_gather(shards[5], ("dp", "psg"), axis=0, tiled=True),
        lax.all_gather(shards[6], ("dp", "psg"), axis=0, tiled=True),
        lax.all_gather(shards[7], ("dp", "psg"), axis=1, tiled=True),
        lax.all_gather(shards[8], ("dp", "psg"), axis=1, tiled=True),
    )
    (
        backward_self_input,
        back_self_out,
        back_cross_query,
        back_cross_keyval,
        back_cross_out,
        back_hidden_in,
        back_hidden_out,
    ) = regathered[:7]
    gain_back = regathered[7].astype(jnp.float32)
    upstream = cotangent.astype(jnp.float32)
    grad_hidden_out = jnp.einsum(
        "qrf,qrd->fd", activated, cotangent, preferred_element_type=jnp.float32
    )
    grad_activ = jnp.einsum(
        "qrd,fd->qrf", cotangent, back_hidden_out, preferred_element_type=jnp.float32
    )
    unused_gelu, gelu_pull = jax.vjp(gelu_tanh, hidden_pre)
    grad_pre = gelu_pull(grad_activ)[0].astype(jnp.bfloat16)
    grad_hidden_in = jnp.einsum(
        "qrd,qrf->df", normed_three, grad_pre, preferred_element_type=jnp.float32
    )
    grad_normed_three = jnp.einsum(
        "qrf,df->qrd", grad_pre, back_hidden_in, preferred_element_type=jnp.float32
    )
    grad_latter, gain_grad_three = norm_back(latter, gain_back[2], grad_normed_three)
    grad_latter = grad_latter + upstream
    grad_cross_part = grad_latter.astype(jnp.bfloat16)
    grad_cross_out = jnp.einsum(
        "qrd,qre->de", cross_att, grad_cross_part, preferred_element_type=jnp.float32
    )
    grad_catt = jnp.einsum(
        "qre,de->qrd", grad_cross_part, back_cross_out, preferred_element_type=jnp.float32
    ).astype(jnp.bfloat16)
    row_delta = jnp.sum(
        (grad_catt.astype(jnp.float32) * cross_sum).reshape(local_count, seq_len, H, DH), axis=-1
    )
    row_delta = jnp.swapaxes(row_delta, 1, 2)
    embeds = jnp.take(passage_bank, passage_ids, axis=0).astype(jnp.float32)
    score_local = jnp.einsum("qe,qpe->qp", query_embed, embeds, precision=lax.Precision.HIGHEST)

    def owner_backward(packed):
        queries_one, blocks_one, row_max, row_sum, grad_one, delta_one = packed
        grad_heads = grad_one.reshape(seq_len, H, DH)

        def grad_step(carry, block):
            keys_one = block[:, 0]
            values_one = block[:, 1]
            weights_one = (
                jnp.exp(cross_scores(queries_one, keys_one) - row_max[..., None])
                / row_sum[..., None]
            )
            grad_weights = jnp.einsum(
                "ihd,jhd->hij", grad_heads, values_one, preferred_element_type=jnp.float32
            )
            grad_scores = (weights_one * (grad_weights - delta_one[..., None])).astype(jnp.bfloat16)
            carry = (
                carry
                + jnp.einsum(
                    "hij,jhd->ihd", grad_scores, keys_one, preferred_element_type=jnp.float32
                )
                * 0.125
            )
            grad_keys = (
                jnp.einsum(
                    "hij,ihd->jhd", grad_scores, queries_one, preferred_element_type=jnp.float32
                )
                * 0.125
            )
            grad_values = jnp.einsum(
                "hij,ihd->jhd",
                weights_one.astype(jnp.bfloat16),
                grad_heads,
                preferred_element_type=jnp.float32,
            )
            grad_pair = (
                jnp.stack([grad_keys, grad_values], axis=1)
                .reshape(key_count, 2 * model_width)
                .astype(jnp.bfloat16)
            )
            return (carry, grad_pair)

        total, pairs = lax.scan(grad_step, jnp.zeros((seq_len, H, DH), jnp.float32), blocks_one)
        return (total.reshape(seq_len, model_width), pairs.reshape(-1, 2 * model_width))

    owner_q, owner_pairs = lax.map(
        owner_backward, (own_queries, owner_heads, own_max, own_sum, grad_catt, row_delta)
    )
    grad_cross_q = owner_q.astype(jnp.bfloat16)
    grad_pairs = lax.all_to_all(owner_pairs, "psg", split_axis=1, concat_axis=0, tiled=True)
    mass_all, score_all = (
        lax.all_gather(mass_rows, "psg", axis=0, tiled=True),
        lax.all_gather(score_local, "psg", axis=1, tiled=True),
    )
    grad_cross_query = jnp.einsum(
        "qrd,qre->de", normed_two, grad_cross_q, preferred_element_type=jnp.float32
    )
    grad_normed_two = jnp.einsum(
        "qre,de->qrd", grad_cross_q, back_cross_query, preferred_element_type=jnp.float32
    )
    grad_cross_keyval = jnp.einsum(
        "qkd,qke->de", enc_rows, grad_pairs, preferred_element_type=jnp.float32
    )
    encoder_grad = jnp.einsum(
        "qke,de->qkd", grad_pairs, back_cross_keyval, preferred_element_type=jnp.float32
    ).reshape(encoder_out.shape)
    grad_middle, gain_grad_two = norm_back(middle, gain_back[1], grad_normed_two)
    grad_middle = grad_middle + grad_latter
    grad_self_part = grad_middle.astype(jnp.bfloat16)
    grad_self_out = jnp.einsum(
        "qrd,qre->de", self_att, grad_self_part, preferred_element_type=jnp.float32
    )
    grad_satt = jnp.einsum(
        "qre,de->qrd", grad_self_part, back_self_out, preferred_element_type=jnp.float32
    ).astype(jnp.bfloat16)
    grad_satt = grad_satt.reshape(local_count, seq_len, H, DH)
    probs_again = jnp.exp(self_scores_of() - self_max) / self_sum
    self_dp = jnp.einsum(
        "qihd,qjhd->qhij", grad_satt, self_values, preferred_element_type=jnp.float32
    )
    self_delta = jnp.sum(probs_again * self_dp, axis=-1, keepdims=True)
    self_score_gradient = (probs_again * (self_dp - self_delta)).astype(jnp.bfloat16)
    self_query_gradient = (
        jnp.einsum(
            "qhij,qjhd->qihd", self_score_gradient, self_keys, preferred_element_type=jnp.float32
        )
        * 0.125
    )
    self_key_gradient = (
        jnp.einsum(
            "qhij,qihd->qjhd", self_score_gradient, self_queries, preferred_element_type=jnp.float32
        )
        * 0.125
    )
    self_value_gradient = jnp.einsum(
        "qhij,qihd->qjhd",
        probs_again.astype(jnp.bfloat16),
        grad_satt,
        preferred_element_type=jnp.float32,
    )
    grad_qkv = (
        jnp.stack([self_query_gradient, self_key_gradient, self_value_gradient], axis=2)
        .reshape(local_count, seq_len, 3 * model_width)
        .astype(jnp.bfloat16)
    )
    grad_self_in = jnp.einsum(
        "qrd,qre->de", normed_one, grad_qkv, preferred_element_type=jnp.float32
    )
    grad_normed_one = jnp.einsum(
        "qre,de->qrd", grad_qkv, backward_self_input, preferred_element_type=jnp.float32
    )
    grad_stream, gain_grad_one = norm_back(stream, gain_back[0], grad_normed_one)
    input_grad = grad_stream + grad_middle
    grad_table = jnp.dot(
        choose.astype(jnp.float32).T, jnp.sum(input_grad, axis=1), precision=lax.Precision.HIGHEST
    )
    gain_grads = jnp.stack([gain_grad_one, gain_grad_two, gain_grad_three])
    summed_grads = (
        lax.psum_scatter(grad_self_in, ("dp", "psg"), scatter_dimension=0, tiled=True),
        lax.psum_scatter(grad_self_out, ("dp", "psg"), scatter_dimension=0, tiled=True),
        lax.psum_scatter(grad_cross_query, ("dp", "psg"), scatter_dimension=0, tiled=True),
        lax.psum_scatter(grad_cross_keyval, ("dp", "psg"), scatter_dimension=0, tiled=True),
        lax.psum_scatter(grad_cross_out, ("dp", "psg"), scatter_dimension=0, tiled=True),
        lax.psum_scatter(grad_hidden_in, ("dp", "psg"), scatter_dimension=0, tiled=True),
        lax.psum_scatter(grad_hidden_out, ("dp", "psg"), scatter_dimension=0, tiled=True),
        lax.psum_scatter(gain_grads, ("dp", "psg"), scatter_dimension=1, tiled=True),
        lax.psum_scatter(grad_table, ("dp", "psg"), scatter_dimension=1, tiled=True),
    )
    weights_all = softmax_weights(score_all) - mass_all
    own_share = lax.dynamic_slice_in_dim(
        weights_all, lax.axis_index("psg") * passages_here, passages_here, 1
    )
    query_grad = lax.psum(
        jnp.einsum("qp,qpe->qe", own_share, embeds, precision=lax.Precision.HIGHEST), "psg"
    )
    return (
        output,
        input_grad,
        encoder_grad,
        summed_grads[0],
        summed_grads[1],
        summed_grads[2],
        summed_grads[3],
        summed_grads[4],
        summed_grads[5],
        summed_grads[6],
        summed_grads[7],
        summed_grads[8],
        query_grad,
    )


def solution(mesh):
    placed = (
        P(("dp", "psg"), None, None),
        P("dp", "psg", None, None),
        P(("dp", "psg"), None, None),
        P(("dp", "psg")),
        P("dp", "psg"),
        P(("dp", "psg")),
        P("dp", None),
        P(),
        P(("dp", "psg"), None),
        P(("dp", "psg"), None),
        P(("dp", "psg"), None),
        P(("dp", "psg"), None),
        P(("dp", "psg"), None),
        P(("dp", "psg"), None),
        P(("dp", "psg"), None),
        P(None, ("dp", "psg")),
        P(None, ("dp", "psg")),
    )
    return jax.shard_map(
        on_device,
        mesh=mesh,
        in_specs=placed,
        out_specs=(
            P(("dp", "psg"), None, None),
            P(("dp", "psg"), None, None),
            P("dp", "psg", None, None),
            P(("dp", "psg"), None),
            P(("dp", "psg"), None),
            P(("dp", "psg"), None),
            P(("dp", "psg"), None),
            P(("dp", "psg"), None),
            P(("dp", "psg"), None),
            P(("dp", "psg"), None),
            P(None, ("dp", "psg")),
            P(None, ("dp", "psg")),
            P("dp", None),
        ),
        check_vma=False,
    )
```

profile of v0, /device:TPU:0, one launch (start us, length us, event | category | flops | bytes accessed | tf_op | source)
XLA Modules:
  0.0 2137.6 jit_solution(14230082692794584256)
XLA Ops:
  11.2 59.8 %all-gather.16.cloned.1.call-done = bf16[768,1536]{1,0:T(8,128)(2,1)} async-done(((bf16[24,1536]{1,0:T(8,128)(2,1)}), bf16[768,1536]{1,0:T(8,128)(2,1)}) %all-gather.16.cloned.1.call-update) | async-done | bytes 2359312 | tf_op jit(solution)/shard_map/all_gather | solution.py:82
  71.0 20.6 convolution_convert_fusion
  100.0 251.8 %all-gather.1 = bf16[32,24,3]{1,2,0:T(4,128)(2,1)S(1)} all-gather(bf16[1,24,3]{1,2,0:T(4,128)(2,1)S(1)} %bitcast.383), channel_id=1, replica_groups=mesh['dp'=8,'psg'=4] {'dp','psg'}, dimensions={0}, use_global_device_ids=true | all-gather | bytes 4752 | tf_op jit(solution)/shard_map/all_gather | solution.py:86
  352.1 36.8 %all-gather = bf16[32,24,3]{1,2,0:T(4,128)(2,1)S(1)} all-gather(bf16[1,24,3]{1,2,0:T(4,128)(2,1)S(1)} %bitcast.384), channel_id=1, replica_groups=mesh['dp'=8,'psg'=4] {'dp','psg'}, dimensions={0}, use_global_device_ids=true | all-gather | bytes 4752 | tf_op jit(solution)/shard_map/all_gather | solution.py:87
  410.5 15.5 fusion.106
  451.4 24.6 %copy.178 = bf16[2,4,768,1536]{2,3,1,0:T(8,128)(2,1)} copy(bf16[2,4,768,1536]{3,2,0,1:T(8,128)(2,1)} %bitcast.29) | data formatting | bytes 37748736 | tf_op jit(solution)/shard_map/all_to_all | solution.py:156
  476.0 289.5 %while.77 = (s32[]{:T(128)}, f32[2,512,768]{1,2,0:T(8,128)}, f32[2,8]{1,0:T(2,128)}, f32[2,12,512]{2,1,0:T(8,128)}, f32[2,12,512]{2,1,0:T(8,128)}, /*index=5*/bf...) while((s32[]{:T(128)}, f32[2,512,768]{1,2,0:T(8,128)}, ...), condition=%wide.region_13.14_spmd.clone, body=%wide.region_4.13_spmd.sunk.clone | while | flops 1859948544 | bytes 105420160 | solution.py:191
  487.0 77.4 %while.75 = (s32[]{:T(128)}, f32[12,512]{1,0:T(8,128)S(1)}, f32[12,512]{1,0:T(8,128)S(1)}, bf16[4,768,2,12,64]{1,4,3,2,0:T(8,128)(2,1)}, bf16[512,12,64]{0,2,1:T(8,128)(2,1)}, /*index=5*/s32[]{:T(128)}, s32[]{:T(128)}) while((s32[]{:T(128)}, f32[12,512]{1,0:T(8,128)S(1)}, f32[12,512]{1,0:T(8,128)S(1)}, ...), condition=%wide.region_8.8_spmd.clone, body=%wide.region_5.7_spmd.clone.sunk | while | flops 627609600 | bytes 47800444 | solution.py:170
  564.4 53.6 %while.76 = (s32[]{:T(128)}, f32[512,12,64]{0,2,1:T(8,128)}, f32[4,2]{1,0:T(4,128)S(1)}, bf16[4,768,2,12,64]{1,4,3,2,0:T(8,128)(2,1)}, bf16[512,12,64]{0,2,1:T(8...) while((s32[]{:T(128)}, f32[512,12,64]{0,2,1:T(8,128)}, ...), condition=%wide.region_12.12_spmd.clone, body=%wide.region_9.11_spmd.clone.sunk | while | flops 1232338944 | bytes 33108164 | solution.py:188
  631.5 77.4 %while.75 = (s32[]{:T(128)}, f32[12,512]{1,0:T(8,128)S(1)}, f32[12,512]{1,0:T(8,128)S(1)}, bf16[4,768,2,12,64]{1,4,3,2,0:T(8,128)(2,1)}, bf16[512,12,64]{0,2,1:T(8,128)(2,1)}, /*index=5*/s32[]{:T(128)}, s32[]{:T(128)}) while((s32[]{:T(128)}, f32[12,512]{1,0:T(8,128)S(1)}, f32[12,512]{1,0:T(8,128)S(1)}, ...), condition=%wide.region_8.8_spmd.clone, body=%wide.region_5.7_spmd.clone.sunk | while | flops 627609600 | bytes 47800444 | solution.py:170
  709.0 53.6 %while.76 = (s32[]{:T(128)}, f32[512,12,64]{0,2,1:T(8,128)}, f32[4,2]{1,0:T(4,128)S(1)}, bf16[4,768,2,12,64]{1,4,3,2,0:T(8,128)(2,1)}, bf16[512,12,64]{0,2,1:T(8...) while((s32[]{:T(128)}, f32[512,12,64]{0,2,1:T(8,128)}, ...), condition=%wide.region_12.12_spmd.clone, body=%wide.region_9.11_spmd.clone.sunk | while | flops 1232338944 | bytes 33108164 | solution.py:188
  786.6 16.9 fusion.22
  827.8 515.3 %while.79 = (s32[]{:T(128)}, bf16[2,512,768]{1,2,0:T(8,128)(2,1)}, bf16[2,3072,1536]{2,1,0:T(8,128)(2,1)}, bf16[2,4,768,2,12,64]{2,5,4,3,1,0:T(8,128)(2,1)}, bf1...) while((s32[]{:T(128)}, bf16[2,512,768]{1,2,0:T(8,128)(2,1)}, ...), condition=%wide.region_20.21_spmd.clone, body=%wide.region_17.20_spmd.sunk.clone | while | flops 3057057792 | bytes 220439152 | solution.py:301
  844.8 230.7 %while.78 = (s32[]{:T(128)}, f32[512,12,64]{0,2,1:T(8,128)}, bf16[4,768,1536]{2,1,0:T(8,128)(2,1)}, bf16[4,768,2,12,64]{1,4,3,2,0:T(8,128)(2,1)}, bf16[512,12,64...) while((s32[]{:T(128)}, f32[512,12,64]{0,2,1:T(8,128)}, ...), condition=%wide.region_19.19_spmd.clone, body=%wide.region_18.18_spmd.clone.sunk | while | flops 3057057792 | bytes 174285104 | solution.py:298
  867.5 13.5 multiply_convert_fusion.18
  924.9 13.3 multiply_convert_fusion.18
  982.6 13.3 multiply_convert_fusion.18
  1040.2 13.3 multiply_convert_fusion.18
  1102.4 230.1 %while.78 = (s32[]{:T(128)}, f32[512,12,64]{0,2,1:T(8,128)}, bf16[4,768,1536]{2,1,0:T(8,128)(2,1)}, bf16[4,768,2,12,64]{1,4,3,2,0:T(8,128)(2,1)}, bf16[512,12,64...) while((s32[]{:T(128)}, f32[512,12,64]{0,2,1:T(8,128)}, ...), condition=%wide.region_19.19_spmd.clone, body=%wide.region_18.18_spmd.clone.sunk | while | flops 3057057792 | bytes 174285104 | solution.py:298
  1181.9 13.3 multiply_convert_fusion.18
  1297.2 13.3 multiply_convert_fusion.18
  1361.8 17.8 multiply_reduce_fusion
  1379.7 23.7 %multiply_convert_fusion.2 = bf16[2,12,512,512]{2,3,1,0:T(8,128)(2,1)} fusion(f32[2,12,512,512]{2,3,1,0:T(8,128)} %get-tuple-element.518, f32[2,12,512]{2,1,0:T(8,128)S(1)} %get-tuple-element.517, f32[2,12,512,512]{2,3,1,0:T(8,128)} %get-tuple-element.508, f32[2,12,512]{2,1,0:T(8,128)S(1)} %copy-done.30), kind=kLoop, calls=%fused_computation.47 | loop fusion | flops 25165824 | bytes 63012864 | tf_op jit(solution)/shard_map/convert_element_type | solution.py:337
  1425.0 13.8 fusion.64
  1462.2 34.8 %copy.191 = bf16[2,3072,1536]{2,0,1:T(2,128)(2,1)} copy(bf16[2,3072,1536]{2,1,0:T(8,128)(2,1)} %get-tuple-element.219) | data formatting | bytes 37748736 | tf_op jit(solution)/shard_map/while | solution.py:301
  1519.5 218.7 %all-gather.2 = f32[4,2,8]{2,1,0:T(2,128)S(1)} all-gather(f32[1,2,8]{2,1,0:T(2,128)S(1)} %bitcast.382), channel_id=1, replica_groups=mesh['dp'=8,'psg'=4] {'psg'}, dimensions={0}, use_global_device_ids=true | all-gather | bytes 320 | tf_op jit(solution)/shard_map/all_gather | solution.py:308
  1753.7 46.0 %copy.224 = bf16[2,4,768,1536]{2,3,0,1:T(8,128)(2,1)} copy(bf16[2,4,768,1536]{3,0,2,1:T(2,128)(2,1)} %bitcast.46) | data formatting | bytes 37748736 | tf_op jit(solution)/shard_map/all_to_all | solution.py:305
  1799.7 21.2 convolution_bitcast_fusion.3
  1834.3 38.3 %all-reduce.2 = (f32[3,768]{1,0:T(4,128)S(1)}, f32[3,768]{1,0:T(4,128)S(1)}) all-reduce(f32[3,768]{1,0:T(4,128)S(1)} %pad_maximum_fusion.2, f32[3,768]{1,0:T(4,128)S(1)} %fusion.95), channel_id=9, replica_groups=mesh['dp'=8,'psg'=4] {'dp','psg'}, use_global_device_ids=true, to_apply=%region_34.35.clone | all-reduce | flops 4608 | bytes 36864
  1909.9 20.3 fusion.52
  1930.3 88.6 %reduce-scatter.22.cloned.1.call-done = f32[96,768]{1,0:T(8,128)} async-done(((f32[3072,768]{1,0:T(8,128)}), f32[96,768]{1,0:T(8,128)}) %reduce-scatter.22.cloned.1.call-update) | async-done | bytes 294928 | tf_op jit(solution)/shard_map/reduce_scatter | solution.py:380
  2018.9 112.0 %reduce-scatter.24.cloned.1.call-done = f32[24,1536]{1,0:T(8,128)} async-done(((f32[768,1536]{1,0:T(8,128)}), f32[24,1536]{1,0:T(8,128)}) %reduce-scatter.24.cloned.1.call-update) | async-done | bytes 147472
  (552 shorter events, 979.9 us)
Async XLA Ops:
  7.2 1511.2 %copy-start = (bf16[2048,768]{1,0:T(8,128)(2,1)S(1)}, bf16[2048,768]{1,0:T(8,128)(2,1)}, u32[]{:S(2)}) copy-start(bf16[2048,768]{1,0:T(8,128)(2,1)} %param.34) | copy-start | bytes 9437188
  7.2 63.8 %all-gather.16.cloned.1.call-start = ((), (), s32[]{:S(2)}) async-start(), calls=%async_computation.11 | async-start | bytes 2433024 | tf_op jit(solution)/shard_map/all_gather | solution.py:82
  7.9 387.0 %all-gather.12.cloned.1.call-start = ((), (), s32[]{:S(2)}) async-start(), calls=%async_computation.9 | async-start | bytes 3649536 | tf_op jit(solution)/shard_map/all_gather | solution.py:79
  8.7 429.6 %all-gather.14.cloned.1.call-start = ((), (), s32[]{:S(2)}) async-start(), calls=%async_computation.10 | async-start | bytes 1216512 | tf_op jit(solution)/shard_map/all_gather | solution.py:80
  9.4 434.5 %all-gather.18.cloned.1.call-start = ((), (), s32[]{:S(2)}) async-start(), calls=%async_computation.12 | async-start | bytes 1216512 | tf_op jit(solution)/shard_map/all_gather | solution.py:81
  10.0 759.1 %all-gather.20.cloned.1.call-start = ((), (), s32[]{:S(2)}) async-start(), calls=%async_computation.13 | async-start | bytes 1216512 | tf_op jit(solution)/shard_map/all_gather | solution.py:83
  10.6 764.9 %all-gather.22.cloned.1.call-start = ((), (), s32[]{:S(2)}) async-start(), calls=%async_computation.14 | async-start | bytes 4866048 | tf_op jit(solution)/shard_map/all_gather | solution.py:84
  91.5 260.6 %copy-start.48 = (bf16[3,24]{1,0:T(4,128)(2,1)S(1)}, bf16[3,24]{1,0:T(4,128)(2,1)}, u32[]{:S(2)}) copy-start(bf16[3,24]{1,0:T(4,128)(2,1)} %param.43) | copy-start | bytes 436
  91.5 299.4 %copy-start.57 = (s32[2]{0:T(128)S(1)}, s32[2]{0:T(128)}, u32[]{:S(2)}) copy-start(s32[2]{0:T(128)} %param.30) | copy-start | bytes 28
  91.6 359.8 %all-to-all-start = ((bf16[8,768,1536]{2,1,0:T(8,128)(2,1)}), bf16[8,768,1536]{2,1,0:T(8,128)(2,1)}, u32[]{:S(2)}, u32[]{:S(2)}) async-start(bf16[8,768,1536]{2,1,0:T(8,128)(2,1)} %convolution_convert_fusion), calls=%async_computation | async-start | bytes 37748736 | tf_op jit(solution)/shard_map/all_to_all | solution.py:156
  99.1 294.5 %copy-start.53 = (s32[2]{0:T(128)S(1)}, s32[2]{0:T(128)}, u32[]{:S(2)}) copy-start(s32[2]{0:T(128)} %param.32) | copy-start | bytes 28
  99.2 687.4 %all-gather.24.cloned.1.call-start = ((), (), s32[]{:S(2)}) async-start(), calls=%async_computation.15 | async-start | bytes 4866048 | tf_op jit(solution)/shard_map/all_gather | solution.py:85
  99.9 1830.3 %reduce-scatter.18.cloned.1.call-start = ((), (), s32[]{:S(2)}) async-start(), calls=%async_computation.19 | async-start | bytes 2433024 | tf_op jit(solution)/shard_map/reduce_scatter | solution.py:378
  389.6 54.3 %copy-start.37 = (f32[768]{0:T(1024)}, f32[768]{0:T(1024)S(1)}, u32[]{:S(2)}) copy-start(f32[768]{0:T(1024)S(1)} %get-tuple-element.417) | copy-start | bytes 9220
  391.2 47.1 %copy-start.33 = (f32[2,768]{1,0:T(2,128)}, f32[2,768]{1,0:T(2,128)S(1)}, u32[]{:S(2)}) copy-start(f32[2,768]{1,0:T(2,128)S(1)} %fusion.96) | copy-start | bytes 18436
  564.4 53.7 %copy-start.49 = (f32[2,8]{1,0:T(2,128)S(1)}, f32[2,8]{1,0:T(2,128)}, u32[]{:S(2)}) copy-start(f32[2,8]{1,0:T(2,128)} %get-tuple-element.991) | copy-start | bytes 196 | tf_op jit(solution)/shard_map/while
  564.4 53.7 %copy-start.23 = (f32[2,12,512]{2,1,0:T(8,128)S(1)}, f32[2,12,512]{2,1,0:T(8,128)}, u32[]{:S(2)}) copy-start(f32[2,12,512]{2,1,0:T(8,128)} %get-tuple-element.992) | copy-start | bytes 147460 | tf_op jit(solution)/shard_map/while
  564.4 53.7 %copy-start.25 = (f32[2,12,512]{2,1,0:T(8,128)S(1)}, f32[2,12,512]{2,1,0:T(8,128)}, u32[]{:S(2)}) copy-start(f32[2,12,512]{2,1,0:T(8,128)} %get-tuple-element.993) | copy-start | bytes 147460 | tf_op jit(solution)/shard_map/while
  708.9 53.7 %copy-start.49 = (f32[2,8]{1,0:T(2,128)S(1)}, f32[2,8]{1,0:T(2,128)}, u32[]{:S(2)}) copy-start(f32[2,8]{1,0:T(2,128)} %get-tuple-element.991) | copy-start | bytes 196 | tf_op jit(solution)/shard_map/while
  708.9 53.7 %copy-start.23 = (f32[2,12,512]{2,1,0:T(8,128)S(1)}, f32[2,12,512]{2,1,0:T(8,128)}, u32[]{:S(2)}) copy-start(f32[2,12,512]{2,1,0:T(8,128)} %get-tuple-element.992) | copy-start | bytes 147460 | tf_op jit(solution)/shard_map/while
  709.0 53.7 %copy-start.25 = (f32[2,12,512]{2,1,0:T(8,128)S(1)}, f32[2,12,512]{2,1,0:T(8,128)}, u32[]{:S(2)}) copy-start(f32[2,12,512]{2,1,0:T(8,128)} %get-tuple-element.993) | copy-start | bytes 147460 | tf_op jit(solution)/shard_map/while
  775.4 34.1 %copy-start.27 = (f32[2,512]{1,0:T(2,128)}, f32[2,512]{1,0:T(2,128)S(1)}, u32[]{:S(2)}) copy-start(f32[2,512]{1,0:T(2,128)S(1)} %fusion.94) | copy-start | bytes 12292
  814.9 1115.3 %reduce-scatter.16.cloned.1.call-start = ((), (), s32[]{:S(2)}) async-start(), calls=%async_computation.18 | async-start | bytes 2433024 | tf_op jit(solution)/shard_map/reduce_scatter | solution.py:376
  827.8 515.4 %copy-start.36 = (f32[2,512]{1,0:T(2,128)S(1)}, f32[2,512]{1,0:T(2,128)}, u32[]{:S(2)}) copy-start(f32[2,512]{1,0:T(2,128)} %copy-done.35) | copy-start | bytes 12292
  827.8 515.4 %copy-start.38 = (f32[768]{0:T(1024)S(1)}, f32[768]{0:T(1024)}, u32[]{:S(2)}) copy-start(f32[768]{0:T(1024)} %copy-done.37) | copy-start | bytes 9220
  1379.7 550.6 %reduce-scatter.14.cloned.1.call-start = ((), (), s32[]{:S(2)}) async-start(), calls=%async_computation.17 | async-start | bytes 2433024 | tf_op jit(solution)/shard_map/reduce_scatter | solution.py:375
  1424.9 505.3 %reduce-scatter.12.cloned.1.call-start = ((), (), s32[]{:S(2)}) async-start(), calls=%async_computation.16 | async-start | bytes 7299072 | tf_op jit(solution)/shard_map/reduce_scatter | solution.py:374
  1450.6 479.7 %reduce-scatter.20.cloned.1.call-start = ((), (), s32[]{:S(2)}) async-start(), calls=%async_computation.20 | async-start | bytes 9732096 | tf_op jit(solution)/shard_map/reduce_scatter | solution.py:379
  1496.9 256.8 %all-to-all-start.1 = ((bf16[2,3072,1536]{2,0,1:T(2,128)(2,1)}), bf16[2,3072,1536]{2,0,1:T(2,128)(2,1)}, u32[]{:S(2)}, u32[]{:S(2)}) async-start(bf16[2,3072,1536]{2,0,1:T(2,128)(2,1)} %copy.191), calls=%async_computation.1 | async-start | bytes 37748736 | tf_op jit(solution)/shard_map/all_to_all | solution.py:305
  1504.4 514.5 %reduce-scatter.22.cloned.1.call-start = ((), (), s32[]{:S(2)}) async-start(), calls=%async_computation.21 | async-start | bytes 9732096 | tf_op jit(solution)/shard_map/reduce_scatter | solution.py:380
  1517.4 220.7 %copy-start.51 = (f32[2,8]{1,0:T(2,128)S(1)}, f32[2,8]{1,0:T(2,128)}, u32[]{:S(2)}) copy-start(f32[2,8]{1,0:T(2,128)} %get-tuple-element.220) | copy-start | bytes 196
  1517.5 613.4 %reduce-scatter.24.cloned.1.call-start = ((), (), s32[]{:S(2)}) async-start(), calls=%async_computation.22 | async-start | bytes 4866048
  (101 other events, 493.4 us)
Sparse Core Ops, SparseCore 0:
  10.9 59.9 all-gather.15
  73.9 64.9 all-gather.11
  141.8 54.2 all-gather.13
  198.9 54.5 all-gather.17
  256.2 54.5 all-gather.19
  313.6 62.6 all-gather.21
  379.2 62.4 all-gather.23
  815.0 96.3 reduce-scatter.17
  1379.8 96.3 reduce-scatter.15
  1481.9 107.8 reduce-scatter.13
  1597.0 138.0 reduce-scatter.11
  1741.4 135.1 reduce-scatter.19
  1884.1 134.7 reduce-scatter.21
  2024.8 106.0 reduce-scatter.23
where the time goes:
time: 2150 us; the launch traced here: 2140 us
  matrix products  784 us (36%)
  blocking collectives  562 us (26%)
  local copies, waits for them, and re-layouts  353 us (16%)
  waiting for transfers between devices  265 us (12%)
  other arithmetic  142 us (7%)
    all_gather x1, blocking collectives, on_device(): lax.all_gather(shards[7], ('dp', 'psg'), axis=1, tiled=True)  252 us
    all_gather x1, blocking collectives, on_device(): lax.all_gather(score_local, 'psg', axis=1, tiled=True)  219 us
    dot_general x24, matrix products, cross_scores(): jnp.einsum('ihd,jhd->hij', queries_one, keys_one, preferred_element_type=...  179 us
    unnamed x15, waiting for transfers between devices  116 us
    dot_general x8, matrix products, grad_step(): jnp.einsum('ihd,jhd->hij', grad_heads, values_one, preferred_element_type...  106 us
    reduce_scatter x1, waiting for transfers between devices, on_device(): lax.psum_scatter(grad_hidden_out, ('dp', 'psg'), scatter_dimension=0, til...  88.6 us
    dot_general x8, matrix products, grad_step(): jnp.einsum('hij,ihd->jhd', weights_one.astype(jnp.bfloat16), grad_heads,...  84.7 us
    reduce_sum x8, other arithmetic, stat_step(): summed = jnp.sum(jnp.exp(scores - biggest[..., None]), axis=-1)  75.8 us
  transfers between devices with their start and end apart: 16, of which 3 were waited for; matrix products, arithmetic and copies ran while one was open for 58% of the time, Pallas kernels for 0%

commit v1 on v0

v1 whole, which is shorter than its diff:
```python
import functools

import jax
import jax.numpy as jnp
from jax import lax
from jax.experimental import pallas as pl
from jax.experimental.pallas import tpu as pltpu
from jax.sharding import PartitionSpec as P

H = 12
DH = 64
PAIR = 2 * DH
BF = jnp.bfloat16
F32 = jnp.float32
LN2 = 0.6931471805599453
QSCALE = 0.125 / LN2
ALL = ("dp", "psg")
NN = (((1,), (0,)), ((), ()))
NT = (((1,), (1,)), ((), ()))
TN = (((0,), (0,)), ((), ()))
VMEM_BYTES = 56 * 2**20


def dot(a, b, dims=NN):
    return lax.dot_general(a, b, dims, preferred_element_type=F32)


def mm(a, b, dims=NN):
    return lax.dot_general(a, b, dims, preferred_element_type=F32)


def head_mask(rows, h):
    lane = lax.broadcasted_iota(jnp.int32, (rows, PAIR), 1)
    return (lane >= DH) == (h == 1)


def cross_fwd_body(idx, q_ref, k_ref, v_ref, o_ref, lse_ref, share_ref, *, npass):
    q, k, v = q_ref[0], k_ref[0], v_ref[0]
    keys, rows = k.shape[0], q.shape[0]
    vt = v.T
    col = lax.broadcasted_iota(jnp.int32, (16, keys), 1) // (keys // npass)
    row = lax.broadcasted_iota(jnp.int32, (16, keys), 0)
    member = (col == row).astype(BF)
    outs = []
    for h in range(2):
        qh = jnp.where(head_mask(rows, h), q, jnp.zeros((), BF))
        s = dot(k, qh, NT)
        m = jnp.max(s, axis=0, keepdims=True)
        p = jnp.exp2(s - m).astype(BF)
        ot = dot(jnp.concatenate([vt[h * DH : (h + 1) * DH], member], axis=0), p)
        parts = ot[DH : DH + npass]
        total = jnp.sum(parts, axis=0, keepdims=True)
        inv = 1.0 / total
        outs.append(ot[:DH] * inv)
        lse_ref[0, 0, h : h + 1, :] = m + jnp.log2(total)
        share_ref[0, 0, h, :, :] = parts * inv
    o_ref[0] = jnp.concatenate(outs, axis=0).T.astype(o_ref.dtype)


def cross_fwd(idx, q, kv, npass):
    nq, rows, width = q.shape
    keys, pairs = kv.shape[1], width // PAIR
    grid = pltpu.PrefetchScalarGridSpec(
        num_scalar_prefetch=1,
        grid=(nq, pairs),
        in_specs=[
            pl.BlockSpec((1, rows, PAIR), lambda n, p, i: (n, 0, p)),
            pl.BlockSpec((1, keys, PAIR), lambda n, p, i: (i[n], 0, p)),
            pl.BlockSpec((1, keys, PAIR), lambda n, p, i: (i[n], 0, pairs + p)),
        ],
        out_specs=[
            pl.BlockSpec((1, rows, PAIR), lambda n, p, i: (n, 0, p)),
            pl.BlockSpec((1, 1, 2, rows), lambda n, p, i: (n, p, 0, 0)),
            pl.BlockSpec((1, 1, 2, npass, rows), lambda n, p, i: (n, p, 0, 0, 0)),
        ],
    )
    return pl.pallas_call(
        functools.partial(cross_fwd_body, npass=npass),
        grid_spec=grid,
        out_shape=[
            jax.ShapeDtypeStruct(q.shape, BF),
            jax.ShapeDtypeStruct((nq, pairs, 2, rows), F32),
            jax.ShapeDtypeStruct((nq, pairs, 2, npass, rows), F32),
        ],
        compiler_params=pltpu.CompilerParams(vmem_limit_bytes=VMEM_BYTES),
        cost_estimate=pl.CostEstimate(
            flops=16 * nq * rows * keys * width,
            bytes_accessed=4 * nq * (rows + keys) * width,
            transcendentals=nq * H * rows * keys,
        ),
    )(idx, q, kv, kv)


def cross_bwd_body(idx, q_ref, k_ref, v_ref, do_ref, stat_ref, *rest, chunk):
    dq_ref, dkv_ref = rest[-2:]
    pair = pl.program_id(1)
    width = dkv_ref.shape[2] // 2
    q, k, v, do = q_ref[0], k_ref[0], v_ref[0], do_ref[0]
    rows = q.shape[0]
    kt = k.T
    dk, dv = 0.0, 0.0
    for c in range(0, rows, chunk):
        outs = []
        for h in range(2):
            mask = head_mask(chunk, h)
            qh = jnp.where(mask, q[c : c + chunk], jnp.zeros((), BF))
            doh = jnp.where(mask, do[c : c + chunk], jnp.zeros((), BF))
            p = jnp.exp2(dot(k, qh, NT) - stat_ref[0, 0, h : h + 1, c : c + chunk])
            dp = dot(v, doh, NT)
            ds = (p * (dp - stat_ref[0, 0, 2 + h : 3 + h, c : c + chunk])).astype(BF)
            dv = dv + dot(p.astype(BF), doh)
            dk = dk + dot(ds, qh)
            outs.append(dot(kt[h * DH : (h + 1) * DH], ds))
        dq_ref[0, c : c + chunk, :] = (jnp.concatenate(outs, axis=0).T * 0.125).astype(BF)
    at = pl.multiple_of(pair * PAIR, PAIR)
    dkv_ref[0, :, pl.ds(at, PAIR)] = (dk * LN2).astype(BF)
    at = pl.multiple_of(width + pair * PAIR, PAIR)
    dkv_ref[0, :, pl.ds(at, PAIR)] = dv.astype(BF)


def cross_bwd(idx, q, kv, do, stats, earlier=None):
    nq, rows, width = q.shape
    keys, pairs = kv.shape[1], width // PAIR
    in_specs = [
        pl.BlockSpec((1, rows, PAIR), lambda n, p, i: (n, 0, p)),
        pl.BlockSpec((1, keys, PAIR), lambda n, p, i: (i[n], 0, p)),
        pl.BlockSpec((1, keys, PAIR), lambda n, p, i: (i[n], 0, pairs + p)),
        pl.BlockSpec((1, rows, PAIR), lambda n, p, i: (n, 0, p)),
        pl.BlockSpec((1, 1, 4, rows), lambda n, p, i: (n, p, 0, 0)),
    ]
    operands = [idx, q, kv, kv, do, stats]
    aliases = {}
    if earlier is not None:
        in_specs.append(pl.BlockSpec(memory_space=pl.ANY))
        operands.append(earlier)
        aliases = {6: 1}
    grid = pltpu.PrefetchScalarGridSpec(
        num_scalar_prefetch=1,
        grid=(nq, pairs),
        in_specs=in_specs,
        out_specs=[
            pl.BlockSpec((1, rows, PAIR), lambda n, p, i: (n, 0, p)),
            pl.BlockSpec((1, keys, 2 * width), lambda n, p, i: (i[n], 0, 0)),
        ],
    )
    return pl.pallas_call(
        functools.partial(cross_bwd_body, chunk=min(rows, 256)),
        grid_spec=grid,
        input_output_aliases=aliases,
        out_shape=[jax.ShapeDtypeStruct(q.shape, BF), jax.ShapeDtypeStruct(kv.shape, BF)],
        compiler_params=pltpu.CompilerParams(vmem_limit_bytes=VMEM_BYTES),
        cost_estimate=pl.CostEstimate(
            flops=40 * nq * rows * keys * width,
            bytes_accessed=nq * (6 * rows + 8 * keys) * width,
            transcendentals=nq * H * rows * keys,
        ),
    )(*operands)


def self_mask(keys, start, chunk, length):
    key = lax.broadcasted_iota(jnp.int32, (keys, chunk), 0)
    row = lax.broadcasted_iota(jnp.int32, (keys, chunk), 1) + start
    return (key <= row) & (key < length)


def self_fwd_body(length_ref, q_ref, k_ref, v_ref, o_ref, lse_ref, *, chunk):
    length = length_ref[pl.program_id(0)]
    q, k, v = q_ref[0], k_ref[0], v_ref[0]
    rows = q.shape[0]
    vt = v.T
    for c in range(0, rows, chunk):
        keys = c + chunk
        allowed = self_mask(keys, c, chunk, length)
        ones = jnp.ones((16, keys), BF)
        outs = []
        for h in range(2):
            qh = jnp.where(head_mask(chunk, h), q[c : c + chunk], jnp.zeros((), BF))
            s = jnp.where(allowed, dot(k[:keys], qh, NT), -1e30)
            m = jnp.max(s, axis=0, keepdims=True)
            p = jnp.exp2(s - m).astype(BF)
            ot = dot(jnp.concatenate([vt[h * DH : (h + 1) * DH, :keys], ones], axis=0), p)
            total = ot[DH : DH + 1]
            outs.append(ot[:DH] * (1.0 / total))
            lse_ref[0, 0, h : h + 1, c : c + chunk] = m + jnp.log2(total)
        o_ref[0, c : c + chunk, :] = jnp.concatenate(outs, axis=0).T.astype(BF)


def self_fwd(lengths, qkv):
    nq, rows, width3 = qkv.shape
    width = width3 // 3
    pairs = width // PAIR
    grid = pltpu.PrefetchScalarGridSpec(
        num_scalar_prefetch=1,
        grid=(nq, pairs),
        in_specs=[
            pl.BlockSpec((1, rows, PAIR), lambda n, p, i: (n, 0, p)),
            pl.BlockSpec((1, rows, PAIR), lambda n, p, i: (n, 0, pairs + p)),
            pl.BlockSpec((1, rows, PAIR), lambda n, p, i: (n, 0, 2 * pairs + p)),
        ],
        out_specs=[
            pl.BlockSpec((1, rows, PAIR), lambda n, p, i: (n, 0, p)),
            pl.BlockSpec((1, 1, 2, rows), lambda n, p, i: (n, p, 0, 0)),
        ],
    )
    return pl.pallas_call(
        functools.partial(self_fwd_body, chunk=min(rows, 256)),
        grid_spec=grid,
        out_shape=[
            jax.ShapeDtypeStruct((nq, rows, width), BF),
            jax.ShapeDtypeStruct((nq, pairs, 2, rows), F32),
        ],
        compiler_params=pltpu.CompilerParams(vmem_limit_bytes=VMEM_BYTES),
        cost_estimate=pl.CostEstimate(
            flops=16 * nq * rows * rows * width,
            bytes_accessed=8 * nq * rows * width,
            transcendentals=nq * H * rows * rows,
        ),
    )(lengths, qkv, qkv, qkv)


def self_bwd_body(length_ref, q_ref, k_ref, v_ref, do_ref, lse_ref, out_ref, dk_acc, dv_acc, *, chunk):
    length = length_ref[pl.program_id(0)]
    pair = pl.program_id(1)
    width = out_ref.shape[2] // 3
    q, k, v, do = q_ref[0], k_ref[0], v_ref[0], do_ref[0]
    rows = q.shape[0]
    kt = k.T
    at = pl.multiple_of(pair * PAIR, PAIR)
    dk_acc[...] = jnp.zeros_like(dk_acc)
    dv_acc[...] = jnp.zeros_like(dv_acc)
    for c in range(0, rows, chunk):
        keys = c + chunk
        allowed = self_mask(keys, c, chunk, length)
        outs = []
        for h in range(2):
            mask = head_mask(chunk, h)
            qh = jnp.where(mask, q[c : c + chunk], jnp.zeros((), BF))
            doh = jnp.where(mask, do[c : c + chunk], jnp.zeros((), BF))
            s = jnp.where(allowed, dot(k[:keys], qh, NT), -1e30)
            p = jnp.exp2(s - lse_ref[0, 0, h : h + 1, c : c + chunk])
            dp = dot(v[:keys], doh, NT)
            delta = jnp.sum(p * dp, axis=0, keepdims=True)
            ds = (p * (dp - delta)).astype(BF)
            dv_acc[:keys] += dot(p.astype(BF), doh)
            dk_acc[:keys] += dot(ds, qh)
            outs.append(dot(kt[h * DH : (h + 1) * DH, :keys], ds))
        out_ref[0, c : c + chunk, pl.ds(at, PAIR)] = (
            jnp.concatenate(outs, axis=0).T * 0.125
        ).astype(BF)
    at = pl.multiple_of(width + pair * PAIR, PAIR)
    out_ref[0, :, pl.ds(at, PAIR)] = (dk_acc[...] * LN2).astype(BF)
    at = pl.multiple_of(2 * width + pair * PAIR, PAIR)
    out_ref[0, :, pl.ds(at, PAIR)] = dv_acc[...].astype(BF)


def self_bwd(lengths, qkv, do, lse):
    nq, rows, width3 = qkv.shape
    width = width3 // 3
    pairs = width // PAIR
    grid = pltpu.PrefetchScalarGridSpec(
        num_scalar_prefetch=1,
        grid=(nq, pairs),
        in_specs=[
            pl.BlockSpec((1, rows, PAIR), lambda n, p, i: (n, 0, p)),
            pl.BlockSpec((1, rows, PAIR), lambda n, p, i: (n, 0, pairs + p)),
            pl.BlockSpec((1, rows, PAIR), lambda n, p, i: (n, 0, 2 * pairs + p)),
            pl.BlockSpec((1, rows, PAIR), lambda n, p, i: (n, 0, p)),
            pl.BlockSpec((1, 1, 2, rows), lambda n, p, i: (n, p, 0, 0)),
        ],
        out_specs=[pl.BlockSpec((1, rows, width3), lambda n, p, i: (n, 0, 0))],
        scratch_shapes=[pltpu.VMEM((rows, PAIR), F32), pltpu.VMEM((rows, PAIR), F32)],
    )
    return pl.pallas_call(
        functools.partial(self_bwd_body, chunk=min(rows, 256)),
        grid_spec=grid,
        out_shape=[jax.ShapeDtypeStruct(qkv.shape, BF)],
        compiler_params=pltpu.CompilerParams(vmem_limit_bytes=VMEM_BYTES),
        cost_estimate=pl.CostEstimate(
            flops=40 * nq * rows * rows * width,
            bytes_accessed=16 * nq * rows * width,
            transcendentals=nq * H * rows * rows,
        ),
    )(lengths, qkv, qkv, qkv, do, lse)[0]


def rms_parts(v):
    return lax.rsqrt(jnp.mean(v * v, axis=-1, keepdims=True) + 1e-06)


def rms_back(v, gain, b):
    r = rms_parts(v)
    gb = gain * b
    grad = r * gb - v * (r * r * r * jnp.mean(v * gb, axis=-1, keepdims=True))
    return grad, jnp.sum(v * r * b, axis=tuple(range(v.ndim - 1)))


def gelu_and_slope(u):
    t = jnp.tanh(0.7978845608028654 * (u + 0.044715 * u * u * u))
    slope = 0.5 * (1.0 + t) + 0.5 * u * (1.0 - t * t) * (
        0.7978845608028654 * (1.0 + 3.0 * 0.044715 * u * u)
    )
    return 0.5 * u * (1.0 + t), slope


def spread(per_head, rows):
    nq = per_head.shape[0]
    flat = jnp.swapaxes(per_head.reshape(nq, H, rows), 1, 2)
    return jnp.repeat(flat, DH, axis=2)


def merge(parts):
    rows = parts[0][0].shape[1]
    top = functools.reduce(jnp.maximum, [lse for _, lse in parts])
    weights = [jnp.exp2(lse - top) for _, lse in parts]
    total = functools.reduce(jnp.add, weights)
    out = 0.0
    for (value, _), weight in zip(parts, weights):
        out = out + value.astype(F32) * spread(weight / total, rows)
    return out, top + jnp.log2(total)


def on_device(
    decoder_input,
    encoder_out,
    cotangent,
    task_ids,
    passage_ids,
    target_lengths,
    query_embed,
    passage_bank,
    self_in,
    self_out,
    cross_query,
    cross_keyval,
    cross_out,
    hidden_in,
    hidden_output_weight,
    norm_gains,
    task_table,
):
    count, rows, width = decoder_input.shape
    group, npass, tokens, _ = encoder_out.shape
    keys = npass * tokens
    psg = lax.axis_size("psg")
    chips = psg // 2
    me = lax.axis_index("psg")
    chip, core = me // 2, me % 2
    shard = self_in.shape[0]
    ff = hidden_in.shape[1]
    n_tasks = task_table.shape[0]

    swap = [(p, p ^ 1) for p in range(psg)]

    def core_swap(x):
        return jax.tree.map(lambda a: lax.ppermute(a, "psg", swap), x)

    def chip_shift(x, step):
        perm = [(p, (p + 2 * step) % psg) for p in range(psg)]
        return jax.tree.map(lambda a: lax.ppermute(a, "psg", perm), x)

    def ids_of(chip_at, core_at):
        return (chip_at * 2 + core_at) * count + jnp.arange(count, dtype=jnp.int32)

    small = jnp.concatenate([norm_gains, task_table], axis=0).T
    small = jnp.pad(small, ((0, 0), (0, 128 - small.shape[1])))
    first = lax.all_gather(
        jnp.concatenate([self_in, cross_keyval, self_out, cross_query, small], axis=1),
        ALL,
        axis=0,
        tiled=True,
    )
    edges = [0, 3 * width, 5 * width, 6 * width, 7 * width, 7 * width + 128]
    w_self_in, w_cross_keyval, w_self_out, w_cross_query, w_small = (
        first[:, a:b] for a, b in zip(edges[:-1], edges[1:])
    )
    second = lax.all_gather(
        jnp.concatenate([cross_out, hidden_in], axis=1), ALL, axis=0, tiled=True
    )
    w_cross_out, w_hidden_in = second[:, :width], second[:, width:]
    w_hidden_out = lax.all_gather(hidden_output_weight, ALL, axis=0, tiled=True)

    embeds = jnp.take(passage_bank, passage_ids, axis=0).astype(F32)
    score = jnp.sum(query_embed[:, None, :] * embeds, axis=-1)
    others = [
        lax.ppermute(score, "psg", [(p, (p + k) % psg) for p in range(psg)]) for k in range(1, psg)
    ]
    every = jnp.concatenate([score] + others, axis=1)
    top = jnp.max(every, axis=1, keepdims=True)
    retrieval = jnp.exp(score - top) / jnp.sum(jnp.exp(every - top), axis=1, keepdims=True)

    smalls = w_small.T.astype(F32)
    gains, table = smalls[:3], smalls[3 : 3 + n_tasks]
    choose = task_ids[:, None] == jnp.arange(n_tasks, dtype=jnp.int32)[None, :]
    task_rows = jnp.sum(jnp.where(choose[:, :, None], table[None], 0.0), axis=1)

    stream = decoder_input.astype(F32) + task_rows[:, None, :]
    normed_one = (stream * rms_parts(stream) * gains[0]).astype(BF)
    col = lax.broadcasted_iota(jnp.int32, (1, 3 * width), 1)
    scale = jnp.where(col < width, QSCALE, 1.0)
    flat = (count * rows, width)
    qkv = (mm(normed_one.reshape(flat), w_self_in) * scale).astype(BF)
    qkv = qkv.reshape(count, rows, 3 * width)
    self_att, self_lse = self_fwd(target_lengths, qkv)
    middle = stream + mm(self_att.reshape(flat), w_self_out).reshape(stream.shape)
    normed_two = (middle * rms_parts(middle) * gains[1]).astype(BF)
    own_q = (mm(normed_two.reshape(flat), w_cross_query) * QSCALE).astype(BF)
    own_q = own_q.reshape(count, rows, width)

    enc = encoder_out.reshape(group * keys, width)
    kv = mm(enc, w_cross_keyval).astype(BF).reshape(group, keys, 2 * width)
    peer_q = core_swap(own_q)
    far_q = []
    for step in range(1, chips):
        same = [chip_shift(own_q[n : n + 1], step) for n in range(count)]
        far_q.append([(s, core_swap(s)) for s in same])

    far_local, far_back = [], []
    for step in range(1, chips):
        source = (chip - step) % chips
        local, back = [], []
        for n in range(count):
            ids = jnp.stack([ids_of(source, core)[n], ids_of(source, 1 - core)[n]])
            queries = jnp.concatenate(far_q[step - 1][n], axis=0)
            part, lse, share = cross_fwd(ids, queries, kv, npass)
            got = core_swap((part[1:], lse[1:]))
            value, joint = merge([(part[:1], lse[:1]), got])
            back.append(chip_shift((value.astype(BF), joint), chips - step))
            local.append((lse, share))
        far_local.append(local)
        far_back.append(back)
    near_ids = jnp.concatenate([ids_of(chip, core), ids_of(chip, 1 - core)])
    part, near_lse, near_share = cross_fwd(
        near_ids, jnp.concatenate([own_q, peer_q], axis=0), kv, npass
    )
    parts = [(part[:count], near_lse[:count]), core_swap((part[count:], near_lse[count:]))]
    for back in far_back:
        parts.append(
            (
                jnp.concatenate([b[0] for b in back], axis=0),
                jnp.concatenate([b[1] for b in back], axis=0),
            )
        )
    cross_sum, cross_lse = merge(parts)
    cross_att = cross_sum.astype(BF)

    latter = middle + mm(cross_att.reshape(flat), w_cross_out).reshape(stream.shape)
    normed_three = (latter * rms_parts(latter) * gains[2]).astype(BF)
    hidden_pre = mm(normed_three.reshape(flat), w_hidden_in)
    activated, slope = gelu_and_slope(hidden_pre)
    activated = activated.astype(BF)
    output = (latter + mm(activated, w_hidden_out).reshape(stream.shape)).astype(BF)
    cot = cotangent.reshape(flat)
    grad_hidden_out = mm(activated, cot, TN).astype(BF)
    grad_pre = (mm(cot, w_hidden_out, NT) * slope).astype(BF)
    grad_hidden_in = mm(normed_three.reshape(flat), grad_pre, TN).astype(BF)
    grad_normed_three = mm(grad_pre, w_hidden_in, NT).reshape(stream.shape)
    grad_latter, gain_three = rms_back(latter, gains[2], grad_normed_three)
    grad_latter = grad_latter + cotangent.astype(F32)
    grad_cross_part = grad_latter.astype(BF)
    grad_cross_out = mm(cross_att.reshape(flat), grad_cross_part.reshape(flat), TN).astype(BF)
    grad_catt = mm(grad_cross_part.reshape(flat), w_cross_out, NT).astype(BF)
    grad_catt = grad_catt.reshape(count, rows, width)
    sum_hidden_out = lax.psum_scatter(grad_hidden_out, ALL, scatter_dimension=0, tiled=True)
    sum_second = lax.psum_scatter(
        jnp.concatenate([grad_cross_out, grad_hidden_in], axis=1),
        ALL,
        scatter_dimension=0,
        tiled=True,
    )

    delta = jnp.sum((grad_catt.astype(F32) * cross_sum).reshape(count, rows, H, DH), axis=-1)
    delta = jnp.swapaxes(delta, 1, 2).reshape(cross_lse.shape)
    own_sent = (grad_catt, jnp.concatenate([cross_lse, delta], axis=2))
    peer_sent = core_swap(own_sent)
    far_sent = []
    for step in range(1, chips):
        same = chip_shift(own_sent, step)
        far_sent.append((same, core_swap(same)))

    dq_own, dkv = cross_bwd(ids_of(chip, core), own_q, kv, *own_sent)
    dq_parts = []
    for step in range(1, chips):
        source = (chip - step) % chips
        ids = jnp.concatenate([ids_of(source, core), ids_of(source, 1 - core)])
        queries = jnp.concatenate(
            [pair[0] for pair in far_q[step - 1]] + [pair[1] for pair in far_q[step - 1]], axis=0
        )
        same, crossed = far_sent[step - 1]
        dq, dkv = cross_bwd(
            ids,
            queries,
            kv,
            jnp.concatenate([same[0], crossed[0]], axis=0),
            jnp.concatenate([same[1], crossed[1]], axis=0),
            dkv,
        )
        joint = dq[:count].astype(F32) + core_swap(dq[count:]).astype(F32)
        dq_parts.append(chip_shift(joint.astype(BF), chips - step))
    dq_peer, dkv = cross_bwd(ids_of(chip, 1 - core), peer_q, kv, *peer_sent, dkv)
    total = dq_own.astype(F32) + core_swap(dq_peer).astype(F32)
    for dq in dq_parts:
        total = total + dq.astype(F32)
    grad_cross_q = total.astype(BF).reshape(flat)

    dkv_flat = dkv.reshape(group * keys, 2 * width)
    grad_cross_query = mm(normed_two.reshape(flat), grad_cross_q, TN).astype(BF)
    grad_cross_keyval = mm(enc, dkv_flat, TN).astype(BF)
    sum_cross = lax.psum_scatter(
        jnp.concatenate([grad_cross_query, grad_cross_keyval], axis=1),
        ALL,
        scatter_dimension=0,
        tiled=True,
    )
    encoder_grad = mm(dkv_flat, w_cross_keyval, NT).reshape(encoder_out.shape)

    grad_normed_two = mm(grad_cross_q, w_cross_query, NT).reshape(stream.shape)
    grad_middle, gain_two = rms_back(middle, gains[1], grad_normed_two)
    grad_middle = grad_middle + grad_latter
    grad_self_part = grad_middle.astype(BF).reshape(flat)
    grad_self_out = mm(self_att.reshape(flat), grad_self_part, TN).astype(BF)
    grad_satt = mm(grad_self_part, w_self_out, NT).astype(BF).reshape(count, rows, width)
    grad_qkv = self_bwd(target_lengths, qkv, grad_satt, self_lse).reshape(count * rows, 3 * width)
    grad_self_in = mm(normed_one.reshape(flat), grad_qkv, TN).astype(BF)
    grad_normed_one = mm(grad_qkv, w_self_in, NT).reshape(stream.shape)
    grad_stream, gain_one = rms_back(stream, gains[0], grad_normed_one)
    input_grad = grad_stream + grad_middle
    per_query = jnp.sum(input_grad, axis=1)
    grad_table = jnp.sum(jnp.where(choose[:, :, None], per_query[:, None, :], 0.0), axis=0)
    tiny = jnp.concatenate([jnp.stack([gain_one, gain_two, gain_three]), grad_table], axis=0).T
    tiny = jnp.pad(tiny, ((0, 0), (0, 256 - tiny.shape[1]))).astype(BF)
    sum_self = lax.psum_scatter(
        jnp.concatenate([grad_self_in, grad_self_out, tiny], axis=1),
        ALL,
        scatter_dimension=0,
        tiled=True,
    )

    sets = [
        (ids_of(chip, core), near_lse[:count], near_share[:count], own_sent[1]),
        (ids_of(chip, 1 - core), near_lse[count:], near_share[count:], peer_sent[1]),
    ]
    for step in range(1, chips):
        source = (chip - step) % chips
        for side in range(2):
            lse = jnp.concatenate([lo[0][side : side + 1] for lo in far_local[step - 1]], axis=0)
            share = jnp.concatenate([lo[1][side : side + 1] for lo in far_local[step - 1]], axis=0)
            ids = ids_of(source, core if side == 0 else 1 - core)
            sets.append((ids, lse, share, far_sent[step - 1][side][1]))
    ids = jnp.concatenate([s[0] for s in sets])
    masses = []
    for _, lse, share, stats in sets:
        weight = jnp.exp2(lse - stats[:, :, :2])
        masses.append(jnp.sum(share * weight[:, :, :, None, :], axis=(1, 2, 4)) / (H * rows))
    masses = jnp.concatenate(masses, axis=0)
    place = ids[None, :] == jnp.arange(group, dtype=jnp.int32)[:, None]
    mass = jnp.sum(jnp.where(place[:, :, None], masses[None], 0.0), axis=1)
    query_grad = jnp.sum((retrieval - mass)[:, :, None] * embeds, axis=1)
    hop = 1
    while hop < psg:
        perm = [(p, p ^ hop) for p in range(psg)]
        query_grad = query_grad + lax.ppermute(query_grad, "psg", perm)
        hop *= 2

    small_sum = sum_self[:, 4 * width :].astype(F32).T
    return (
        output,
        input_grad,
        encoder_grad,
        sum_self[:, : 3 * width].astype(F32),
        sum_self[:, 3 * width : 4 * width].astype(F32),
        sum_cross[:, :width].astype(F32),
        sum_cross[:, width:].astype(F32),
        sum_second[:, :width].astype(F32),
        sum_second[:, width:].astype(F32),
        sum_hidden_out.astype(F32),
        small_sum[:3],
        small_sum[3 : 3 + n_tasks],
        query_grad,
    )


def solution(mesh):
    rows = P(ALL, None)
    tokens = P(ALL, None, None)
    passages = P("dp", "psg", None, None)
    columns = P(None, ALL)
    return jax.shard_map(
        on_device,
        mesh=mesh,
        in_specs=(tokens, passages, tokens, P(ALL), P("dp", "psg"), P(ALL), P("dp", None), P())
        + (rows,) * 7
        + (columns, columns),
        out_specs=(tokens, tokens, passages) + (rows,) * 7 + (columns, columns, P("dp", None)),
        check_vma=False,
    )
```

time: 2150 us -> 923 us (0.43)
  matrix products: 784 us -> 176 us
  blocking collectives: 562 us -> 0 us
  local copies, waits for them, and re-layouts: 353 us -> 87.4 us
  Pallas kernels: 0 us -> 249 us
  other arithmetic: 142 us -> 80.5 us
  waiting for transfers between devices: 265 us -> 293 us
    dot_general x94 -> x21, matrix products: 768 us -> 176 us  [mm(): return lax.dot_general(a, b, dims, preferred_element_type=F32)]
    all_gather x4 -> x0, blocking collectives: 513 us -> none  [the longest x1 252 us: on_device(): lax.all_gather(shards[7], ('dp', 'psg'), axis=1, tiled=True)]
    pallas_call x0 -> x8, Pallas kernels: none -> 249 us  [the longest x3 117 us: cross_bwd(): pl.pallas_call(functools.partial(cross_bwd_body, chunk=min(rows, 256)), g...]
    squeeze x36 -> x0, local copies, waits for them, and re-layouts: 91 us -> none  [the longest x24 45.5 us: owner_forward(): (row_max, row_sum), unused_stat = lax.scan(stat_step, start, blocks_one)]
    unnamed x15 -> x8, waiting for transfers between devices: 116 us -> 28.1 us
    dynamic_update_slice x34 -> x0, local copies, waits for them, and re-layouts: 86.8 us -> none  [the longest x16 60.4 us: owner_backward(): lax.scan(grad_step, jnp.zeros((seq_len, H, DH), jnp.float32), blocks_one)]
    ppermute x0 -> x29, waiting for transfers between devices: none -> 85.5 us  [the longest x9 80.8 us: chip_shift(): return jax.tree.map(lambda a: lax.ppermute(a, 'psg', perm), x)]
    all_to_all x3 -> x0, local copies, waits for them, and re-layouts: 83 us -> none  [the longest x2 58.4 us: on_device(): lax.all_to_all(owner_pairs, 'psg', split_axis=1, concat_axis=0, tiled=True)]
  transfers between devices with their start and end apart: 16 -> 36, of which waited for: 3 -> 8; matrix products, arithmetic and copies ran while one was open for 58% -> 31% of each run, Pallas kernels for 0% -> 27%
where the time goes in v1:
time: 923 us; the launch traced here: 917 us
  waiting for transfers between devices  293 us (32%)
  Pallas kernels  249 us (27%)
  matrix products  176 us (19%)
  local copies, waits for them, and re-layouts  87.4 us (9%)
  other arithmetic  80.5 us (9%)
  starting transfers between devices  16 us (2%)
  between operations  15.9 us (2%)
    dot_general x21, matrix products, mm(): return lax.dot_general(a, b, dims, preferred_element_type=F32)  176 us
    pallas_call x3, Pallas kernels, cross_bwd(): pl.pallas_call(functools.partial(cross_bwd_body, chunk=min(rows, 256)), g...  117 us
    reduce_scatter x1, waiting for transfers between devices, on_device(): lax.psum_scatter(jnp.concatenate([grad_self_in, grad_self_out, tiny], axi...  109 us
    pallas_call x3, Pallas kernels, cross_fwd(): pl.pallas_call(functools.partial(cross_fwd_body, npass=npass), grid_spec=...  84.2 us
    ppermute x9, waiting for transfers between devices, chip_shift(): return jax.tree.map(lambda a: lax.ppermute(a, 'psg', perm), x)  80.8 us
    all_gather x1, waiting for transfers between devices, on_device(): lax.all_gather(jnp.concatenate([self_in, cross_keyval, self_out, cross_qu...  69.6 us
    unnamed x8, waiting for transfers between devices  28.1 us
    unnamed x216, local copies, waits for them, and re-layouts  25.8 us
  transfers between devices with their start and end apart: 36, of which 8 were waited for; matrix products, arithmetic and copies ran while one was open for 31% of the time, Pallas kernels for 27%

profile of v1, /device:TPU:0, one launch (start us, length us, event | category | flops | bytes accessed | tf_op | source)
XLA Modules:
  0.0 917.5 jit_solution(11562576865145394270)
XLA Ops:
  23.3 69.6 %all-gather.4.cloned.1.call-done = bf16[768,5504]{1,0:T(8,128)(2,1)} async-done(((bf16[24,5504]{1,0:T(8,128)(2,1)}), bf16[768,5504]{1,0:T(8,128)(2,1)}) %all-gather.4.cloned.1.call-update) | async-done | bytes 8454160 | tf_op jit(solution)/shard_map/all_gather | solution.py:366
  96.0 7.9 multiply_convert_fusion.1
  104.0 21.3 %shard_map.264 = (bf16[2,512,768]{2,1,0:T(8,128)(2,1)}, f32[2,6,2,512]{3,2,1,0:T(2,128)}) custom-call(s32[2]{0:T(128)} %length_ref.3, bf16[2,512,2304]{2,1,0:T(8,128)(2,1)} %bitcast.186, bf16[2,512,2304]{2,1,0:T(8,128)(2,1)} %bitcast.187, bf16[2,512,2304]{2,1,0:T(8,128)(2,1)} %bitcast.188), custom_call_target="tpu_custom_call" | custom-call | flops 6442450944 | bytes 6291456 | tf_op jit(solution)/shard_map/pallas_call | solution.py:205
  141.9 23.5 %collective-permute-done.6 = bf16[1,512,768]{2,1,0:T(8,128)(2,1)S(1)} collective-permute-done((bf16[1,512,768]{2,1,0:T(8,128)(2,1)}, bf16[1,512,768]{2,1,0:T(8,128)(2,1)S(1)}, u32[]{:S(2)}, u32[]{:S(2)}) %collective-permute-start.6) | collective-permute-done | bytes 786464 | tf_op jit(solution)/shard_map/ppermute | solution.py:359
  165.4 21.0 %fusion = bf16[6144,1536]{0,1:T(8,128)(2,1)} fusion(bf16[6144,768]{1,0:T(8,128)(2,1)} %bitcast.182, bf16[768,5504]{1,0:T(8,128)(2,1)} %all-gather.4.cloned.1.call-done), kind=kOutput, calls=%fused_computation.2 | convolution fusion | flops 14504951808 | bytes 30670848 | tf_op jit(solution)/shard_map/dot_general | solution.py:29
  186.4 24.6 %copy.195 = bf16[6144,1536]{1,0:T(8,128)(2,1)} copy(bf16[6144,1536]{0,1:T(8,128)(2,1)} %fusion) | data formatting | bytes 37748736 | tf_op jit(solution)/shard_map/convert_element_type | solution.py:410
  212.7 21.9 %shard_map.267 = (bf16[2,512,768]{2,1,0:T(8,128)(2,1)}, f32[2,6,2,512]{3,2,1,0:T(2,128)}, f32[2,6,2,2,512]{4,3,2,1,0:T(2,128)}) custom-call(s32[2]{0:T(128)} %pad_add_fusion.2.idx, bf16[2,512,768]{2,1,0:T(8,128)(2,1)} %pad_maximum_fusion.6.q_ref, bf16[8,768,1536]{2,1,0:T(8,128)(2,1)} %bitcast.130, bf16[8,768,1536]{2,1,0:T(8,128)(2,1)} %bitcast.131), custom_call_target="tpu_custom_call" | custom-call | flops 9663676416 | bytes 7864320 | tf_op jit(solution)/shard_map/pallas_call | solution.py:77
  237.1 21.6 %shard_map.266 = (bf16[2,512,768]{2,1,0:T(8,128)(2,1)}, f32[2,6,2,512]{3,2,1,0:T(2,128)}, f32[2,6,2,2,512]{4,3,2,1,0:T(2,128)}) custom-call(s32[2]{0:T(128)} %pad_add_fusion.1.idx, bf16[2,512,768]{2,1,0:T(8,128)(2,1)} %pad_maximum_fusion.5.q_ref, bf16[8,768,1536]{2,1,0:T(8,128)(2,1)} %bitcast.132, bf16[8,768,1536]{2,1,0:T(8,128)(2,1)} %bitcast.133), custom_call_target="tpu_custom_call" | custom-call | flops 9663676416 | bytes 7864320 | tf_op jit(solution)/shard_map/pallas_call | solution.py:77
  265.4 40.7 %shard_map.265 = (bf16[4,512,768]{2,1,0:T(8,128)(2,1)}, f32[4,6,2,512]{3,2,1,0:T(2,128)}, f32[4,6,2,2,512]{4,3,2,1,0:T(2,128)}) custom-call(s32[4]{0:T(128)} %pad_add_fusion.idx, bf16[4,512,768]{2,1,0:T(8,128)(2,1)} %pad_maximum_fusion.2.q_ref, bf16[8,768,1536]{2,1,0:T(8,128)(2,1)} %bitcast.134, bf16[8,768,1536]{2,1,0:T(8,128)(2,1)} %bitcast.135), custom_call_target="tpu_custom_call" | custom-call | flops 19327352832 | bytes 15728640 | tf_op jit(solution)/shard_map/pallas_call | solution.py:77
  331.4 30.0 %collective-permute-done.9 = f32[1,6,2,512]{3,2,1,0:T(2,128)S(1)} collective-permute-done((f32[1,6,2,512]{3,2,1,0:T(2,128)S(1)}, f32[1,6,2,512]{3,2,1,0:T(2,128)S(1)}, u32[]{:S(2)}, u32[]{:S(2)}) %collective-permute-start.9) | collective-permute-done | bytes 24608 | tf_op jit(solution)/shard_map/ppermute | solution.py:359
  371.0 7.7 multiply_add_fusion.1
  378.7 4.8 multiply_reduce_fusion.6
  383.9 5.1 fusion.13
  393.8 8.5 convolution_convert_fusion.1
  402.3 14.8 %fusion.8 = bf16[1024,3072]{1,0:T(8,128)(2,1)S(1)} fusion(f32[1024,3072]{1,0:T(8,128)} %copy-done.99, bf16[1024,768]{1,0:T(8,128)(2,1)} %bitcast.147, bf16[3072,768]{1,0:T(8,128)(2,1)} %all-gather.8.cloned.1.call-done), kind=kOutput, calls=%fused_computation.12 | convolution fusion | flops 4891607040 | bytes 25165824 | tf_op jit(solution)/shard_map/dot_general | solution.py:29
  417.1 9.7 %fusion.11 = f32[1024,768]{1,0:T(8,128)S(1)} fusion(bf16[1024,3072]{1,0:T(8,128)(2,1)S(1)} %fusion.8, bf16[768,3840]{1,0:T(8,128)(2,1)} %all-gather.6.cloned.1.call-done), kind=kOutput, calls=%fused_computation.22 | convolution fusion | flops 4831838208 | bytes 14155776 | tf_op jit(solution)/shard_map/dot_general | solution.py:29
  445.5 12.9 %fusion.58 = f32[1024,768]{1,0:T(8,128)} fusion(bf16[3072,768]{1,0:T(8,128)(2,1)} %all-gather.8.cloned.1.call-done, f32[1024,3072]{1,0:T(8,128)} %copy-done.99), kind=kOutput, calls=%fused_computation.192 | convolution fusion | flops 4860149760 | bytes 20447232 | tf_op jit(solution)/shard_map/dot_general | solution.py:29
  458.4 30.1 %shard_map.268 = (bf16[2,512,768]{2,1,0:T(8,128)(2,1)}, bf16[8,768,1536]{2,1,0:T(8,128)(2,1)}) custom-call(s32[2]{0:T(128)} %copy-done.95, bf16[2,512,768]{2,1,0:T(8,128)(2,1)} %bitcast.154, bf16[8,768,1536]{2,1,0:T(8,128)(2,1)} %bitcast.136, bf16[8,768,1536]{2,1,0:T(8,128)(2,1)} %bitcast.137, bf16[2,512,768]{2,1,0:T(8,128)(2,1)} %bitcast.166, ...), custom_call_target="tpu_custom_call" | custom-call | flops 24159191040 | bytes 14155776 | tf_op jit(solution)/shard_map/pallas_call | solution.py:146
  488.9 9.6 %convolution_convert_fusion.2 = bf16[768,3072]{1,0:T(8,128)(2,1)} fusion(bf16[1024,768]{1,0:T(8,128)(2,1)S(1)} %bitcast.162, bf16[1024,3072]{1,0:T(8,128)(2,1)} %copy-done.98), kind=kOutput, calls=%fused_computation.21 | convolution fusion | flops 4834197504 | bytes 12582912 | tf_op jit(solution)/shard_map/dot_general | solution.py:29
  502.9 5.2 pad_maximum_fusion
  513.4 57.0 %shard_map.269 = (bf16[4,512,768]{2,1,0:T(8,128)(2,1)}, bf16[8,768,1536]{2,1,0:T(8,128)(2,1)}) custom-call(s32[4]{0:T(128)} %pad_add_fusion.3.idx, bf16[4,512,768]{2,1,0:T(8,128)(2,1)} %pad_maximum_fusion.3.q_ref, bf16[8,768,1536]{2,1,0:T(8,128)(2,1)} %bitcast.138, bf16[8,768,1536]{2,1,0:T(8,128)(2,1)} %bitcast.139, ...), custom_call_target="tpu_custom_call", output_to_operand_aliasing={{1}: (6, {})} | custom-call | flops 48318382080 | bytes 28311552 | tf_op jit(solution)/shard_map/pallas_call | solution.py:146
  572.8 30.4 %shard_map.270 = (bf16[2,512,768]{2,1,0:T(8,128)(2,1)}, bf16[8,768,1536]{2,1,0:T(8,128)(2,1)}) custom-call(s32[2]{0:T(128)} %copy-done.94, bf16[2,512,768]{2,1,0:T(8,128)(2,1)} %collective-permute-done.q_ref, bf16[8,768,1536]{2,1,0:T(8,128)(2,1)} %bitcast.140, bf16[8,768,1536]{2,1,0:T(8,128)(2,1)} %bitcast.141, ...), custom_call_target="tpu_custom_call", output_to_operand_aliasing={{1}: (6, {})} | custom-call | flops 24159191040 | bytes 14155776 | tf_op jit(solution)/shard_map/pallas_call | solution.py:146
  604.4 21.8 %fusion.21 = bf16[768,1536]{0,1:T(8,128)(2,1)S(1)} fusion(bf16[6144,1536]{1,0:T(8,128)(2,1)} %bitcast.184, bf16[6144,768]{1,0:T(8,128)(2,1)} %bitcast.183), kind=kOutput, calls=%fused_computation.59 | convolution fusion | flops 14496694272 | bytes 30670848 | tf_op jit(solution)/shard_map/dot_general | solution.py:29
  626.2 27.2 %collective-permute-done.23 = bf16[2,512,768]{2,1,0:T(8,128)(2,1)S(1)} collective-permute-done((bf16[2,512,768]{2,1,0:T(8,128)(2,1)S(1)}, bf16[2,512,768]{2,1,0:T(8,128)(2,1)S(1)}, u32[]{:S(2)}, u32[]{:S(2)}) %collective-permute-start.23) | collective-permute-done | bytes 1572896 | tf_op jit(solution)/shard_map/ppermute | solution.py:359
  653.5 5.0 multiply_reduce_fusion.1
  662.1 5.8 copy.234
  670.0 7.3 fusion.60
  681.7 25.7 %shard_map.271 = bf16[2,512,2304]{2,1,0:T(8,128)(2,1)} custom-call(s32[2]{0:T(128)} %length_ref.3, bf16[2,512,2304]{2,1,0:T(8,128)(2,1)} %bitcast.189, bf16[2,512,2304]{2,1,0:T(8,128)(2,1)} %bitcast.190, bf16[2,512,2304]{2,1,0:T(8,128)(2,1)} %bitcast.191, bf16[2,512,768]{2,1,0:T(8,128)(2,1)} %bitcast.192, f32[2,6,2,512]{3,2,1,0:T(2,128)} %get-tuple-element.42.lse_ref), custom_call_target="tpu_custom_call" | custom-call | flops 16106127360 | bytes 12582912 | tf_op jit(solution)/shard_map/pallas_call | solution.py:273
  707.4 7.4 multiply_reduce_fusion.2
  736.0 22.0 %fusion.22 = f32[8,2,384,768]{3,2,1,0:T(8,128)} fusion(bf16[8,2,384,1536]{3,2,1,0:T(8,128)(2,1)} %bitcast.185, bf16[768,5504]{1,0:T(8,128)(2,1)} %all-gather.4.cloned.1.call-done), kind=kOutput, calls=%fused_computation.60 | convolution fusion | flops 14495514624 | bytes 40108032 | tf_op jit(solution)/shard_map/dot_general | solution.py:29
  762.8 28.0 %reduce-scatter.13.cloned.1.call-done = bf16[24,2304]{1,0:T(8,128)(2,1)} async-done(((bf16[768,2304]{1,0:T(8,128)(2,1)}), bf16[24,2304]{1,0:T(8,128)(2,1)}) %reduce-scatter.13.cloned.1.call-update) | async-done | bytes 110608
  795.9 109.3 %reduce-scatter.7.cloned.1.call-done = bf16[24,3328]{1,0:T(8,128)(2,1)} async-done(((bf16[768,3328]{1,0:T(8,128)(2,1)}), bf16[24,3328]{1,0:T(8,128)(2,1)}) %reduce-scatter.7.cloned.1.call-update) | async-done | bytes 159760 | tf_op jit(solution)/shard_map/reduce_scatter | solution.py:531
  (436 shorter events, 164.0 us)
Async XLA Ops:
  7.2 85.7 %all-gather.4.cloned.1.call-start = ((), (), s32[]{:S(2)}) async-start(), calls=%async_computation.4 | async-start | bytes 8718336 | tf_op jit(solution)/shard_map/all_gather | solution.py:366
  12.3 366.4 %all-gather.6.cloned.1.call-start = ((), (), s32[]{:S(2)}) async-start(), calls=%async_computation.5 | async-start | bytes 6082560 | tf_op jit(solution)/shard_map/all_gather | solution.py:376
  14.0 388.4 %all-gather.8.cloned.1.call-start = ((), (), s32[]{:S(2)}) async-start(), calls=%async_computation.6 | async-start | bytes 4866048 | tf_op jit(solution)/shard_map/all_gather | solution.py:380
  17.3 122.9 %collective-permute-start.26 = (f32[8,2]{1,0:T(8,128)S(1)}, f32[8,2]{1,0:T(8,128)S(1)}, u32[]{:S(2)}, u32[]{:S(2)}) collective-permute-start(f32[8,2]{1,0:T(8,128)S(1)} %fusion.40), channel_id=1, source_target_pairs={{0,3},{1,0},{2,1},{3,2},{4,7},{5,4},{6,5},{7,6},{8,11},{9,8},{10,9... | collective-permute-start | bytes 200 | tf_op jit(solution)/shard_map/ppermute | solution.py:385
  19.8 120.5 %collective-permute-start.25 = (f32[8,2]{1,0:T(8,128)S(1)}, f32[8,2]{1,0:T(8,128)S(1)}, u32[]{:S(2)}, u32[]{:S(2)}) collective-permute-start(f32[8,2]{1,0:T(8,128)S(1)} %fusion.40), channel_id=1, source_target_pairs={{0,2},{1,3},{2,0},{3,1},{4,6},{5,7},{6,4},{7,5},{8,10},{9,11},{10,... | collective-permute-start | bytes 200 | tf_op jit(solution)/shard_map/ppermute | solution.py:385
  20.4 120.0 %collective-permute-start.24 = (f32[8,2]{1,0:T(8,128)S(1)}, f32[8,2]{1,0:T(8,128)S(1)}, u32[]{:S(2)}, u32[]{:S(2)}) collective-permute-start(f32[8,2]{1,0:T(8,128)S(1)} %fusion.40), channel_id=1, source_target_pairs={{0,1},{1,2},{2,3},{3,0},{4,5},{5,6},{6,7},{7,4},{8,9},{9,10},{10,1... | collective-permute-start | bytes 200 | tf_op jit(solution)/shard_map/ppermute | solution.py:385
  20.6 737.4 %reduce-scatter.11.cloned.1.call-start = ((), (), s32[]{:S(2)}) async-start(), calls=%async_computation.9 | async-start | bytes 4866048 | tf_op jit(solution)/shard_map/reduce_scatter | solution.py:463
  134.3 31.1 %collective-permute-start.6 = (bf16[1,512,768]{2,1,0:T(8,128)(2,1)}, bf16[1,512,768]{2,1,0:T(8,128)(2,1)S(1)}, u32[]{:S(2)}, u32[]{:S(2)}) collective-permute-start(bf16[1,512,768]{2,1,0:T(8,128)(2,1)} %get-tuple-element.145), channel_id=1, source_target_pairs={{0,2},{1,3},{2,0},{3,1},{4,6},{5,7},{6,4},{7,5},{8,10},{9,11},{10,... | collective-permute-start | bytes 2359304 | tf_op jit(solution)/shard_map/ppermute | solution.py:359
  141.3 69.8 %collective-permute-start.2 = (bf16[1,512,768]{2,1,0:T(8,128)(2,1)}, bf16[1,512,768]{2,1,0:T(8,128)(2,1)S(1)}, u32[]{:S(2)}, u32[]{:S(2)}) collective-permute-start(bf16[1,512,768]{2,1,0:T(8,128)(2,1)} %get-tuple-element.146), channel_id=1, source_target_pairs={{0,2},{1,3},{2,0},{3,1},{4,6},{5,7},{6,4},{7,5},{8,10},{9,11},{10,... | collective-permute-start | bytes 2359304 | tf_op jit(solution)/shard_map/ppermute | solution.py:359
  141.9 120.2 %collective-permute-start = (bf16[2,512,768]{2,1,0:T(8,128)(2,1)}, bf16[2,512,768]{2,1,0:T(8,128)(2,1)}, u32[]{:S(2)}, u32[]{:S(2)}) collective-permute-start(bf16[2,512,768]{2,1,0:T(8,128)(2,1)} %bitcast.153), channel_id=1, source_target_pairs={{0,1},{1,0},{2,3},{3,2},{4,5},{5,4},{6,7},{7,6},{8,9},{9,8},{10,11... | collective-permute-start | bytes 4718600 | tf_op jit(solution)/shard_map/ppermute | solution.py:355
  165.4 45.9 %collective-permute-start.7 = (bf16[1,512,768]{2,1,0:T(8,128)(2,1)S(1)}, bf16[1,512,768]{2,1,0:T(8,128)(2,1)S(1)}, u32[]{:S(2)}, u32[]{:S(2)}) collective-permute-start(bf16[1,512,768]{2,1,0:T(8,128)(2,1)S(1)} %collective-permute-done.6), channel_id=1, source_target_pairs={{0,1},{1,0},{2,3},{3,2},{4,5},{5,4},{6,7},{7,6},{8,9},{9,8},{10,11... | collective-permute-start | bytes 2359304 | tf_op jit(solution)/shard_map/ppermute | solution.py:355
  211.1 24.6 %collective-permute-start.3 = (bf16[1,512,768]{2,1,0:T(8,128)(2,1)S(1)}, bf16[1,512,768]{2,1,0:T(8,128)(2,1)S(1)}, u32[]{:S(2)}, u32[]{:S(2)}) collective-permute-start(bf16[1,512,768]{2,1,0:T(8,128)(2,1)S(1)} %collective-permute-done.2), channel_id=1, source_target_pairs={{0,1},{1,0},{2,3},{3,2},{4,5},{5,4},{6,7},{7,6},{8,9},{9,8},{10,11... | collective-permute-start | bytes 2359304 | tf_op jit(solution)/shard_map/ppermute | solution.py:355
  235.4 75.7 %collective-permute-start.8 = (f32[1,6,2,512]{3,2,1,0:T(2,128)S(1)}, f32[1,6,2,512]{3,2,1,0:T(2,128)S(1)}, u32[]{:S(2)}, u32[]{:S(2)}) collective-permute-start(f32[1,6,2,512]{3,2,1,0:T(2,128)S(1)} %slice.188), channel_id=1, source_target_pairs={{0,1},{1,0},{2,3},{3,2},{4,5},{5,4},{6,7},{7,6},{8,9},{9,8},{10,11... | collective-permute-start | bytes 73736 | tf_op jit(solution)/shard_map/ppermute | solution.py:355
  259.4 52.7 %collective-permute-start.4 = (f32[1,6,2,512]{3,2,1,0:T(2,128)S(1)}, f32[1,6,2,512]{3,2,1,0:T(2,128)S(1)}, u32[]{:S(2)}, u32[]{:S(2)}) collective-permute-start(f32[1,6,2,512]{3,2,1,0:T(2,128)S(1)} %slice.182), channel_id=1, source_target_pairs={{0,1},{1,0},{2,3},{3,2},{4,5},{5,4},{6,7},{7,6},{8,9},{9,8},{10,11... | collective-permute-start | bytes 73736 | tf_op jit(solution)/shard_map/ppermute | solution.py:355
  261.8 58.9 %collective-permute-start.11 = (bf16[1,512,768]{2,1,0:T(8,128)(2,1)}, bf16[1,512,768]{2,1,0:T(8,128)(2,1)}, u32[]{:S(2)}, u32[]{:S(2)}) collective-permute-start(bf16[1,512,768]{2,1,0:T(8,128)(2,1)} %slice.191), channel_id=1, source_target_pairs={{0,1},{1,0},{2,3},{3,2},{4,5},{5,4},{6,7},{7,6},{8,9},{9,8},{10,11... | collective-permute-start | bytes 2359304 | tf_op jit(solution)/shard_map/ppermute | solution.py:355
  306.9 54.5 %collective-permute-start.1 = (f32[2,6,2,512]{3,2,1,0:T(2,128)S(1)}, f32[2,6,2,512]{3,2,1,0:T(2,128)S(1)}, u32[]{:S(2)}, u32[]{:S(2)}) collective-permute-start(f32[2,6,2,512]{3,2,1,0:T(2,128)S(1)} %slice.176), channel_id=1, source_target_pairs={{0,1},{1,0},{2,3},{3,2},{4,5},{5,4},{6,7},{7,6},{8,9},{9,8},{10,11... | collective-permute-start | bytes 147464 | tf_op jit(solution)/shard_map/ppermute | solution.py:355
  311.1 59.8 %collective-permute-start.10 = (bf16[2,512,768]{2,1,0:T(8,128)(2,1)}, bf16[2,512,768]{2,1,0:T(8,128)(2,1)}, u32[]{:S(2)}, u32[]{:S(2)}) collective-permute-start(bf16[2,512,768]{2,1,0:T(8,128)(2,1)} %slice.189), channel_id=1, source_target_pairs={{0,1},{1,0},{2,3},{3,2},{4,5},{5,4},{6,7},{7,6},{8,9},{9,8},{10,11... | collective-permute-start | bytes 4718600 | tf_op jit(solution)/shard_map/ppermute | solution.py:355
  312.9 18.0 %collective-permute-start.5 = (f32[1,6,2,512]{3,2,1,0:T(2,128)S(1)}, f32[1,6,2,512]{3,2,1,0:T(2,128)S(1)}, u32[]{:S(2)}, u32[]{:S(2)}) collective-permute-start(f32[1,6,2,512]{3,2,1,0:T(2,128)S(1)} %get-tuple-element.155), channel_id=1, source_target_pairs={{0,2},{1,3},{2,0},{3,1},{4,6},{5,7},{6,4},{7,5},{8,10},{9,11},{10,... | collective-permute-start | bytes 73736 | tf_op jit(solution)/shard_map/ppermute | solution.py:359
  324.4 46.5 %collective-permute-start.12 = (bf16[1,512,768]{2,1,0:T(8,128)(2,1)}, bf16[1,512,768]{2,1,0:T(8,128)(2,1)}, u32[]{:S(2)}, u32[]{:S(2)}) collective-permute-start(bf16[1,512,768]{2,1,0:T(8,128)(2,1)} %add_convert_fusion.4), channel_id=1, source_target_pairs={{0,2},{1,3},{2,0},{3,1},{4,6},{5,7},{6,4},{7,5},{8,10},{9,11},{10,... | collective-permute-start | bytes 2359304 | tf_op jit(solution)/shard_map/ppermute | solution.py:359
  327.4 43.5 %collective-permute-start.14 = (bf16[1,512,768]{2,1,0:T(8,128)(2,1)}, bf16[1,512,768]{2,1,0:T(8,128)(2,1)}, u32[]{:S(2)}, u32[]{:S(2)}) collective-permute-start(bf16[1,512,768]{2,1,0:T(8,128)(2,1)} %add_convert_fusion.3), channel_id=1, source_target_pairs={{0,2},{1,3},{2,0},{3,1},{4,6},{5,7},{6,4},{7,5},{8,10},{9,11},{10,... | collective-permute-start | bytes 2359304 | tf_op jit(solution)/shard_map/ppermute | solution.py:359
  330.8 30.6 %collective-permute-start.9 = (f32[1,6,2,512]{3,2,1,0:T(2,128)S(1)}, f32[1,6,2,512]{3,2,1,0:T(2,128)S(1)}, u32[]{:S(2)}, u32[]{:S(2)}) collective-permute-start(f32[1,6,2,512]{3,2,1,0:T(2,128)S(1)} %get-tuple-element.158), channel_id=1, source_target_pairs={{0,2},{1,3},{2,0},{3,1},{4,6},{5,7},{6,4},{7,5},{8,10},{9,11},{10,... | collective-permute-start | bytes 73736 | tf_op jit(solution)/shard_map/ppermute | solution.py:359
  443.1 59.4 %collective-permute-start.19 = (f32[2,6,4,512]{3,2,1,0:T(4,128)S(1)}, f32[2,6,4,512]{3,2,1,0:T(4,128)S(1)}, u32[]{:S(2)}, u32[]{:S(2)}) collective-permute-start(f32[2,6,4,512]{3,2,1,0:T(4,128)S(1)} %pad_maximum_fusion.9.stat_ref), channel_id=1, source_target_pairs={{0,2},{1,3},{2,0},{3,1},{4,6},{5,7},{6,4},{7,5},{8,10},{9,11},{10,... | collective-permute-start | bytes 294920 | tf_op jit(solution)/shard_map/ppermute | solution.py:359
  443.6 128.6 %collective-permute-start.16 = (f32[2,6,4,512]{3,2,1,0:T(4,128)S(1)}, f32[2,6,4,512]{3,2,1,0:T(4,128)S(1)}, u32[]{:S(2)}, u32[]{:S(2)}) collective-permute-start(f32[2,6,4,512]{3,2,1,0:T(4,128)S(1)} %pad_maximum_fusion.9.stat_ref), channel_id=1, source_target_pairs={{0,1},{1,0},{2,3},{3,2},{4,5},{5,4},{6,7},{7,6},{8,9},{9,8},{10,11... | collective-permute-start | bytes 294920 | tf_op jit(solution)/shard_map/ppermute | solution.py:355
  443.6 44.9 %collective-permute-start.17 = (bf16[2,512,768]{2,1,0:T(8,128)(2,1)}, bf16[2,512,768]{2,1,0:T(8,128)(2,1)}, u32[]{:S(2)}, u32[]{:S(2)}) collective-permute-start(bf16[2,512,768]{2,1,0:T(8,128)(2,1)} %bitcast.164), channel_id=1, source_target_pairs={{0,2},{1,3},{2,0},{3,1},{4,6},{5,7},{6,4},{7,5},{8,10},{9,11},{10,... | collective-permute-start | bytes 4718600 | tf_op jit(solution)/shard_map/ppermute | solution.py:359
  445.2 127.0 %collective-permute-start.15 = (bf16[2,512,768]{2,1,0:T(8,128)(2,1)}, bf16[2,512,768]{2,1,0:T(8,128)(2,1)}, u32[]{:S(2)}, u32[]{:S(2)}) collective-permute-start(bf16[2,512,768]{2,1,0:T(8,128)(2,1)} %bitcast.165), channel_id=1, source_target_pairs={{0,1},{1,0},{2,3},{3,2},{4,5},{5,4},{6,7},{7,6},{8,9},{9,8},{10,11... | collective-permute-start | bytes 4718600 | tf_op jit(solution)/shard_map/ppermute | solution.py:355
  445.5 314.2 %reduce-scatter.9.cloned.1.call-start = ((), (), s32[]{:S(2)}) async-start(), calls=%async_computation.8 | async-start | bytes 6082560 | tf_op jit(solution)/shard_map/reduce_scatter | solution.py:464
  488.5 21.0 %collective-permute-start.18 = (bf16[2,512,768]{2,1,0:T(8,128)(2,1)}, bf16[2,512,768]{2,1,0:T(8,128)(2,1)}, u32[]{:S(2)}, u32[]{:S(2)}) collective-permute-start(bf16[2,512,768]{2,1,0:T(8,128)(2,1)} %collective-permute-done.17), channel_id=1, source_target_pairs={{0,1},{1,0},{2,3},{3,2},{4,5},{5,4},{6,7},{7,6},{8,9},{9,8},{10,11... | collective-permute-start | bytes 4718600 | tf_op jit(solution)/shard_map/ppermute | solution.py:355
  508.7 282.1 %reduce-scatter.13.cloned.1.call-start = ((), (), s32[]{:S(2)}) async-start(), calls=%async_computation.10 | async-start | bytes 3649536
  571.9 31.6 %collective-permute-start.22 = (bf16[2,512,768]{2,1,0:T(8,128)(2,1)S(1)}, bf16[2,512,768]{2,1,0:T(8,128)(2,1)S(1)}, u32[]{:S(2)}, u32[]{:S(2)}) collective-permute-start(bf16[2,512,768]{2,1,0:T(8,128)(2,1)S(1)} %slice.198), channel_id=1, source_target_pairs={{0,1},{1,0},{2,3},{3,2},{4,5},{5,4},{6,7},{7,6},{8,9},{9,8},{10,11... | collective-permute-start | bytes 4718600 | tf_op jit(solution)/shard_map/ppermute | solution.py:355
  603.2 23.0 %collective-permute-start.21 = (bf16[2,512,768]{2,1,0:T(8,128)(2,1)}, bf16[2,512,768]{2,1,0:T(8,128)(2,1)S(1)}, u32[]{:S(2)}, u32[]{:S(2)}) collective-permute-start(bf16[2,512,768]{2,1,0:T(8,128)(2,1)} %get-tuple-element.40), channel_id=1, source_target_pairs={{0,1},{1,0},{2,3},{3,2},{4,5},{5,4},{6,7},{7,6},{8,9},{9,8},{10,11... | collective-permute-start | bytes 4718600 | tf_op jit(solution)/shard_map/ppermute | solution.py:355
  603.9 49.6 %collective-permute-start.23 = (bf16[2,512,768]{2,1,0:T(8,128)(2,1)S(1)}, bf16[2,512,768]{2,1,0:T(8,128)(2,1)S(1)}, u32[]{:S(2)}, u32[]{:S(2)}) collective-permute-start(bf16[2,512,768]{2,1,0:T(8,128)(2,1)S(1)} %add_convert_fusion.1), channel_id=1, source_target_pairs={{0,2},{1,3},{2,0},{3,1},{4,6},{5,7},{6,4},{7,5},{8,10},{9,11},{10,... | collective-permute-start | bytes 4718600 | tf_op jit(solution)/shard_map/ppermute | solution.py:359
  668.0 237.3 %reduce-scatter.7.cloned.1.call-start = ((), (), s32[]{:S(2)}) async-start(), calls=%async_computation.7 | async-start | bytes 5271552 | tf_op jit(solution)/shard_map/reduce_scatter | solution.py:531
  (104 other events, 2048.0 us)
Sparse Core Ops, SparseCore 0:
  12.4 80.4 all-gather.3
  96.4 77.4 all-gather.5
  176.8 62.2 all-gather.7
  445.6 105.5 reduce-scatter.10
  557.6 124.6 reduce-scatter.8
  688.5 102.2 reduce-scatter.12
  797.3 107.9 reduce-scatter.6

commit v2 on v1

v2 whole, which is shorter than its diff:
```python
import functools

import jax
import jax.numpy as jnp
from jax import lax
from jax.experimental import pallas as pl
from jax.experimental.pallas import tpu as pltpu
from jax.sharding import PartitionSpec as P

H = 12
DH = 64
PAIR = 2 * DH
BF = jnp.bfloat16
F32 = jnp.float32
LN2 = 0.6931471805599453
QSCALE = 0.125 / LN2
ALL = ("dp", "psg")
NN = (((1,), (0,)), ((), ()))
NT = (((1,), (1,)), ((), ()))
TN = (((0,), (0,)), ((), ()))
VMEM_BYTES = 56 * 2**20


def dot(a, b, dims=NN):
    return lax.dot_general(a, b, dims, preferred_element_type=F32)


def mm(a, b, dims=NN):
    return lax.dot_general(a, b, dims, preferred_element_type=F32)


STEP = 3
SAFE = 80.0


def halves_of(x, h):
    lane = lax.broadcasted_iota(jnp.int32, x.shape, 1)
    return jnp.where((lane >= DH) == (h == 1), x, jnp.zeros((), x.dtype))


def squared_norms(x):
    wide = x.astype(F32)
    return dot(selector(16, 1), (wide * wide).astype(BF), NT)


def params():
    return pltpu.CompilerParams(vmem_limit_bytes=VMEM_BYTES)


def cross_fwd_body(idx, q_ref, k_ref, v_ref, o_ref, lse_ref, share_ref, *, npass):
    keys = k_ref.shape[1]
    blocks = [slice(j * PAIR, (j + 1) * PAIR) for j in range(q_ref.shape[2] // PAIR)]
    col = lax.broadcasted_iota(jnp.int32, (16, keys), 1) // (keys // npass)
    row = lax.broadcasted_iota(jnp.int32, (16, keys), 0)
    member = (col == row).astype(BF)

    def run(shift):
        for j, at in enumerate(blocks):
            q, k, vt = q_ref[0, :, at], k_ref[0, :, at], v_ref[0, :, at].T
            outs = []
            for h in range(2):
                s = dot(k, halves_of(q, h), NT)
                top = jnp.max(s, axis=0, keepdims=True) if shift else None
                p = jnp.exp2(s - top if shift else s).astype(BF)
                ot = dot(jnp.concatenate([vt[h * DH : (h + 1) * DH], member], axis=0), p)
                parts = ot[DH : DH + npass]
                total = jnp.sum(parts, axis=0, keepdims=True)
                inv = 1.0 / total
                outs.append(ot[:DH] * inv)
                lse = jnp.log2(total)
                lse_ref[0, j, h : h + 1, :] = top + lse if shift else lse
                share_ref[0, j, h, :, :] = parts * inv
            o_ref[0, :, at] = jnp.concatenate(outs, axis=0).T.astype(o_ref.dtype)

    longest_q = functools.reduce(jnp.maximum, [squared_norms(q_ref[0, :, at]) for at in blocks])
    longest_k = functools.reduce(jnp.maximum, [squared_norms(k_ref[0, :, at]) for at in blocks])
    small = jnp.max(longest_q) * jnp.max(longest_k) < SAFE * SAFE
    pl.when(small)(lambda: run(False))
    pl.when(jnp.logical_not(small))(lambda: run(True))


def cross_fwd(idx, q, kv, npass):
    nq, rows, width = q.shape
    keys, pairs = kv.shape[1], width // PAIR
    steps, wide = pairs // STEP, STEP * PAIR
    grid = pltpu.PrefetchScalarGridSpec(
        num_scalar_prefetch=1,
        grid=(nq, steps),
        in_specs=[
            pl.BlockSpec((1, rows, wide), lambda n, p, i: (n, 0, p)),
            pl.BlockSpec((1, keys, wide), lambda n, p, i: (i[n], 0, p)),
            pl.BlockSpec((1, keys, wide), lambda n, p, i: (i[n], 0, steps + p)),
        ],
        out_specs=[
            pl.BlockSpec((1, rows, wide), lambda n, p, i: (n, 0, p)),
            pl.BlockSpec((1, STEP, 2, rows), lambda n, p, i: (n, p, 0, 0)),
            pl.BlockSpec((1, STEP, 2, npass, rows), lambda n, p, i: (n, p, 0, 0, 0)),
        ],
    )
    return pl.pallas_call(
        functools.partial(cross_fwd_body, npass=npass),
        grid_spec=grid,
        out_shape=[
            jax.ShapeDtypeStruct(q.shape, BF),
            jax.ShapeDtypeStruct((nq, pairs, 2, rows), F32),
            jax.ShapeDtypeStruct((nq, pairs, 2, npass, rows), F32),
        ],
        compiler_params=params(),
        cost_estimate=pl.CostEstimate(
            flops=16 * nq * rows * keys * width,
            bytes_accessed=4 * nq * (rows + keys) * width,
            transcendentals=nq * H * rows * keys,
        ),
    )(idx, q, kv, kv)


def cross_bwd_body(idx, q_ref, k_ref, v_ref, do_ref, stat_ref, *rest, chunk):
    dq_ref, dkv_ref = rest[-2:]
    first = pl.program_id(1) * STEP
    width = dkv_ref.shape[2] // 2
    rows = q_ref.shape[1]
    for j in range(STEP):
        at = slice(j * PAIR, (j + 1) * PAIR)
        q, k, v, do = q_ref[0, :, at], k_ref[0, :, at], v_ref[0, :, at], do_ref[0, :, at]
        kt = k.T
        dk, dv = 0.0, 0.0
        for c in range(0, rows, chunk):
            outs = []
            for h in range(2):
                qh = halves_of(q[c : c + chunk], h)
                doh = halves_of(do[c : c + chunk], h)
                p = jnp.exp2(dot(k, qh, NT) - stat_ref[0, j, h : h + 1, c : c + chunk])
                dp = dot(v, doh, NT)
                ds = (p * (dp - stat_ref[0, j, 2 + h : 3 + h, c : c + chunk])).astype(BF)
                dv = dv + dot(p.astype(BF), doh)
                dk = dk + dot(ds, qh)
                outs.append(dot(kt[h * DH : (h + 1) * DH], ds))
            dq_ref[0, c : c + chunk, at] = (jnp.concatenate(outs, axis=0).T * 0.125).astype(BF)
        start = pl.multiple_of((first + j) * PAIR, PAIR)
        dkv_ref[0, :, pl.ds(start, PAIR)] = (dk * LN2).astype(BF)
        start = pl.multiple_of(width + (first + j) * PAIR, PAIR)
        dkv_ref[0, :, pl.ds(start, PAIR)] = dv.astype(BF)


def cross_bwd(idx, q, kv, do, stats, earlier=None):
    nq, rows, width = q.shape
    keys, steps, wide = kv.shape[1], width // PAIR // STEP, STEP * PAIR
    in_specs = [
        pl.BlockSpec((1, rows, wide), lambda n, p, i: (n, 0, p)),
        pl.BlockSpec((1, keys, wide), lambda n, p, i: (i[n], 0, p)),
        pl.BlockSpec((1, keys, wide), lambda n, p, i: (i[n], 0, steps + p)),
        pl.BlockSpec((1, rows, wide), lambda n, p, i: (n, 0, p)),
        pl.BlockSpec((1, STEP, 4, rows), lambda n, p, i: (n, p, 0, 0)),
    ]
    operands = [idx, q, kv, kv, do, stats]
    aliases = {}
    if earlier is not None:
        in_specs.append(pl.BlockSpec(memory_space=pl.ANY))
        operands.append(earlier)
        aliases = {6: 1}
    grid = pltpu.PrefetchScalarGridSpec(
        num_scalar_prefetch=1,
        grid=(nq, steps),
        in_specs=in_specs,
        out_specs=[
            pl.BlockSpec((1, rows, wide), lambda n, p, i: (n, 0, p)),
            pl.BlockSpec((1, keys, 2 * width), lambda n, p, i: (i[n], 0, 0)),
        ],
    )
    return pl.pallas_call(
        functools.partial(cross_bwd_body, chunk=min(rows, 256)),
        grid_spec=grid,
        input_output_aliases=aliases,
        out_shape=[jax.ShapeDtypeStruct(q.shape, BF), jax.ShapeDtypeStruct(kv.shape, BF)],
        compiler_params=params(),
        cost_estimate=pl.CostEstimate(
            flops=40 * nq * rows * keys * width,
            bytes_accessed=nq * (6 * rows + 8 * keys) * width,
            transcendentals=nq * H * rows * keys,
        ),
    )(*operands)


def self_mask(rows, length):
    key = lax.broadcasted_iota(jnp.int32, (rows, rows), 0)
    row = lax.broadcasted_iota(jnp.int32, (rows, rows), 1)
    return (key <= row) & (key < length)


def self_fwd_body(length_ref, q_ref, k_ref, v_ref, o_ref, lse_ref):
    rows = q_ref.shape[1]
    allowed = self_mask(rows, length_ref[pl.program_id(0)])
    ones = jnp.ones((16, rows), BF)
    for j in range(STEP):
        at = slice(j * PAIR, (j + 1) * PAIR)
        q, k, vt = q_ref[0, :, at], k_ref[0, :, at], v_ref[0, :, at].T
        outs = []
        for h in range(2):
            s = jnp.where(allowed, dot(k, halves_of(q, h), NT), -1e30)
            top = jnp.max(s, axis=0, keepdims=True)
            p = jnp.exp2(s - top).astype(BF)
            ot = dot(jnp.concatenate([vt[h * DH : (h + 1) * DH], ones], axis=0), p)
            total = ot[DH : DH + 1]
            outs.append(ot[:DH] * (1.0 / total))
            lse_ref[0, j, h : h + 1, :] = top + jnp.log2(total)
        o_ref[0, :, at] = jnp.concatenate(outs, axis=0).T.astype(BF)


def self_fwd(lengths, qkv):
    nq, rows, width = qkv.shape[0], qkv.shape[1], qkv.shape[2] // 3
    pairs = width // PAIR
    steps, wide = pairs // STEP, STEP * PAIR
    grid = pltpu.PrefetchScalarGridSpec(
        num_scalar_prefetch=1,
        grid=(nq, steps),
        in_specs=[
            pl.BlockSpec((1, rows, wide), lambda n, p, i: (n, 0, p)),
            pl.BlockSpec((1, rows, wide), lambda n, p, i: (n, 0, steps + p)),
            pl.BlockSpec((1, rows, wide), lambda n, p, i: (n, 0, 2 * steps + p)),
        ],
        out_specs=[
            pl.BlockSpec((1, rows, wide), lambda n, p, i: (n, 0, p)),
            pl.BlockSpec((1, STEP, 2, rows), lambda n, p, i: (n, p, 0, 0)),
        ],
    )
    return pl.pallas_call(
        self_fwd_body,
        grid_spec=grid,
        out_shape=[
            jax.ShapeDtypeStruct((nq, rows, width), BF),
            jax.ShapeDtypeStruct((nq, pairs, 2, rows), F32),
        ],
        compiler_params=params(),
        cost_estimate=pl.CostEstimate(
            flops=16 * nq * rows * rows * width,
            bytes_accessed=8 * nq * rows * width,
            transcendentals=nq * H * rows * rows,
        ),
    )(lengths, qkv, qkv, qkv)


def self_bwd_body(length_ref, q_ref, k_ref, v_ref, do_ref, lse_ref, out_ref, dk_acc, dv_acc, *, chunk):
    length = length_ref[pl.program_id(0)]
    first = pl.program_id(1) * STEP
    width = out_ref.shape[2] // 3
    rows = q_ref.shape[1]
    for j in range(STEP):
        at = slice(j * PAIR, (j + 1) * PAIR)
        q, k, v, do = q_ref[0, :, at], k_ref[0, :, at], v_ref[0, :, at], do_ref[0, :, at]
        kt = k.T
        start = pl.multiple_of((first + j) * PAIR, PAIR)
        for c in reversed(range(0, rows, chunk)):
            keys = c + chunk
            key = lax.broadcasted_iota(jnp.int32, (keys, chunk), 0)
            row = lax.broadcasted_iota(jnp.int32, (keys, chunk), 1) + c
            allowed = (key <= row) & (key < length)
            outs = []
            dk, dv = 0.0, 0.0
            for h in range(2):
                qh = halves_of(q[c : c + chunk], h)
                doh = halves_of(do[c : c + chunk], h)
                s = jnp.where(allowed, dot(k[:keys], qh, NT), -1e30)
                p = jnp.exp2(s - lse_ref[0, j, h : h + 1, c : c + chunk])
                dp = dot(v[:keys], doh, NT)
                delta = jnp.sum(p * dp, axis=0, keepdims=True)
                ds = (p * (dp - delta)).astype(BF)
                dv = dv + dot(p.astype(BF), doh)
                dk = dk + dot(ds, qh)
                outs.append(dot(kt[h * DH : (h + 1) * DH, :keys], ds))
            if keys == rows:
                dk_acc[...], dv_acc[...] = dk, dv
            else:
                dk_acc[:keys] += dk
                dv_acc[:keys] += dv
            out_ref[0, c : c + chunk, pl.ds(start, PAIR)] = (
                jnp.concatenate(outs, axis=0).T * 0.125
            ).astype(BF)
        start = pl.multiple_of(width + (first + j) * PAIR, PAIR)
        out_ref[0, :, pl.ds(start, PAIR)] = (dk_acc[...] * LN2).astype(BF)
        start = pl.multiple_of(2 * width + (first + j) * PAIR, PAIR)
        out_ref[0, :, pl.ds(start, PAIR)] = dv_acc[...].astype(BF)


def self_bwd(lengths, qkv, do, lse):
    nq, rows, width = do.shape
    steps, wide = width // PAIR // STEP, STEP * PAIR
    grid = pltpu.PrefetchScalarGridSpec(
        num_scalar_prefetch=1,
        grid=(nq, steps),
        in_specs=[
            pl.BlockSpec((1, rows, wide), lambda n, p, i: (n, 0, p)),
            pl.BlockSpec((1, rows, wide), lambda n, p, i: (n, 0, steps + p)),
            pl.BlockSpec((1, rows, wide), lambda n, p, i: (n, 0, 2 * steps + p)),
            pl.BlockSpec((1, rows, wide), lambda n, p, i: (n, 0, p)),
            pl.BlockSpec((1, STEP, 2, rows), lambda n, p, i: (n, p, 0, 0)),
        ],
        out_specs=[pl.BlockSpec((1, rows, 3 * width), lambda n, p, i: (n, 0, 0))],
        scratch_shapes=[pltpu.VMEM((rows, PAIR), F32), pltpu.VMEM((rows, PAIR), F32)],
    )
    return pl.pallas_call(
        functools.partial(self_bwd_body, chunk=min(rows, 256)),
        grid_spec=grid,
        out_shape=[jax.ShapeDtypeStruct((nq, rows, 3 * width), BF)],
        compiler_params=params(),
        cost_estimate=pl.CostEstimate(
            flops=40 * nq * rows * rows * width,
            bytes_accessed=16 * nq * rows * width,
            transcendentals=nq * H * rows * rows,
        ),
    )(lengths, qkv, qkv, qkv, do, lse)[0]


def selector(rows, levels):
    row = lax.broadcasted_iota(jnp.int32, (rows, PAIR), 0)
    lane = lax.broadcasted_iota(jnp.int32, (rows, PAIR), 1)
    return (((lane >= DH) == (row % 2 == 1)) & (row < 2 * levels)).astype(BF)


def merge_body(*refs, parts, full):
    values, lses, outs = refs[:parts], refs[parts : 2 * parts], refs[2 * parts :]
    rows = values[0].shape[1]
    row = lax.broadcasted_iota(jnp.int32, (16, rows), 0)
    pick = selector(16, 2)
    for j in range(values[0].shape[2] // PAIR):
        at = slice(j * PAIR, (j + 1) * PAIR)
        top = functools.reduce(jnp.maximum, [lse[0, j] for lse in lses])
        weights = [jnp.exp2(lse[0, j] - top) for lse in lses]
        total = functools.reduce(jnp.add, weights)
        inv = 1.0 / total
        out = 0.0
        for value, weight in zip(values, weights):
            w = weight * inv
            both = jnp.where(row % 2 == 1, w[1:2], w[0:1])
            high = both.astype(BF).astype(F32)
            split = jnp.where(row < 2, high, both - high).astype(BF)
            out = out + value[0, :, at].astype(F32) * dot(split, pick, TN)
        outs[0][0, :, at] = out.astype(BF)
        outs[1][0, j] = top + jnp.log2(total)
        if full:
            outs[2][0, :, at] = out


def merge(parts, full=False):
    nq, rows, width = parts[0][0].shape
    pairs = width // PAIR
    wide = pl.BlockSpec((1, rows, width), lambda n: (n, 0, 0))
    stat = pl.BlockSpec((1, pairs, 2, rows), lambda n: (n, 0, 0, 0))
    return pl.pallas_call(
        functools.partial(merge_body, parts=len(parts), full=full),
        grid=(nq,),
        in_specs=[wide] * len(parts) + [stat] * len(parts),
        out_specs=[wide, stat] + [wide] * full,
        out_shape=[
            jax.ShapeDtypeStruct((nq, rows, width), BF),
            jax.ShapeDtypeStruct((nq, pairs, 2, rows), F32),
        ]
        + [jax.ShapeDtypeStruct((nq, rows, width), F32)] * full,
        compiler_params=params(),
        cost_estimate=pl.CostEstimate(
            flops=4 * nq * rows * width,
            bytes_accessed=nq * rows * width * (2 * len(parts) + 2 + 4 * full),
            transcendentals=nq * H * rows,
        ),
    )(*[p[0] for p in parts], *[p[1] for p in parts])


def stats_body(do_ref, sum_ref, lse_ref, out_ref):
    pick = selector(16, 1)
    for j in range(do_ref.shape[2] // PAIR):
        at = slice(j * PAIR, (j + 1) * PAIR)
        product = do_ref[0, :, at].astype(F32) * sum_ref[0, :, at]
        high = product.astype(BF)
        low = (product - high.astype(F32)).astype(BF)
        out_ref[0, j, 0:2] = lse_ref[0, j]
        out_ref[0, j, 2:4] = (dot(pick, high, NT) + dot(pick, low, NT))[0:2]


def row_stats(do, cross_sum, lse):
    nq, rows, width = do.shape
    pairs = width // PAIR
    wide = pl.BlockSpec((1, rows, width), lambda n: (n, 0, 0))
    return pl.pallas_call(
        stats_body,
        grid=(nq,),
        in_specs=[wide, wide, pl.BlockSpec((1, pairs, 2, rows), lambda n: (n, 0, 0, 0))],
        out_specs=pl.BlockSpec((1, pairs, 4, rows), lambda n: (n, 0, 0, 0)),
        out_shape=jax.ShapeDtypeStruct((nq, pairs, 4, rows), F32),
        compiler_params=params(),
        cost_estimate=pl.CostEstimate(
            flops=4 * nq * rows * width, bytes_accessed=6 * nq * rows * width, transcendentals=0
        ),
    )(do, cross_sum, lse)


def keyval_body(enc_ref, w_ref, out_ref):
    out_ref[...] = dot(enc_ref[...], w_ref[...]).astype(BF)


def keyval(enc, w):
    n, depth = enc.shape
    width = w.shape[1]
    block = 512
    return pl.pallas_call(
        keyval_body,
        grid=(n // block,),
        in_specs=[
            pl.BlockSpec((block, depth), lambda i: (i, 0)),
            pl.BlockSpec((depth, width), lambda i: (0, 0)),
        ],
        out_specs=pl.BlockSpec((block, width), lambda i: (i, 0)),
        out_shape=jax.ShapeDtypeStruct((n, width), BF),
        compiler_params=params(),
        cost_estimate=pl.CostEstimate(
            flops=2 * n * depth * width, bytes_accessed=2 * n * (depth + width), transcendentals=0
        ),
    )(enc, w)


def bits_below(n):
    return [1 << b for b in range(n.bit_length() - 1)]


def exchanges():
    dp, psg = lax.axis_size("dp"), lax.axis_size("psg")
    flat = bits_below(dp)
    cut = max(1, len(flat) // 3)
    xs = [("dp", b) for b in flat[:cut]]
    zs = [("dp", b) for b in flat[cut:]]
    ys = [("psg", b) for b in bits_below(psg)[1:]]
    order = [("dp", b) for b in reversed(flat)] + [("psg", b) for b in reversed(bits_below(psg))]
    return ("psg", 1), xs, ys, zs, order


def swap_bit(x, hop):
    axis, bit = hop
    n = lax.axis_size(axis)
    return lax.ppermute(x, axis, [(p, p ^ bit) for p in range(n)])


def my_bit(hop):
    return (lax.axis_index(hop[0]) // hop[1]) % 2


def after(x, *others):
    return lax.optimization_barrier((x, others))[0]


def partner(hop):
    axis, bit = hop
    me = lax.axis_index(axis)
    return {axis: me + bit * (1 - 2 * ((me // bit) % 2))}


def gather_body(*refs, columns, core, orders, order):
    n, n_out = len(columns), 1 + max(c[0] for c in columns)
    ins, outs = refs[:n], refs[n : n + n_out]
    local, send, recv = refs[n + n_out :]
    place = tuple(my_bit(h) for h in order)

    def block(k, have, flip=None):
        out, start, width = columns[k]
        at = tuple(
            slice(None) if h in have else 1 - p if h == flip else p for h, p in zip(order, place)
        )
        return outs[out].at[at + (slice(None), pl.ds(start, width))]

    def copy(k, ref, hop, sem):
        moved = pltpu.make_async_remote_copy(
            src_ref=ref,
            dst_ref=ref,
            send_sem=send.at[k, sem],
            recv_sem=recv.at[k, sem],
            device_id=partner(hop),
            device_id_type=pl.DeviceIdType.MESH,
        )
        moved.start()
        return moved

    own = [pltpu.make_async_copy(ins[k], block(k, ()), local.at[k]) for k in range(n)]
    for c in own:
        c.start()
    barrier = pltpu.get_barrier_semaphore()
    for hop in order:
        pl.semaphore_signal(
            barrier, inc=1, device_id=partner(hop), device_id_type=pl.DeviceIdType.MESH
        )
    pl.semaphore_wait(barrier, len(order))
    for c in own:
        c.wait()
    steps = len(order) - 1
    far = [[] for _ in range(n)]
    near = [[] for _ in range(n)]
    for k in range(n):
        far[k].append(copy(k, block(k, ()), orders[k][0], 0))
        near[k].append(copy(k, block(k, ()), core, steps))
    for t in range(steps):
        for k in range(n):
            have = orders[k][:t]
            far[k][t].wait_recv()
            if t + 1 < steps:
                far[k].append(copy(k, block(k, orders[k][: t + 1]), orders[k][t + 1], t + 1))
            near[k].append(copy(k, block(k, have, orders[k][t]), core, steps + 1 + t))
    for k in range(n):
        for c in far[k]:
            c.wait_send()
        for c in near[k]:
            c.wait()


def gather_rows(stripes, columns, widths):
    core, xs, ys, zs, order = exchanges()
    orders = [zs + xs + ys, zs + ys + xs, xs + zs + ys, ys + zs + xs, xs + ys + zs]
    orders = [orders[k % len(orders)] for k in range(len(stripes))]
    rows, n = stripes[0].shape[0], len(stripes)
    outs = pl.pallas_call(
        functools.partial(gather_body, columns=columns, core=core, orders=orders, order=order),
        in_specs=[pl.BlockSpec(memory_space=pl.ANY)] * n,
        out_specs=[pl.BlockSpec(memory_space=pl.ANY)] * len(widths),
        out_shape=[
            jax.ShapeDtypeStruct((2,) * len(order) + (rows, w), stripes[0].dtype) for w in widths
        ],
        scratch_shapes=[
            pltpu.SemaphoreType.DMA((n,)),
            pltpu.SemaphoreType.DMA((n, 2 * len(order))),
            pltpu.SemaphoreType.DMA((n, 2 * len(order))),
        ],
        compiler_params=pltpu.CompilerParams(collective_id=0, has_side_effects=True),
    )(*stripes)
    return [o.reshape(rows << len(order), o.shape[-1]) for o in outs]


def sum_rows(stripes, work):
    core, xs, ys, zs, order = exchanges()
    hops = [[core] + h for h in (xs + ys + zs, ys + zs + xs, zs + xs + ys)]
    states = [[a.reshape((2,) * len(order) + (-1, a.shape[1])) for a in s] for s in stripes]
    names = [order] * len(stripes)
    made = []
    for step in range(len(order)):
        keep, send = [], []
        for arrays, held, hop in zip(states, names, [h[step] for h in hops]):
            at, bit = held.index(hop), my_bit(hop)
            for side, b in ((keep, bit), (send, 1 - bit)):
                side.append(
                    jnp.concatenate(
                        [lax.dynamic_index_in_dim(a, b, at, keepdims=False) for a in arrays], axis=-1
                    )
                )
        send = lax.optimization_barrier(send)
        got = [swap_bit(x, h[step]) for x, h in zip(send, hops)]
        if step < len(work):
            made.append(work[step](send))
            got = after(got, made[-1])
        got = lax.optimization_barrier(got)
        states = [[(k.astype(F32) + g.astype(F32)).astype(BF)] for k, g in zip(keep, got)]
        names = [[n for n in held if n != h[step]] for held, h in zip(names, hops)]
    return [arrays[0] for arrays in states], made


def rms_parts(v):
    return lax.rsqrt(jnp.mean(v * v, axis=-1, keepdims=True) + 1e-06)


def rms_back(v, gain, b):
    r = rms_parts(v)
    gb = gain * b
    grad = r * gb - v * (r * r * r * jnp.mean(v * gb, axis=-1, keepdims=True))
    return grad, jnp.sum(v * r * b, axis=tuple(range(v.ndim - 1)))


def gelu_and_slope(u):
    t = jnp.tanh(0.7978845608028654 * (u + 0.044715 * u * u * u))
    slope = 0.5 * (1.0 + t) + 0.5 * u * (1.0 - t * t) * (
        0.7978845608028654 * (1.0 + 3.0 * 0.044715 * u * u)
    )
    return 0.5 * u * (1.0 + t), slope


def on_device(
    decoder_input,
    encoder_out,
    cotangent,
    task_ids,
    passage_ids,
    target_lengths,
    query_embed,
    passage_bank,
    self_in,
    self_out,
    cross_query,
    cross_keyval,
    cross_out,
    hidden_in,
    hidden_output_weight,
    norm_gains,
    task_table,
):
    count, rows, width = decoder_input.shape
    group, npass, tokens, _ = encoder_out.shape
    keys = npass * tokens
    psg = lax.axis_size("psg")
    chips = psg // 2
    me = lax.axis_index("psg")
    chip, core = me // 2, me % 2
    shard = self_in.shape[0]
    ff = hidden_in.shape[1]
    n_tasks = task_table.shape[0]

    swap = [(p, p ^ 1) for p in range(psg)]

    def core_swap(x):
        return jax.tree.map(lambda a: lax.ppermute(a, "psg", swap), x)

    def chip_shift(x, step):
        perm = [(p, (p + 2 * step) % psg) for p in range(psg)]
        return jax.tree.map(lambda a: lax.ppermute(a, "psg", perm), x)

    def ids_of(chip_at, core_at):
        return (chip_at * 2 + core_at) * count + jnp.arange(count, dtype=jnp.int32)

    small = jnp.concatenate([norm_gains, task_table], axis=0).T
    small = jnp.pad(small, ((0, 0), (0, 128 - small.shape[1])))
    enc = encoder_out.reshape(group * keys, width)
    w_self_in, w_out, w_rest = gather_rows(
        [self_in[:, k * width : (k + 1) * width] for k in range(3)]
        + [self_out, jnp.concatenate([cross_query, small], axis=1)],
        [(0, 0, width), (0, width, width), (0, 2 * width, width), (1, 0, width), (2, 0, width + 128)],
        [3 * width, width, width + 128],
    )
    w_self_out, w_cross_query, w_small = w_out, w_rest[:, :width], w_rest[:, width:]
    w_keyval = lax.all_gather(cross_keyval, ALL, axis=0, tiled=True)

    embeds = jnp.take(passage_bank, passage_ids, axis=0).astype(F32)
    score = jnp.sum(query_embed[:, None, :] * embeds, axis=-1)
    others = [
        lax.ppermute(score, "psg", [(p, (p + k) % psg) for p in range(psg)]) for k in range(1, psg)
    ]
    every = jnp.concatenate([score] + others, axis=1)
    top = jnp.max(every, axis=1, keepdims=True)
    retrieval = jnp.exp(score - top) / jnp.sum(jnp.exp(every - top), axis=1, keepdims=True)

    smalls = w_small.T.astype(F32)
    gains, table = smalls[:3], smalls[3 : 3 + n_tasks]
    choose = task_ids[:, None] == jnp.arange(n_tasks, dtype=jnp.int32)[None, :]
    task_rows = jnp.sum(jnp.where(choose[:, :, None], table[None], 0.0), axis=1)

    stream = decoder_input.astype(F32) + task_rows[:, None, :]
    normed_one = (stream * rms_parts(stream) * gains[0]).astype(BF)
    col = lax.broadcasted_iota(jnp.int32, (1, 3 * width), 1)
    scale = jnp.where(col < width, QSCALE, 1.0)
    flat = (count * rows, width)
    qkv = (mm(normed_one.reshape(flat), w_self_in) * scale).astype(BF)
    qkv = qkv.reshape(count, rows, 3 * width)
    self_att, self_lse = self_fwd(target_lengths, qkv)
    second = lax.all_gather(
        after(jnp.concatenate([cross_out, hidden_in], axis=1), self_att), ALL, axis=0, tiled=True
    )
    w_cross_out, w_hidden_in = second[:, :width], second[:, width:]
    w_hidden_out = lax.all_gather(
        after(hidden_output_weight, self_att), ALL, axis=0, tiled=True
    )
    middle = stream + mm(self_att.reshape(flat), w_self_out).reshape(stream.shape)
    normed_two = (middle * rms_parts(middle) * gains[1]).astype(BF)
    own_q = (mm(normed_two.reshape(flat), w_cross_query) * QSCALE).astype(BF)
    own_q = own_q.reshape(count, rows, width)

    near_ids = (ids_of(chip, core), ids_of(chip, 1 - core))
    far_ids, far_same_q = [], []
    for step in range(1, chips):
        far_same_q.append([chip_shift(own_q[n : n + 1], step) for n in range(count)])
        source = (chip - step) % chips
        far_ids.append((ids_of(source, core), ids_of(source, 1 - core)))
    peer_q = core_swap(own_q)
    kv = keyval(after(enc, own_q), w_keyval).reshape(group, keys, 2 * width)
    peer_part = cross_fwd(near_ids[1], peer_q, kv, npass)
    latest = peer_part
    far_q, far_local, far_back = [], [], []
    for step in range(1, chips):
        queries, local, back = [], [], []
        for n in range(count):
            same_q = after(far_same_q[step - 1][n], latest)
            crossed_q = core_swap(same_q)
            same = cross_fwd(far_ids[step - 1][0][n : n + 1], same_q, kv, npass)
            crossed = cross_fwd(
                far_ids[step - 1][1][n : n + 1], after(crossed_q, same), kv, npass
            )
            value, joint = merge([same[:2], core_swap(crossed[:2])])
            latest = crossed
            back.append(chip_shift((value, joint), chips - step))
            local.append((same[1:], crossed[1:]))
            queries.append((same_q, crossed_q))
        far_q.append(queries)
        far_local.append(local)
        far_back.append(back)
    own_part = cross_fwd(near_ids[0], after(own_q, latest), kv, npass)
    parts = [own_part[:2], core_swap(peer_part[:2])]
    for back in far_back:
        parts.append(tuple(jnp.concatenate([b[k] for b in back], axis=0) for k in range(2)))
    cross_att, cross_lse, cross_sum = merge(parts, full=True)

    latter = middle + mm(cross_att.reshape(flat), w_cross_out).reshape(stream.shape)
    normed_three = (latter * rms_parts(latter) * gains[2]).astype(BF)
    hidden_pre = mm(normed_three.reshape(flat), w_hidden_in)
    activated, slope = gelu_and_slope(hidden_pre)
    activated = activated.astype(BF)
    output = (latter + mm(activated, w_hidden_out).reshape(stream.shape)).astype(BF)
    cot = cotangent.reshape(flat)
    grad_hidden_out = mm(activated, cot, TN).astype(BF)
    grad_pre = (mm(cot, w_hidden_out, NT) * slope).astype(BF)
    grad_hidden_in = mm(normed_three.reshape(flat), grad_pre, TN).astype(BF)
    grad_normed_three = mm(grad_pre, w_hidden_in, NT).reshape(stream.shape)
    grad_latter, gain_three = rms_back(latter, gains[2], grad_normed_three)
    grad_latter = grad_latter + cotangent.astype(F32)
    grad_cross_part = grad_latter.astype(BF)
    grad_cross_out = mm(cross_att.reshape(flat), grad_cross_part.reshape(flat), TN).astype(BF)
    grad_catt = mm(grad_cross_part.reshape(flat), w_cross_out, NT).astype(BF)
    grad_catt = grad_catt.reshape(count, rows, width)
    fold = hidden_output_weight.shape[0] // shard
    folded = grad_hidden_out.reshape(-1, fold, shard, width)
    folded = [folded[:, k].reshape(-1, width) for k in range(fold)]
    grad_second = jnp.concatenate([grad_cross_out, grad_hidden_in] + folded, axis=1)
    sum_second = lax.psum_scatter(grad_second, ALL, scatter_dimension=0, tiled=True)

    own_sent = (grad_catt, row_stats(grad_catt, cross_sum, cross_lse))
    far_same = [chip_shift(own_sent, step) for step in range(1, chips)]
    peer_sent = core_swap(own_sent)
    dq_own, dkv = cross_bwd(near_ids[0], own_q, kv, *after(own_sent, grad_second))
    far_same = [after(same, dq_own) for same in far_same]
    far_sent = [(same, core_swap(same)) for same in far_same]
    dq_peer, dkv = cross_bwd(near_ids[1], peer_q, kv, *after(peer_sent, dq_own), dkv)
    dq_back = core_swap(dq_peer)
    latest = dq_peer
    dq_parts = []
    for step in range(1, chips):
        same, crossed = far_sent[step - 1]
        back = []
        for n in range(count):
            same_q, crossed_q = far_q[step - 1][n]
            one = slice(n, n + 1)
            sent = [x[one] for x in after(crossed, latest)]
            dq_crossed, dkv = cross_bwd(far_ids[step - 1][1][one], crossed_q, kv, *sent, dkv)
            sent = [x[one] for x in same]
            dq_same, dkv = cross_bwd(far_ids[step - 1][0][one], same_q, kv, *sent, dkv)
            joint = (dq_same.astype(F32) + core_swap(dq_crossed).astype(F32)).astype(BF)
            latest = dq_same
            back.append(chip_shift(joint, chips - step))
        dq_parts.append(jnp.concatenate(back, axis=0))
    dkv_flat = after(dkv, joint).reshape(group * keys, 2 * width)
    grad_cross_keyval = mm(enc, dkv_flat, TN).astype(BF)
    total = dq_own.astype(F32) + dq_back.astype(F32)
    for dq in after(dq_parts, grad_cross_keyval, sum_second):
        total = total + dq.astype(F32)
    grad_cross_q = total.astype(BF).reshape(flat)
    grad_cross_query = mm(normed_two.reshape(flat), grad_cross_q, TN).astype(BF)

    grad_normed_two = mm(grad_cross_q, w_cross_query, NT).reshape(stream.shape)
    grad_middle, gain_two = rms_back(middle, gains[1], grad_normed_two)
    grad_middle = grad_middle + grad_latter
    grad_self_part = grad_middle.astype(BF).reshape(flat)
    grad_self_out = mm(self_att.reshape(flat), grad_self_part, TN).astype(BF)
    grad_satt = mm(grad_self_part, w_self_out, NT).astype(BF).reshape(count, rows, width)
    grad_qkv = self_bwd(target_lengths, qkv, grad_satt, self_lse)
    grad_qkv = grad_qkv.reshape(count * rows, 3 * width)
    grad_normed_one = mm(grad_qkv, w_self_in, NT).reshape(stream.shape)
    grad_stream, gain_one = rms_back(stream, gains[0], grad_normed_one)
    input_grad = grad_stream + grad_middle
    per_query = jnp.sum(input_grad, axis=1)
    grad_table = jnp.sum(jnp.where(choose[:, :, None], per_query[:, None, :], 0.0), axis=0)
    tiny = jnp.concatenate([jnp.stack([gain_one, gain_two, gain_three]), grad_table], axis=0).T
    tiny = jnp.pad(tiny, ((0, 0), (0, 128 - tiny.shape[1]))).astype(BF)
    grad_self_in = mm(normed_one.reshape(flat), grad_qkv, TN).astype(BF)

    def distillation(sent):
        sets = [
            (near_ids[0], *own_part[1:], own_sent[1]),
            (near_ids[1], *peer_part[1:], peer_sent[1]),
        ]
        for step in range(1, chips):
            for side in range(2):
                lse, share = (
                    jnp.concatenate([lo[side][k] for lo in far_local[step - 1]], axis=0)
                    for k in range(2)
                )
                sets.append((far_ids[step - 1][side], lse, share, far_sent[step - 1][side][1]))
        ids = jnp.concatenate([s[0] for s in sets])
        masses = []
        for _, lse, share, stats in sets:
            weight = jnp.exp2(lse - stats[:, :, :2])
            masses.append(jnp.sum(share * weight[:, :, :, None, :], axis=(1, 2, 4)) / (H * rows))
        masses = jnp.concatenate(masses, axis=0)
        place = ids[None, :] == jnp.arange(group, dtype=jnp.int32)[:, None]
        mass = jnp.sum(jnp.where(place[:, :, None], masses[None], 0.0), axis=1)
        query_grad = jnp.sum((after(retrieval, sent) - mass)[:, :, None] * embeds, axis=1)
        hop = 1
        while hop < psg:
            perm = [(p, p ^ hop) for p in range(psg)]
            query_grad = query_grad + lax.ppermute(query_grad, "psg", perm)
            hop *= 2
        return query_grad

    def encoder_part(sent):
        return mm(after(dkv_flat, sent), w_keyval, NT).reshape(encoder_out.shape)

    half = width // 2
    summed, (query_grad, encoder_grad) = sum_rows(
        [
            [grad_self_in[:, :width], grad_cross_query, tiny],
            [grad_self_in[:, width : 2 * width], grad_cross_keyval[:, :width], grad_self_out[:, :half]],
            [grad_self_in[:, 2 * width :], grad_cross_keyval[:, width:], grad_self_out[:, half:]],
        ],
        [distillation, encoder_part],
    )
    summed = [x.astype(F32) for x in summed]
    small_sum = summed[0][:, 2 * width :].T
    return (
        output,
        input_grad,
        encoder_grad,
        jnp.concatenate([x[:, :width] for x in summed], axis=1),
        jnp.concatenate([x[:, 2 * width :] for x in summed[1:]], axis=1),
        summed[0][:, width : 2 * width],
        jnp.concatenate([x[:, width : 2 * width] for x in summed[1:]], axis=1),
        sum_second[:, :width].astype(F32),
        sum_second[:, width : width + ff].astype(F32),
        jnp.concatenate(
            [sum_second[:, width * k : width * (k + 1)] for k in range(1 + ff // width, 1 + ff // width + fold)]
        ).astype(F32),
        small_sum[:3],
        small_sum[3 : 3 + n_tasks],
        query_grad,
    )


def solution(mesh):
    rows = P(ALL, None)
    tokens = P(ALL, None, None)
    passages = P("dp", "psg", None, None)
    columns = P(None, ALL)
    return jax.shard_map(
        on_device,
        mesh=mesh,
        in_specs=(tokens, passages, tokens, P(ALL), P("dp", "psg"), P(ALL), P("dp", None), P())
        + (rows,) * 7
        + (columns, columns),
        out_specs=(tokens, tokens, passages) + (rows,) * 7 + (columns, columns, P("dp", None)),
        check_vma=False,
    )
```

time: 923 us -> 704 us (0.76)
  waiting for transfers between devices: 293 us -> 63.5 us
  Pallas kernels: 249 us -> 321 us
  other arithmetic: 80.5 us -> 45.3 us
  local copies, waits for them, and re-layouts: 87.4 us -> 61.7 us
  matrix products: 176 us -> 153 us
  starting transfers between devices: 16 us -> 33.8 us
    reduce_scatter x3 -> x1, waiting for transfers between devices: 109 us -> 0.02 us  [on_device(): lax.psum_scatter(grad_second, ALL, scatter_dimension=0, tiled=True)]
    pallas_call x1 -> x7, Pallas kernels: 21.3 us -> 106 us  [the longest x1 56.2 us: gather_rows(): pl.pallas_call(functools.partial(gather_body, columns=columns, core=core,...]
    all_gather x3, waiting for transfers between devices: 69.6 us -> 0.02 us  [the longest x1 0.02 us: on_device(): lax.all_gather(after(jnp.concatenate([cross_out, hidden_in], axis=1), sel...]
    ppermute x9 -> x10, waiting for transfers between devices: 80.8 us -> 33 us  [chip_shift(): return jax.tree.map(lambda a: lax.ppermute(a, 'psg', perm), x)]
    unnamed x8 -> x4, waiting for transfers between devices: 28.1 us -> 0.73 us
    convert_element_type x1 -> x0, local copies, waits for them, and re-layouts: 24.6 us -> none  [on_device(): kv = mm(enc, w_cross_keyval).astype(BF).reshape(group, keys, 2 * width)]
    dot_general x21 -> x20, matrix products: 176 us -> 153 us  [mm(): return lax.dot_general(a, b, dims, preferred_element_type=F32)]
    ppermute x2 -> x17, waiting for transfers between devices: 4.63 us -> 28 us  [the longest x15 22.7 us: swap_bit(): return lax.ppermute(x, axis, [(p, p ^ bit) for p in range(n)])]
  transfers between devices with their start and end apart: 36 -> 50, of which waited for: 8 -> 12; matrix products, arithmetic and copies ran while one was open for 31% -> 22% of each run, Pallas kernels for 27% -> 42%
where the time goes in v2:
time: 704 us; the launch traced here: 694 us
  Pallas kernels  321 us (46%)
  matrix products  153 us (22%)
  waiting for transfers between devices  63.5 us (9%)
  local copies, waits for them, and re-layouts  61.7 us (9%)
  other arithmetic  45.3 us (6%)
  starting transfers between devices  33.8 us (5%)
  between operations  15.6 us (2%)
    dot_general x20, matrix products, mm(): return lax.dot_general(a, b, dims, preferred_element_type=F32)  153 us
    pallas_call x6, Pallas kernels, cross_bwd(): pl.pallas_call(functools.partial(cross_bwd_body, chunk=min(rows, 256)), g...  122 us
    pallas_call x6, Pallas kernels, cross_fwd(): pl.pallas_call(functools.partial(cross_fwd_body, npass=npass), grid_spec=...  68.6 us
    pallas_call x1, Pallas kernels, gather_rows(): pl.pallas_call(functools.partial(gather_body, columns=columns, core=core,...  56.2 us
    ppermute x10, waiting for transfers between devices, chip_shift(): return jax.tree.map(lambda a: lax.ppermute(a, 'psg', perm), x)  33 us
    unnamed x228, local copies, waits for them, and re-layouts  26.9 us
    pallas_call x1, Pallas kernels, self_bwd(): pl.pallas_call(functools.partial(self_bwd_body, chunk=min(rows, 256)), gr...  24.3 us
    ppermute x15, waiting for transfers between devices, swap_bit(): return lax.ppermute(x, axis, [(p, p ^ bit) for p in range(n)])  22.7 us
  transfers between devices with their start and end apart: 50, of which 12 were waited for; matrix products, arithmetic and copies ran while one was open for 22% of the time, Pallas kernels for 42%

profile of v2, /device:TPU:0, one launch (start us, length us, event | category | flops | bytes accessed | tf_op | source)
XLA Modules:
  0.0 694.0 jit_solution(8158111741748448929)
XLA Ops:
  11.8 56.2 %shard_map.264 = (bf16[2,2,2,2,2,24,2304]{6,5,4,3,2,1,0:T(8,128)(2,1)}, bf16[2,2,2,2,2,24,768]{6,5,4,3,2,1,0:T(8,128)(2,1)}, bf16[2,2,2,2,2,24,896]{6,5,4,3,2,1,0:T(8,128)(2,1)}) custom-call(bf16[24,768]{1,0:T(8,128)(2,1)} %get-tuple-element.363.refs_0_, bf16[24,768]{1,0:T(8,128)(2,1)} %get-tuple-element.364.refs_1_, ...), custom_call_target="tpu_custom_call" | custom-call | tf_op jit(solution)/shard_map/pallas_call | solution.py:515
  80.1 8.5 %multiply_convert_fusion.1 = bf16[1024,2304]{1,0:T(8,128)(2,1)} fusion(bf16[1024,768]{1,0:T(8,128)(2,1)} %bitcast.258, bf16[768,2304]{1,0:T(8,128)(2,1)} %bitcast.271, f32[2304]{0:T(1024)S(1)} %copy-done.88), kind=kOutput, calls=%fused_computation.12 | convolution fusion | flops 3628597248 | bytes 9839616 | tf_op jit(solution)/shard_map/dot_general | solution.py:29
  88.6 13.5 %shard_map.265 = (bf16[2,512,768]{2,1,0:T(8,128)(2,1)}, f32[2,6,2,512]{3,2,1,0:T(2,128)}) custom-call(s32[2]{0:T(128)} %length_ref.3, bf16[2,512,2304]{2,1,0:T(8,128)(2,1)} %bitcast.276, bf16[2,512,2304]{2,1,0:T(8,128)(2,1)} %bitcast.277, bf16[2,512,2304]{2,1,0:T(8,128)(2,1)} %bitcast.278), custom_call_target="tpu_custom_call" | custom-call | flops 6442450944 | bytes 6291456 | tf_op jit(solution)/shard_map/pallas_call | solution.py:226
  117.6 21.6 %shard_map.266 = bf16[6144,1536]{1,0:T(8,128)(2,1)} custom-call(bf16[6144,768]{1,0:T(8,128)(2,1)} %bitcast.269, bf16[768,1536]{1,0:T(8,128)(2,1)} %all-gather.4.cloned.1.call-done.w_ref), custom_call_target="tpu_custom_call" | custom-call | flops 14495514624 | bytes 28311552 | tf_op jit(solution)/shard_map/pallas_call | solution.py:403
  139.2 15.6 %shard_map.267 = (bf16[2,512,768]{2,1,0:T(8,128)(2,1)}, f32[2,6,2,512]{3,2,1,0:T(2,128)}, f32[2,6,2,2,512]{4,3,2,1,0:T(2,128)}) custom-call(s32[2]{0:T(128)} %iota_add_fusion.1.idx, bf16[2,512,768]{2,1,0:T(8,128)(2,1)} %collective-permute-done.2.q_ref, bf16[8,768,1536]{2,1,0:T(8,128)(2,1)} %bitcast.210, bf16[8,768,1536]{2,1,0:T(8,128)(2,1)} %bitcast.211), custom_call_target="tpu_custom_call" | custom-call | flops 9663676416 | bytes 7864320 | tf_op jit(solution)/shard_map/pallas_call | solution.py:100
  156.6 9.6 %shard_map.268 = (bf16[1,512,768]{2,1,0:T(8,128)(2,1)}, f32[1,6,2,512]{3,2,1,0:T(2,128)}, f32[1,6,2,2,512]{4,3,2,1,0:T(2,128)}) custom-call(s32[1]{0:T(128)} %get-tuple-element.370.idx, bf16[1,512,768]{2,1,0:T(8,128)(2,1)} %collective-permute-done.1.q_ref, bf16[8,768,1536]{2,1,0:T(8,128)(2,1)} %bitcast.212, bf16[8,768,1536]{2,1,0:T(8,128)(2,1)} %bitcast.213), custom_call_target="tpu_custom_call" | custom-call | flops 4831838208 | bytes 3932160 | tf_op jit(solution)/shard_map/pallas_call | solution.py:100
  167.0 9.3 %shard_map.269 = (bf16[1,512,768]{2,1,0:T(8,128)(2,1)}, f32[1,6,2,512]{3,2,1,0:T(2,128)}, f32[1,6,2,2,512]{4,3,2,1,0:T(2,128)}) custom-call(s32[1]{0:T(128)} %get-tuple-element.371.idx, bf16[1,512,768]{2,1,0:T(8,128)(2,1)} %copy-done.23, bf16[8,768,1536]{2,1,0:T(8,128)(2,1)} %bitcast.214, bf16[8,768,1536]{2,1,0:T(8,128)(2,1)} %bitcast.215), custom_call_target="tpu_custom_call" | custom-call | flops 4831838208 | bytes 3932160 | tf_op jit(solution)/shard_map/pallas_call | solution.py:100
  180.6 9.1 %shard_map.270 = (bf16[1,512,768]{2,1,0:T(8,128)(2,1)}, f32[1,6,2,512]{3,2,1,0:T(2,128)}, f32[1,6,2,2,512]{4,3,2,1,0:T(2,128)}) custom-call(s32[1]{0:T(128)} %get-tuple-element.369.idx, bf16[1,512,768]{2,1,0:T(8,128)(2,1)} %collective-permute-done.q_ref, bf16[8,768,1536]{2,1,0:T(8,128)(2,1)} %bitcast.216, bf16[8,768,1536]{2,1,0:T(8,128)(2,1)} %bitcast.217), custom_call_target="tpu_custom_call" | custom-call | flops 4831838208 | bytes 3932160 | tf_op jit(solution)/shard_map/pallas_call | solution.py:100
  190.6 9.4 %shard_map.271 = (bf16[1,512,768]{2,1,0:T(8,128)(2,1)}, f32[1,6,2,512]{3,2,1,0:T(2,128)}, f32[1,6,2,2,512]{4,3,2,1,0:T(2,128)}) custom-call(s32[1]{0:T(128)} %get-tuple-element.372.idx, bf16[1,512,768]{2,1,0:T(8,128)(2,1)} %copy-done.24, bf16[8,768,1536]{2,1,0:T(8,128)(2,1)} %bitcast.218, bf16[8,768,1536]{2,1,0:T(8,128)(2,1)} %bitcast.219), custom_call_target="tpu_custom_call" | custom-call | flops 4831838208 | bytes 3932160 | tf_op jit(solution)/shard_map/pallas_call | solution.py:100
  217.6 15.7 %shard_map.272 = (bf16[2,512,768]{2,1,0:T(8,128)(2,1)}, f32[2,6,2,512]{3,2,1,0:T(2,128)}, f32[2,6,2,2,512]{4,3,2,1,0:T(2,128)}) custom-call(s32[2]{0:T(128)} %copy-done.96, bf16[2,512,768]{2,1,0:T(8,128)(2,1)} %bitcast.9.q_ref, bf16[8,768,1536]{2,1,0:T(8,128)(2,1)} %bitcast.221, bf16[8,768,1536]{2,1,0:T(8,128)(2,1)} %bitcast.220), custom_call_target="tpu_custom_call" | custom-call | flops 9663676416 | bytes 7864320 | tf_op jit(solution)/shard_map/pallas_call | solution.py:100
  233.3 5.9 collective-permute-done.14
  239.9 15.7 %collective-permute-done.11 = bf16[1,512,768]{2,1,0:T(8,128)(2,1)S(1)} collective-permute-done((bf16[1,512,768]{2,1,0:T(8,128)(2,1)}, bf16[1,512,768]{2,1,0:T(8,128)(2,1)S(1)}, u32[]{:S(2)}, u32[]{:S(2)}) %collective-permute-start.11) | collective-permute-done | bytes 786464 | tf_op jit(solution)/shard_map/ppermute | solution.py:615
  258.0 5.3 shard_map.275
  268.1 5.1 fusion.11
  277.8 8.5 %convolution_convert_fusion = bf16[3072,768]{1,0:T(8,128)(2,1)} fusion(bf16[1024,768]{1,0:T(8,128)(2,1)S(1)} %bitcast.238, f32[1024,3072]{1,0:T(8,128)S(1)} %fusion.11), kind=kOutput, calls=%fused_computation.14 | convolution fusion | flops 4862509056 | bytes 18874368 | tf_op jit(solution)/shard_map/dot_general | solution.py:29
  286.3 14.8 %fusion.7 = bf16[1024,3072]{1,0:T(8,128)(2,1)S(1)} fusion(f32[1024,3072]{1,0:T(8,128)} %copy-done.106, bf16[3072,768]{1,0:T(8,128)(2,1)} %all-gather.8.cloned.1.call-done, bf16[1024,768]{1,0:T(8,128)(2,1)} %bitcast.237), kind=kOutput, calls=%fused_computation.10 | convolution fusion | flops 4891607040 | bytes 25165824 | tf_op jit(solution)/shard_map/dot_general | solution.py:29
  301.1 9.7 %fusion.9 = f32[1024,768]{1,0:T(8,128)S(1)} fusion(bf16[1024,3072]{1,0:T(8,128)(2,1)S(1)} %fusion.7, bf16[768,3840]{1,0:T(8,128)(2,1)} %all-gather.6.cloned.1.call-done), kind=kOutput, calls=%fused_computation.17 | convolution fusion | flops 4831838208 | bytes 14155776 | tf_op jit(solution)/shard_map/dot_general | solution.py:29
  333.6 9.2 %fusion.8 = bf16[768,6912]{1,0:T(8,128)(2,1)} fusion(bf16[768,6912]{1,0:T(8,128)(2,1)} %constant_dynamic-update-slice_fusion.4, bf16[1024,768]{1,0:T(8,128)(2,1)} %bitcast.260, bf16[1024,3072]{1,0:T(8,128)(2,1)} %copy-done.105), kind=kOutput, calls=%fused_computation.16 | convolution fusion | flops 4834197504 | bytes 12582912 | tf_op jit(solution)/shard_map/dot_general | solution.py:29
  347.9 13.0 %fusion.59 = f32[1024,768]{1,0:T(8,128)} fusion(bf16[3072,768]{1,0:T(8,128)(2,1)} %all-gather.8.cloned.1.call-done, f32[1024,3072]{1,0:T(8,128)} %copy-done.106), kind=kOutput, calls=%fused_computation.207 | convolution fusion | flops 4860149760 | bytes 20447232 | tf_op jit(solution)/shard_map/dot_general | solution.py:29
  360.9 28.8 %shard_map.277 = (bf16[2,512,768]{2,1,0:T(8,128)(2,1)}, bf16[8,768,1536]{2,1,0:T(8,128)(2,1)}) custom-call(s32[2]{0:T(128)} %copy-done.96, bf16[2,512,768]{2,1,0:T(8,128)(2,1)} %bitcast.9.q_ref, bf16[8,768,1536]{2,1,0:T(8,128)(2,1)} %bitcast.222, bf16[8,768,1536]{2,1,0:T(8,128)(2,1)} %bitcast.223, bf16[2,512,768]{2,1,0:T(8,128)(2,1)} %bitcast.21.do_ref, ...), custom_call_target="tpu_custom_call" | custom-call | flops 24159191040 | bytes 14155776 | tf_op jit(solution)/shard_map/pallas_call | solution.py:170
  395.2 29.0 %shard_map.278 = (bf16[2,512,768]{2,1,0:T(8,128)(2,1)}, bf16[8,768,1536]{2,1,0:T(8,128)(2,1)}) custom-call(s32[2]{0:T(128)} %iota_add_fusion.1.idx, bf16[2,512,768]{2,1,0:T(8,128)(2,1)} %collective-permute-done.2.q_ref, bf16[8,768,1536]{2,1,0:T(8,128)(2,1)} %bitcast.224, bf16[8,768,1536]{2,1,0:T(8,128)(2,1)} %bitcast.225, ...), custom_call_target="tpu_custom_call", output_to_operand_aliasing={{1}: (6, {})} | custom-call | flops 24159191040 | bytes 14155776 | tf_op jit(solution)/shard_map/pallas_call | solution.py:170
  426.6 16.0 %shard_map.279 = (bf16[1,512,768]{2,1,0:T(8,128)(2,1)}, bf16[8,768,1536]{2,1,0:T(8,128)(2,1)}) custom-call(s32[1]{0:T(128)} %get-tuple-element.371.idx, bf16[1,512,768]{2,1,0:T(8,128)(2,1)} %copy-done.23, bf16[8,768,1536]{2,1,0:T(8,128)(2,1)} %bitcast.226, bf16[8,768,1536]{2,1,0:T(8,128)(2,1)} %bitcast.227, ...), custom_call_target="tpu_custom_call", output_to_operand_aliasing={{1}: (6, {})} | custom-call | flops 12079595520 | bytes 7077888 | tf_op jit(solution)/shard_map/pallas_call | solution.py:170
  442.7 16.3 %shard_map.280 = (bf16[1,512,768]{2,1,0:T(8,128)(2,1)}, bf16[8,768,1536]{2,1,0:T(8,128)(2,1)}) custom-call(s32[1]{0:T(128)} %get-tuple-element.370.idx, bf16[1,512,768]{2,1,0:T(8,128)(2,1)} %collective-permute-done.1.q_ref, bf16[8,768,1536]{2,1,0:T(8,128)(2,1)} %bitcast.228, bf16[8,768,1536]{2,1,0:T(8,128)(2,1)} %bitcast.229, ...), custom_call_target="tpu_custom_call", output_to_operand_aliasing={{1}: (6, {})} | custom-call | flops 12079595520 | bytes 7077888 | tf_op jit(solution)/shard_map/pallas_call | solution.py:170
  460.5 16.1 %shard_map.281 = (bf16[1,512,768]{2,1,0:T(8,128)(2,1)}, bf16[8,768,1536]{2,1,0:T(8,128)(2,1)}) custom-call(s32[1]{0:T(128)} %get-tuple-element.372.idx, bf16[1,512,768]{2,1,0:T(8,128)(2,1)} %copy-done.24, bf16[8,768,1536]{2,1,0:T(8,128)(2,1)} %bitcast.230, bf16[8,768,1536]{2,1,0:T(8,128)(2,1)} %bitcast.231, ...), custom_call_target="tpu_custom_call", output_to_operand_aliasing={{1}: (6, {})} | custom-call | flops 12079595520 | bytes 7077888 | tf_op jit(solution)/shard_map/pallas_call | solution.py:170
  477.1 16.2 %shard_map.282 = (bf16[1,512,768]{2,1,0:T(8,128)(2,1)}, bf16[8,768,1536]{2,1,0:T(8,128)(2,1)}) custom-call(s32[1]{0:T(128)} %get-tuple-element.369.idx, bf16[1,512,768]{2,1,0:T(8,128)(2,1)} %collective-permute-done.q_ref, bf16[8,768,1536]{2,1,0:T(8,128)(2,1)} %bitcast.232, bf16[8,768,1536]{2,1,0:T(8,128)(2,1)} %bitcast.233, ...), custom_call_target="tpu_custom_call", output_to_operand_aliasing={{1}: (6, {})} | custom-call | flops 12079595520 | bytes 7077888 | tf_op jit(solution)/shard_map/pallas_call | solution.py:170
  497.0 21.2 %fusion.15 = bf16[768,1536]{1,0:T(8,128)(2,1)S(1)} fusion(bf16[6144,1536]{1,0:T(8,128)(2,1)} %bitcast.234, bf16[6144,768]{1,0:T(8,128)(2,1)} %bitcast.270), kind=kOutput, calls=%fused_computation.43 | convolution fusion | flops 14496694272 | bytes 30670848 | tf_op jit(solution)/shard_map/dot_general | solution.py:29
  519.8 11.5 %collective-permute-done.23 = bf16[1,512,768]{2,1,0:T(8,128)(2,1)S(1)} collective-permute-done((bf16[1,512,768]{2,1,0:T(8,128)(2,1)S(1)}, bf16[1,512,768]{2,1,0:T(8,128)(2,1)S(1)}, u32[]{:S(2)}, u32[]{:S(2)}) %collective-permute-start.23) | collective-permute-done | bytes 786464 | tf_op jit(solution)/shard_map/ppermute | solution.py:615
  532.6 5.8 multiply_reduce_fusion.1
  548.8 24.3 %shard_map.283 = bf16[2,512,2304]{2,1,0:T(8,128)(2,1)} custom-call(s32[2]{0:T(128)} %length_ref.3, bf16[2,512,2304]{2,1,0:T(8,128)(2,1)} %bitcast.279, bf16[2,512,2304]{2,1,0:T(8,128)(2,1)} %bitcast.280, bf16[2,512,2304]{2,1,0:T(8,128)(2,1)} %bitcast.281, bf16[2,512,768]{2,1,0:T(8,128)(2,1)} %bitcast.282, f32[2,6,2,512]{3,2,1,0:T(2,128)} %get-tuple-element.173.lse_ref), custom_call_target="tpu_custom_call" | custom-call | flops 16106127360 | bytes 12582912 | tf_op jit(solution)/shard_map/pallas_call | solution.py:300
  573.1 6.8 bitcast_convert_fusion
  620.7 21.2 %fusion.76 = f32[6144,768]{1,0:T(8,128)} fusion(bf16[6144,1536]{1,0:T(8,128)(2,1)} %bitcast.235, bf16[768,1536]{1,0:T(8,128)(2,1)S(1)} %copy-done.100), kind=kOutput, calls=%fused_computation.224 | convolution fusion | flops 14495514624 | bytes 40108032 | tf_op jit(solution)/shard_map/dot_general | solution.py:29
  650.6 9.3 %collective-permute-done.38 = bf16[2,2,24,1920]{3,2,1,0:T(8,128)(2,1)S(1)} collective-permute-done((bf16[2,2,24,1920]{3,2,1,0:T(8,128)(2,1)S(1)}, bf16[2,2,24,1920]{3,2,1,0:T(8,128)(2,1)S(1)}, u32[]{:S(2)}, u32[]{:S(2)}) %collective-permute-start.38) | collective-permute-done | bytes 368672 | tf_op jit(solution)/shard_map/ppermute | solution.py:437
  (483 shorter events, 200.4 us)
Async XLA Ops:
  7.2 110.4 %all-gather.4.cloned.1.call-start = ((), (), s32[]{:S(2)}) async-start(), calls=%async_computation.1 | async-start | bytes 2433024 | tf_op jit(solution)/shard_map/all_gather | solution.py:630
  7.9 255.4 %all-gather.6.cloned.1.call-start = ((), (), s32[]{:S(2)}) async-start(), calls=%async_computation.2 | async-start | bytes 6082560 | tf_op jit(solution)/shard_map/all_gather | solution.py:654
  102.2 184.2 %all-gather.8.cloned.1.call-start = ((), (), s32[]{:S(2)}) async-start(), calls=%async_computation.3 | async-start | bytes 4866048 | tf_op jit(solution)/shard_map/all_gather | solution.py:658
  113.7 41.1 %collective-permute-start.1 = (bf16[1,512,768]{2,1,0:T(8,128)(2,1)}, bf16[1,512,768]{2,1,0:T(8,128)(2,1)}, u32[]{:S(2)}, u32[]{:S(2)}) collective-permute-start(bf16[1,512,768]{2,1,0:T(8,128)(2,1)} %get-tuple-element.329), channel_id=1, source_target_pairs={{0,2},{1,3},{2,0},{3,1},{4,6},{5,7},{6,4},{7,5},{8,10},{9,11},{10,... | collective-permute-start | bytes 2359304 | tf_op jit(solution)/shard_map/ppermute | solution.py:615
  115.1 61.3 %collective-permute-start = (bf16[1,512,768]{2,1,0:T(8,128)(2,1)}, bf16[1,512,768]{2,1,0:T(8,128)(2,1)}, u32[]{:S(2)}, u32[]{:S(2)}) collective-permute-start(bf16[1,512,768]{2,1,0:T(8,128)(2,1)} %get-tuple-element.330), channel_id=1, source_target_pairs={{0,2},{1,3},{2,0},{3,1},{4,6},{5,7},{6,4},{7,5},{8,10},{9,11},{10,... | collective-permute-start | bytes 2359304 | tf_op jit(solution)/shard_map/ppermute | solution.py:615
  115.7 23.5 %collective-permute-start.2 = (bf16[2,512,768]{2,1,0:T(8,128)(2,1)}, bf16[2,512,768]{2,1,0:T(8,128)(2,1)}, u32[]{:S(2)}, u32[]{:S(2)}) collective-permute-start(bf16[2,512,768]{2,1,0:T(8,128)(2,1)} %bitcast.9.q_ref), channel_id=1, source_target_pairs={{0,1},{1,0},{2,3},{3,2},{4,5},{5,4},{6,7},{7,6},{8,9},{9,8},{10,11... | collective-permute-start | bytes 4718600 | tf_op jit(solution)/shard_map/ppermute | solution.py:611
  115.8 416.8 %reduce-scatter.2.cloned.1.call-start = ((), (), s32[]{:S(2)}) async-start(), calls=%async_computation.4 | async-start | bytes 10948608 | tf_op jit(solution)/shard_map/reduce_scatter | solution.py:721
  176.7 24.0 %collective-permute-start.31 = (f32[8,2]{1,0:T(8,128)S(1)}, f32[8,2]{1,0:T(8,128)S(1)}, u32[]{:S(2)}, u32[]{:S(2)}) collective-permute-start(f32[8,2]{1,0:T(8,128)S(1)} %fusion.41), channel_id=1, source_target_pairs={{0,3},{1,0},{2,1},{3,2},{4,7},{5,4},{6,5},{7,6},{8,11},{9,8},{10,9... | collective-permute-start | bytes 200 | tf_op jit(solution)/shard_map/ppermute | solution.py:635
  178.2 22.6 %collective-permute-start.30 = (f32[8,2]{1,0:T(8,128)S(1)}, f32[8,2]{1,0:T(8,128)S(1)}, u32[]{:S(2)}, u32[]{:S(2)}) collective-permute-start(f32[8,2]{1,0:T(8,128)S(1)} %fusion.41), channel_id=1, source_target_pairs={{0,2},{1,3},{2,0},{3,1},{4,6},{5,7},{6,4},{7,5},{8,10},{9,11},{10,... | collective-permute-start | bytes 200 | tf_op jit(solution)/shard_map/ppermute | solution.py:635
  178.8 22.1 %collective-permute-start.29 = (f32[8,2]{1,0:T(8,128)S(1)}, f32[8,2]{1,0:T(8,128)S(1)}, u32[]{:S(2)}, u32[]{:S(2)}) collective-permute-start(f32[8,2]{1,0:T(8,128)S(1)} %fusion.41), channel_id=1, source_target_pairs={{0,1},{1,2},{2,3},{3,0},{4,5},{5,6},{6,7},{7,4},{8,9},{9,10},{10,1... | collective-permute-start | bytes 200 | tf_op jit(solution)/shard_map/ppermute | solution.py:635
  179.1 25.6 %collective-permute-start.6 = (bf16[1,512,768]{2,1,0:T(8,128)(2,1)}, bf16[1,512,768]{2,1,0:T(8,128)(2,1)S(1)}, u32[]{:S(2)}, u32[]{:S(2)}) collective-permute-start(bf16[1,512,768]{2,1,0:T(8,128)(2,1)} %get-tuple-element.126), channel_id=1, source_target_pairs={{0,1},{1,0},{2,3},{3,2},{4,5},{5,4},{6,7},{7,6},{8,9},{9,8},{10,11... | collective-permute-start | bytes 2359304 | tf_op jit(solution)/shard_map/ppermute | solution.py:611
  201.0 55.9 %collective-permute-start.5 = (bf16[2,512,768]{2,1,0:T(8,128)(2,1)}, bf16[2,512,768]{2,1,0:T(8,128)(2,1)S(1)}, u32[]{:S(2)}, u32[]{:S(2)}) collective-permute-start(bf16[2,512,768]{2,1,0:T(8,128)(2,1)} %get-tuple-element.118), channel_id=1, source_target_pairs={{0,1},{1,0},{2,3},{3,2},{4,5},{5,4},{6,7},{7,6},{8,9},{9,8},{10,11... | collective-permute-start | bytes 4718600 | tf_op jit(solution)/shard_map/ppermute | solution.py:611
  209.1 24.2 %collective-permute-start.13 = (f32[1,6,2,512]{3,2,1,0:T(2,128)}, f32[1,6,2,512]{3,2,1,0:T(2,128)S(1)}, u32[]{:S(2)}, u32[]{:S(2)}) collective-permute-start(f32[1,6,2,512]{3,2,1,0:T(2,128)} %get-tuple-element.142), channel_id=1, source_target_pairs={{0,2},{1,3},{2,0},{3,1},{4,6},{5,7},{6,4},{7,5},{8,10},{9,11},{10,... | collective-permute-start | bytes 73736 | tf_op jit(solution)/shard_map/ppermute | solution.py:615
  209.8 30.1 %collective-permute-start.8 = (bf16[1,512,768]{2,1,0:T(8,128)(2,1)}, bf16[1,512,768]{2,1,0:T(8,128)(2,1)S(1)}, u32[]{:S(2)}, u32[]{:S(2)}) collective-permute-start(bf16[1,512,768]{2,1,0:T(8,128)(2,1)} %get-tuple-element.139), channel_id=1, source_target_pairs={{0,2},{1,3},{2,0},{3,1},{4,6},{5,7},{6,4},{7,5},{8,10},{9,11},{10,... | collective-permute-start | bytes 2359304 | tf_op jit(solution)/shard_map/ppermute | solution.py:615
  215.6 23.7 %collective-permute-start.14 = (f32[1,6,2,512]{3,2,1,0:T(2,128)}, f32[1,6,2,512]{3,2,1,0:T(2,128)S(1)}, u32[]{:S(2)}, u32[]{:S(2)}) collective-permute-start(f32[1,6,2,512]{3,2,1,0:T(2,128)} %get-tuple-element.143), channel_id=1, source_target_pairs={{0,2},{1,3},{2,0},{3,1},{4,6},{5,7},{6,4},{7,5},{8,10},{9,11},{10,... | collective-permute-start | bytes 73736 | tf_op jit(solution)/shard_map/ppermute | solution.py:615
  216.2 39.4 %collective-permute-start.11 = (bf16[1,512,768]{2,1,0:T(8,128)(2,1)}, bf16[1,512,768]{2,1,0:T(8,128)(2,1)S(1)}, u32[]{:S(2)}, u32[]{:S(2)}) collective-permute-start(bf16[1,512,768]{2,1,0:T(8,128)(2,1)} %get-tuple-element.140), channel_id=1, source_target_pairs={{0,2},{1,3},{2,0},{3,1},{4,6},{5,7},{6,4},{7,5},{8,10},{9,11},{10,... | collective-permute-start | bytes 2359304 | tf_op jit(solution)/shard_map/ppermute | solution.py:615
  233.3 23.6 %collective-permute-start.12 = (f32[2,6,2,512]{3,2,1,0:T(2,128)S(1)}, f32[2,6,2,512]{3,2,1,0:T(2,128)S(1)}, u32[]{:S(2)}, u32[]{:S(2)}) collective-permute-start(f32[2,6,2,512]{3,2,1,0:T(2,128)S(1)} %copy-done.62), channel_id=1, source_target_pairs={{0,1},{1,0},{2,3},{3,2},{4,5},{5,4},{6,7},{7,6},{8,9},{9,8},{10,11... | collective-permute-start | bytes 147464 | tf_op jit(solution)/shard_map/ppermute | solution.py:611
  324.8 67.1 %collective-permute-start.19 = (f32[2,6,4,512]{3,2,1,0:T(4,128)}, f32[2,6,4,512]{3,2,1,0:T(4,128)S(1)}, u32[]{:S(2)}, u32[]{:S(2)}) collective-permute-start(f32[2,6,4,512]{3,2,1,0:T(4,128)} %shard_map.276.stat_ref), channel_id=1, source_target_pairs={{0,2},{1,3},{2,0},{3,1},{4,6},{5,7},{6,4},{7,5},{8,10},{9,11},{10,... | collective-permute-start | bytes 294920 | tf_op jit(solution)/shard_map/ppermute | solution.py:615
  325.9 65.2 %collective-permute-start.16 = (f32[2,6,4,512]{3,2,1,0:T(4,128)}, f32[2,6,4,512]{3,2,1,0:T(4,128)S(1)}, u32[]{:S(2)}, u32[]{:S(2)}) collective-permute-start(f32[2,6,4,512]{3,2,1,0:T(4,128)} %shard_map.276.stat_ref), channel_id=1, source_target_pairs={{0,1},{1,0},{2,3},{3,2},{4,5},{5,4},{6,7},{7,6},{8,9},{9,8},{10,11... | collective-permute-start | bytes 294920 | tf_op jit(solution)/shard_map/ppermute | solution.py:611
  325.9 66.0 %collective-permute-start.18 = (bf16[2,512,768]{2,1,0:T(8,128)(2,1)}, bf16[2,512,768]{2,1,0:T(8,128)(2,1)}, u32[]{:S(2)}, u32[]{:S(2)}) collective-permute-start(bf16[2,512,768]{2,1,0:T(8,128)(2,1)} %bitcast.21.do_ref), channel_id=1, source_target_pairs={{0,2},{1,3},{2,0},{3,1},{4,6},{5,7},{6,4},{7,5},{8,10},{9,11},{10,... | collective-permute-start | bytes 4718600 | tf_op jit(solution)/shard_map/ppermute | solution.py:615
  326.8 65.1 %collective-permute-start.15 = (bf16[2,512,768]{2,1,0:T(8,128)(2,1)}, bf16[2,512,768]{2,1,0:T(8,128)(2,1)}, u32[]{:S(2)}, u32[]{:S(2)}) collective-permute-start(bf16[2,512,768]{2,1,0:T(8,128)(2,1)} %bitcast.21.do_ref), channel_id=1, source_target_pairs={{0,1},{1,0},{2,3},{3,2},{4,5},{5,4},{6,7},{7,6},{8,9},{9,8},{10,11... | collective-permute-start | bytes 4718600 | tf_op jit(solution)/shard_map/ppermute | solution.py:611
  391.9 33.1 %collective-permute-start.21 = (f32[2,6,4,512]{3,2,1,0:T(4,128)S(1)}, f32[2,6,4,512]{3,2,1,0:T(4,128)S(1)}, u32[]{:S(2)}, u32[]{:S(2)}) collective-permute-start(f32[2,6,4,512]{3,2,1,0:T(4,128)S(1)} %collective-permute-done.19), channel_id=1, source_target_pairs={{0,1},{1,0},{2,3},{3,2},{4,5},{5,4},{6,7},{7,6},{8,9},{9,8},{10,11... | collective-permute-start | bytes 294920 | tf_op jit(solution)/shard_map/ppermute | solution.py:611
  392.2 32.8 %collective-permute-start.20 = (bf16[2,512,768]{2,1,0:T(8,128)(2,1)}, bf16[2,512,768]{2,1,0:T(8,128)(2,1)S(1)}, u32[]{:S(2)}, u32[]{:S(2)}) collective-permute-start(bf16[2,512,768]{2,1,0:T(8,128)(2,1)} %collective-permute-done.18), channel_id=1, source_target_pairs={{0,1},{1,0},{2,3},{3,2},{4,5},{5,4},{6,7},{7,6},{8,9},{9,8},{10,11... | collective-permute-start | bytes 4718600 | tf_op jit(solution)/shard_map/ppermute | solution.py:611
  424.8 107.8 %collective-permute-start.17 = (bf16[2,512,768]{2,1,0:T(8,128)(2,1)}, bf16[2,512,768]{2,1,0:T(8,128)(2,1)}, u32[]{:S(2)}, u32[]{:S(2)}) collective-permute-start(bf16[2,512,768]{2,1,0:T(8,128)(2,1)} %get-tuple-element.155), channel_id=1, source_target_pairs={{0,1},{1,0},{2,3},{3,2},{4,5},{5,4},{6,7},{7,6},{8,9},{9,8},{10,11... | collective-permute-start | bytes 4718600 | tf_op jit(solution)/shard_map/ppermute | solution.py:611
  476.6 16.7 %collective-permute-start.24 = (bf16[1,512,768]{2,1,0:T(8,128)(2,1)}, bf16[1,512,768]{2,1,0:T(8,128)(2,1)S(1)}, u32[]{:S(2)}, u32[]{:S(2)}) collective-permute-start(bf16[1,512,768]{2,1,0:T(8,128)(2,1)} %get-tuple-element.169), channel_id=1, source_target_pairs={{0,1},{1,0},{2,3},{3,2},{4,5},{5,4},{6,7},{7,6},{8,9},{9,8},{10,11... | collective-permute-start | bytes 2359304 | tf_op jit(solution)/shard_map/ppermute | solution.py:611
  476.8 18.9 %collective-permute-start.22 = (bf16[1,512,768]{2,1,0:T(8,128)(2,1)S(1)}, bf16[1,512,768]{2,1,0:T(8,128)(2,1)S(1)}, u32[]{:S(2)}, u32[]{:S(2)}) collective-permute-start(bf16[1,512,768]{2,1,0:T(8,128)(2,1)S(1)} %copy-done.102), channel_id=1, source_target_pairs={{0,1},{1,0},{2,3},{3,2},{4,5},{5,4},{6,7},{7,6},{8,9},{9,8},{10,11... | collective-permute-start | bytes 2359304 | tf_op jit(solution)/shard_map/ppermute | solution.py:611
  494.6 25.1 %collective-permute-start.25 = (bf16[1,512,768]{2,1,0:T(8,128)(2,1)S(1)}, bf16[1,512,768]{2,1,0:T(8,128)(2,1)S(1)}, u32[]{:S(2)}, u32[]{:S(2)}) collective-permute-start(bf16[1,512,768]{2,1,0:T(8,128)(2,1)S(1)} %add_convert_fusion.5), channel_id=1, source_target_pairs={{0,2},{1,3},{2,0},{3,1},{4,6},{5,7},{6,4},{7,5},{8,10},{9,11},{10,... | collective-permute-start | bytes 2359304 | tf_op jit(solution)/shard_map/ppermute | solution.py:615
  495.9 35.3 %collective-permute-start.23 = (bf16[1,512,768]{2,1,0:T(8,128)(2,1)S(1)}, bf16[1,512,768]{2,1,0:T(8,128)(2,1)S(1)}, u32[]{:S(2)}, u32[]{:S(2)}) collective-permute-start(bf16[1,512,768]{2,1,0:T(8,128)(2,1)S(1)} %add_convert_fusion.6), channel_id=1, source_target_pairs={{0,2},{1,3},{2,0},{3,1},{4,6},{5,7},{6,4},{7,5},{8,10},{9,11},{10,... | collective-permute-start | bytes 2359304 | tf_op jit(solution)/shard_map/ppermute | solution.py:615
  618.5 23.4 %collective-permute-start.34 = (bf16[2,2,2,24,1664]{4,3,2,1,0:T(8,128)(2,1)S(1)}, bf16[2,2,2,24,1664]{4,3,2,1,0:T(8,128)(2,1)S(1)}, u32[]{:S(2)}, u32[]{:S(2)}) collective-permute-start(bf16[2,2,2,24,1664]{4,3,2,1,0:T(8,128)(2,1)S(1)} %dynamic-slice_bitcast_fusion.2), channel_id=1, source_target_pairs={{0,4},{4,0},{8,12},{12,8},{16,20},{20,16},{24,28},{28,24},{1,5},{5... | collective-permute-start | bytes 1916936 | tf_op jit(solution)/shard_map/ppermute | solution.py:437
  619.5 22.4 %collective-permute-start.35 = (bf16[2,2,2,24,1920]{4,3,2,1,0:T(8,128)(2,1)S(1)}, bf16[2,2,2,24,1920]{4,3,2,1,0:T(8,128)(2,1)S(1)}, u32[]{:S(2)}, u32[]{:S(2)}) collective-permute-start(bf16[2,2,2,24,1920]{4,3,2,1,0:T(8,128)(2,1)S(1)} %dynamic-slice_bitcast_fusion.1), channel_id=1, source_target_pairs={{0,2},{1,3},{2,0},{3,1},{4,6},{5,7},{6,4},{7,5},{8,10},{9,11},{10,... | collective-permute-start | bytes 2211848 | tf_op jit(solution)/shard_map/ppermute | solution.py:437
  620.7 21.2 %collective-permute-start.36 = (bf16[2,2,2,24,1920]{4,3,2,1,0:T(8,128)(2,1)S(1)}, bf16[2,2,2,24,1920]{4,3,2,1,0:T(8,128)(2,1)S(1)}, u32[]{:S(2)}, u32[]{:S(2)}) collective-permute-start(bf16[2,2,2,24,1920]{4,3,2,1,0:T(8,128)(2,1)S(1)} %dynamic-slice_bitcast_fusion), channel_id=1, source_target_pairs={{0,8},{4,12},{8,0},{12,4},{16,24},{20,28},{24,16},{28,20},{1,9},{5... | collective-permute-start | bytes 2211848 | tf_op jit(solution)/shard_map/ppermute | solution.py:437
  645.5 17.9 %collective-permute-start.39 = (bf16[2,2,24,1920]{3,2,1,0:T(8,128)(2,1)S(1)}, bf16[2,2,24,1920]{3,2,1,0:T(8,128)(2,1)S(1)}, u32[]{:S(2)}, u32[]{:S(2)}) collective-permute-start(bf16[2,2,24,1920]{3,2,1,0:T(8,128)(2,1)S(1)} %dynamic-slice_bitcast_fusion.15), channel_id=1, source_target_pairs={{0,16},{4,20},{8,24},{12,28},{16,0},{20,4},{24,8},{28,12},{1,17},{... | collective-permute-start | bytes 1105928 | tf_op jit(solution)/shard_map/ppermute | solution.py:437
  (129 other events, 1497.4 us)
Sparse Core Ops, SparseCore 0:
  10.9 77.1 all-gather.3
  102.3 71.4 all-gather.5
  176.7 71.8 all-gather.7
  348.0 143.6 reduce-scatter.1

commit v3 on v2

--- a/solution.py
+++ b/solution.py
@@ -399,7 +399,7 @@
 def keyval(enc, w):
     n, depth = enc.shape
     width = w.shape[1]
-    block = 512
+    block = 1024
     return pl.pallas_call(
         keyval_body,
         grid=(n // block,),
@@ -414,6 +414,113 @@
             flops=2 * n * depth * width, bytes_accessed=2 * n * (depth + width), transcendentals=0
         ),
     )(enc, w)
+
+
+def feed_forward_body(
+    middle_ref,
+    att_ref,
+    cot_ref,
+    gain_ref,
+    w_out_ref,
+    w_in_ref,
+    w_down_ref,
+    out_ref,
+    grad_ref,
+    catt_ref,
+    gain_grad_ref,
+    w_grad_ref,
+    latter,
+    normed,
+    hidden,
+    slopes,
+    total,
+    back,
+):
+    step = pl.program_id(0)
+    last = pl.num_programs(0) - 1
+    gain = gain_ref[...]
+
+    @pl.when(step == 0)
+    def _():
+        v = middle_ref[...] + dot(att_ref[...], w_out_ref[...])
+        latter[...] = v
+        normed[...] = (v * rms_parts(v) * gain).astype(BF)
+
+    @pl.when((step < last) & (step % 2 == 0))
+    def _():
+        act, slope = gelu_and_slope(dot(normed[...], w_in_ref[...]))
+        hidden[...] = act.astype(BF)
+        slopes[...] = (dot(cot_ref[...], w_down_ref[...], NT) * slope).astype(BF)
+        more = dot(slopes[...], w_in_ref[...], NT)
+        back[...] = jnp.where(step == 0, more, back[...] + more)
+        w_grad_ref[...] = dot(normed[...], slopes[...], TN).astype(BF)
+
+    @pl.when((step < last) & (step % 2 == 1))
+    def _():
+        more = dot(hidden[...], w_down_ref[...])
+        total[...] = jnp.where(step == 1, more, total[...] + more)
+        w_grad_ref[...] = dot(hidden[...], cot_ref[...], TN).astype(BF)
+
+    @pl.when(step == last)
+    def _():
+        v, b = latter[...], back[...]
+        out_ref[...] = (v + total[...]).astype(BF)
+        r = rms_parts(v)
+        gb = gain * b
+        grad = r * gb - v * (r * r * r * jnp.mean(v * gb, axis=-1, keepdims=True))
+        grad = cot_ref[...].astype(F32) + grad
+        gain_grad_ref[...] = jnp.sum(v * r * b, axis=0, keepdims=True)
+        grad_ref[...] = grad
+        hidden[...] = grad.astype(BF)
+        catt_ref[...] = dot(hidden[...], w_out_ref[...], NT).astype(BF)
+        w_grad_ref[...] = dot(att_ref[...], hidden[...], TN).astype(BF)
+
+
+def feed_forward(middle, att, cot, gain, weights):
+    tokens, width = middle.shape
+    chunks = (weights.shape[1] // width - 1) // 2
+    steps = 2 * chunks + 1
+
+    def whole(rows, columns):
+        return pl.BlockSpec((rows, columns), lambda s: (0, 0))
+
+    def chunk_of(s):
+        return jnp.minimum(s // 2, chunks - 1)
+
+    square = (width, width)
+    wide = [pltpu.VMEM((tokens, width), t) for t in (F32, BF, BF, BF, F32, F32)]
+    return pl.pallas_call(
+        feed_forward_body,
+        grid=(steps,),
+        in_specs=[whole(tokens, width)] * 3
+        + [
+            whole(1, width),
+            whole(*square),
+            pl.BlockSpec(square, lambda s: (0, 1 + chunk_of(s))),
+            pl.BlockSpec(square, lambda s: (0, 1 + chunks + chunk_of(s))),
+        ],
+        out_specs=[whole(tokens, width)] * 3
+        + [
+            whole(1, width),
+            pl.BlockSpec(
+                square, lambda s: (0, jnp.where(s == steps - 1, 0, 1 + s // 2 + chunks * (s % 2)))
+            ),
+        ],
+        out_shape=[
+            jax.ShapeDtypeStruct((tokens, width), BF),
+            jax.ShapeDtypeStruct((tokens, width), F32),
+            jax.ShapeDtypeStruct((tokens, width), BF),
+            jax.ShapeDtypeStruct((1, width), F32),
+            jax.ShapeDtypeStruct(weights.shape, BF),
+        ],
+        scratch_shapes=wide,
+        compiler_params=params(),
+        cost_estimate=pl.CostEstimate(
+            flops=2 * tokens * width * width * (6 * chunks + 3),
+            bytes_accessed=tokens * width * 14 + 4 * width * weights.shape[1],
+            transcendentals=tokens * width * chunks,
+        ),
+    )(middle, att, cot, gain, weights, weights, weights)
 
 
 def bits_below(n):
@@ -651,17 +758,22 @@
     qkv = (mm(normed_one.reshape(flat), w_self_in) * scale).astype(BF)
     qkv = qkv.reshape(count, rows, 3 * width)
     self_att, self_lse = self_fwd(target_lengths, qkv)
-    second = lax.all_gather(
-        after(jnp.concatenate([cross_out, hidden_in], axis=1), self_att), ALL, axis=0, tiled=True
-    )
-    w_cross_out, w_hidden_in = second[:, :width], second[:, width:]
-    w_hidden_out = lax.all_gather(
-        after(hidden_output_weight, self_att), ALL, axis=0, tiled=True
-    )
     middle = stream + mm(self_att.reshape(flat), w_self_out).reshape(stream.shape)
     normed_two = (middle * rms_parts(middle) * gains[1]).astype(BF)
     own_q = (mm(normed_two.reshape(flat), w_cross_query) * QSCALE).astype(BF)
     own_q = own_q.reshape(count, rows, width)
+
+    n_dev = width // shard
+    fold = hidden_output_weight.shape[0] // shard
+    in_turn = after(hidden_in, own_q).reshape(shard, n_dev, fold, shard)
+    in_turn = in_turn.swapaxes(1, 2).reshape(shard, ff)
+    folded = [hidden_output_weight[shard * k : shard * (k + 1)] for k in range(fold)]
+    second = lax.all_gather(
+        jnp.concatenate([cross_out, in_turn] + folded, axis=1),
+        ALL,
+        axis=0,
+        tiled=True,
+    )
 
     near_ids = (ids_of(chip, core), ids_of(chip, 1 - core))
     far_ids, far_same_q = [], []
@@ -672,19 +784,18 @@
     peer_q = core_swap(own_q)
     kv = keyval(after(enc, own_q), w_keyval).reshape(group, keys, 2 * width)
     peer_part = cross_fwd(near_ids[1], peer_q, kv, npass)
-    latest = peer_part
+    latest, crossed = peer_part, None
     far_q, far_local, far_back = [], [], []
     for step in range(1, chips):
         queries, local, back = [], [], []
         for n in range(count):
-            same_q = after(far_same_q[step - 1][n], latest)
+            same_q = after(far_same_q[step - 1][n], peer_part if crossed is None else crossed)
             crossed_q = core_swap(same_q)
             same = cross_fwd(far_ids[step - 1][0][n : n + 1], same_q, kv, npass)
-            crossed = cross_fwd(
-                far_ids[step - 1][1][n : n + 1], after(crossed_q, same), kv, npass
-            )
+            crossed_q = after(crossed_q, same, latest)
+            crossed = cross_fwd(far_ids[step - 1][1][n : n + 1], crossed_q, kv, npass)
             value, joint = merge([same[:2], core_swap(crossed[:2])])
-            latest = crossed
+            latest = value
             back.append(chip_shift((value, joint), chips - step))
             local.append((same[1:], crossed[1:]))
             queries.append((same_q, crossed_q))
@@ -697,27 +808,11 @@
         parts.append(tuple(jnp.concatenate([b[k] for b in back], axis=0) for k in range(2)))
     cross_att, cross_lse, cross_sum = merge(parts, full=True)
 
-    latter = middle + mm(cross_att.reshape(flat), w_cross_out).reshape(stream.shape)
-    normed_three = (latter * rms_parts(latter) * gains[2]).astype(BF)
-    hidden_pre = mm(normed_three.reshape(flat), w_hidden_in)
-    activated, slope = gelu_and_slope(hidden_pre)
-    activated = activated.astype(BF)
-    output = (latter + mm(activated, w_hidden_out).reshape(stream.shape)).astype(BF)
-    cot = cotangent.reshape(flat)
-    grad_hidden_out = mm(activated, cot, TN).astype(BF)
-    grad_pre = (mm(cot, w_hidden_out, NT) * slope).astype(BF)
-    grad_hidden_in = mm(normed_three.reshape(flat), grad_pre, TN).astype(BF)
-    grad_normed_three = mm(grad_pre, w_hidden_in, NT).reshape(stream.shape)
-    grad_latter, gain_three = rms_back(latter, gains[2], grad_normed_three)
-    grad_latter = grad_latter + cotangent.astype(F32)
-    grad_cross_part = grad_latter.astype(BF)
-    grad_cross_out = mm(cross_att.reshape(flat), grad_cross_part.reshape(flat), TN).astype(BF)
-    grad_catt = mm(grad_cross_part.reshape(flat), w_cross_out, NT).astype(BF)
-    grad_catt = grad_catt.reshape(count, rows, width)
-    fold = hidden_output_weight.shape[0] // shard
-    folded = grad_hidden_out.reshape(-1, fold, shard, width)
-    folded = [folded[:, k].reshape(-1, width) for k in range(fold)]
-    grad_second = jnp.concatenate([grad_cross_out, grad_hidden_in] + folded, axis=1)
+    output, grad_latter, grad_catt, gain_three, grad_second = feed_forward(
+        middle.reshape(flat), cross_att.reshape(flat), cotangent.reshape(flat), gains[2:3], second
+    )
+    output, grad_latter = output.reshape(stream.shape), grad_latter.reshape(stream.shape)
+    grad_catt, gain_three = grad_catt.reshape(stream.shape), gain_three[0]
     sum_second = lax.psum_scatter(grad_second, ALL, scatter_dimension=0, tiled=True)
 
     own_sent = (grad_catt, row_stats(grad_catt, cross_sum, cross_lse))
@@ -741,7 +836,7 @@
             sent = [x[one] for x in same]
             dq_same, dkv = cross_bwd(far_ids[step - 1][0][one], same_q, kv, *sent, dkv)
             joint = (dq_same.astype(F32) + core_swap(dq_crossed).astype(F32)).astype(BF)
-            latest = dq_same
+            latest = joint
             back.append(chip_shift(joint, chips - step))
         dq_parts.append(jnp.concatenate(back, axis=0))
     dkv_flat = after(dkv, joint).reshape(group * keys, 2 * width)
@@ -811,6 +906,8 @@
     )
     summed = [x.astype(F32) for x in summed]
     small_sum = summed[0][:, 2 * width :].T
+    sum_in = sum_second[:, width : width + ff].reshape(shard, fold, n_dev, shard)
+    sum_in = sum_in.swapaxes(1, 2).reshape(shard, ff)
     return (
         output,
         input_grad,
@@ -820,9 +917,9 @@
         summed[0][:, width : 2 * width],
         jnp.concatenate([x[:, width : 2 * width] for x in summed[1:]], axis=1),
         sum_second[:, :width].astype(F32),
-        sum_second[:, width : width + ff].astype(F32),
+        sum_in.astype(F32),
         jnp.concatenate(
-            [sum_second[:, width * k : width * (k + 1)] for k in range(1 + ff // width, 1 + ff // width + fold)]
+            [sum_second[:, width * k : width * (k + 1)] for k in range(1 + fold, 1 + 2 * fold)]
         ).astype(F32),
         small_sum[:3],
         small_sum[3 : 3 + n_tasks],

time: 704 us -> 645 us (0.916)
  matrix products: 153 us -> 76.1 us
  Pallas kernels: 321 us -> 366 us
  waiting for transfers between devices: 63.5 us -> 42.5 us
    dot_general x20 -> x11, matrix products: 153 us -> 76.1 us  [mm(): return lax.dot_general(a, b, dims, preferred_element_type=F32)]
    pallas_call x0 -> x1, Pallas kernels: none -> 46 us  [feed_forward(): pl.pallas_call(feed_forward_body, grid=(steps,), in_specs=[whole(tokens,...]
    ppermute x10, waiting for transfers between devices: 33 us -> 19.1 us  [chip_shift(): return jax.tree.map(lambda a: lax.ppermute(a, 'psg', perm), x)]
    unnamed x228 -> x212, local copies, waits for them, and re-layouts: 26.9 us -> 22.7 us
  transfers between devices with their start and end apart: 50 -> 49, of which waited for: 12 -> 10; matrix products, arithmetic and copies ran while one was open for 22% -> 16% of each run, Pallas kernels for 42% -> 47%
where the time goes in v3:
time: 645 us; the launch traced here: 636 us
  Pallas kernels  366 us (57%)
  matrix products  76.1 us (12%)
  local copies, waits for them, and re-layouts  62.3 us (10%)
  waiting for transfers between devices  42.5 us (7%)
  other arithmetic  38.9 us (6%)
  starting transfers between devices  34.2 us (5%)
  between operations  15.5 us (2%)
    pallas_call x6, Pallas kernels, cross_bwd(): pl.pallas_call(functools.partial(cross_bwd_body, chunk=min(rows, 256)), g...  122 us
    dot_general x11, matrix products, mm(): return lax.dot_general(a, b, dims, preferred_element_type=F32)  76.1 us
    pallas_call x6, Pallas kernels, cross_fwd(): pl.pallas_call(functools.partial(cross_fwd_body, npass=npass), grid_spec=...  69.6 us
    pallas_call x1, Pallas kernels, gather_rows(): pl.pallas_call(functools.partial(gather_body, columns=columns, core=core,...  56.2 us
    pallas_call x1, Pallas kernels, feed_forward(): pl.pallas_call(feed_forward_body, grid=(steps,), in_specs=[whole(tokens,...  46 us
    pallas_call x1, Pallas kernels, self_bwd(): pl.pallas_call(functools.partial(self_bwd_body, chunk=min(rows, 256)), gr...  24.4 us
    unnamed x212, local copies, waits for them, and re-layouts  22.7 us
    pallas_call x1, Pallas kernels, keyval(): pl.pallas_call(keyval_body, grid=(n // block,), in_specs=[pl.BlockSpec((b...  19.6 us
  transfers between devices with their start and end apart: 49, of which 10 were waited for; matrix products, arithmetic and copies ran while one was open for 16% of the time, Pallas kernels for 47%

profile of v3, /device:TPU:0, one launch (start us, length us, event | category | flops | bytes accessed | tf_op | source)
XLA Modules:
  0.0 635.7 jit_solution(80338796063134355)
XLA Ops:
  11.8 56.2 %shard_map.264 = (bf16[2,2,2,2,2,24,2304]{6,5,4,3,2,1,0:T(8,128)(2,1)}, bf16[2,2,2,2,2,24,768]{6,5,4,3,2,1,0:T(8,128)(2,1)}, bf16[2,2,2,2,2,24,896]{6,5,4,3,2,1,0:T(8,128)(2,1)}) custom-call(bf16[24,768]{1,0:T(8,128)(2,1)} %get-tuple-element.364.refs_0_, bf16[24,768]{1,0:T(8,128)(2,1)} %get-tuple-element.365.refs_1_, ...), custom_call_target="tpu_custom_call" | custom-call | tf_op jit(solution)/shard_map/pallas_call | solution.py:622
  73.8 5.4 multiply_convert_fusion
  79.2 13.7 %shard_map.265 = (bf16[2,512,768]{2,1,0:T(8,128)(2,1)}, f32[2,6,2,512]{3,2,1,0:T(2,128)}) custom-call(s32[2]{0:T(128)} %length_ref.3, bf16[2,512,2304]{2,1,0:T(8,128)(2,1)} %bitcast.236, bf16[2,512,2304]{2,1,0:T(8,128)(2,1)} %bitcast.237, bf16[2,512,2304]{2,1,0:T(8,128)(2,1)} %bitcast.238), custom_call_target="tpu_custom_call" | custom-call | flops 6442450944 | bytes 6291456 | tf_op jit(solution)/shard_map/pallas_call | solution.py:226
  118.0 19.6 %shard_map.266 = bf16[6144,1536]{1,0:T(8,128)(2,1)} custom-call(bf16[6144,768]{1,0:T(8,128)(2,1)} %bitcast.227, bf16[768,1536]{1,0:T(8,128)(2,1)} %all-gather.3.cloned.1.call-done.w_ref), custom_call_target="tpu_custom_call" | custom-call | flops 14495514624 | bytes 28311552 | tf_op jit(solution)/shard_map/pallas_call | solution.py:403
  137.6 15.7 %shard_map.267 = (bf16[2,512,768]{2,1,0:T(8,128)(2,1)}, f32[2,6,2,512]{3,2,1,0:T(2,128)}, f32[2,6,2,2,512]{4,3,2,1,0:T(2,128)}) custom-call(s32[2]{0:T(128)} %iota_add_fusion.idx, bf16[2,512,768]{2,1,0:T(8,128)(2,1)} %collective-permute-done.2.q_ref, bf16[8,768,1536]{2,1,0:T(8,128)(2,1)} %bitcast.173, bf16[8,768,1536]{2,1,0:T(8,128)(2,1)} %bitcast.174), custom_call_target="tpu_custom_call" | custom-call | flops 9663676416 | bytes 7864320 | tf_op jit(solution)/shard_map/pallas_call | solution.py:100
  154.6 9.4 %shard_map.268 = (bf16[1,512,768]{2,1,0:T(8,128)(2,1)}, f32[1,6,2,512]{3,2,1,0:T(2,128)}, f32[1,6,2,2,512]{4,3,2,1,0:T(2,128)}) custom-call(s32[1]{0:T(128)} %get-tuple-element.372.idx, bf16[1,512,768]{2,1,0:T(8,128)(2,1)} %collective-permute-done.1.q_ref, bf16[8,768,1536]{2,1,0:T(8,128)(2,1)} %bitcast.175, bf16[8,768,1536]{2,1,0:T(8,128)(2,1)} %bitcast.176), custom_call_target="tpu_custom_call" | custom-call | flops 4831838208 | bytes 3932160 | tf_op jit(solution)/shard_map/pallas_call | solution.py:100
  164.9 9.9 %shard_map.269 = (bf16[1,512,768]{2,1,0:T(8,128)(2,1)}, f32[1,6,2,512]{3,2,1,0:T(2,128)}, f32[1,6,2,2,512]{4,3,2,1,0:T(2,128)}) custom-call(s32[1]{0:T(128)} %get-tuple-element.371.idx, bf16[1,512,768]{2,1,0:T(8,128)(2,1)} %copy-done.13, bf16[8,768,1536]{2,1,0:T(8,128)(2,1)} %bitcast.177, bf16[8,768,1536]{2,1,0:T(8,128)(2,1)} %bitcast.178), custom_call_target="tpu_custom_call" | custom-call | flops 4831838208 | bytes 3932160 | tf_op jit(solution)/shard_map/pallas_call | solution.py:100
  177.8 9.2 %shard_map.270 = (bf16[1,512,768]{2,1,0:T(8,128)(2,1)}, f32[1,6,2,512]{3,2,1,0:T(2,128)}, f32[1,6,2,2,512]{4,3,2,1,0:T(2,128)}) custom-call(s32[1]{0:T(128)} %get-tuple-element.373.idx, bf16[1,512,768]{2,1,0:T(8,128)(2,1)} %collective-permute-done.q_ref, bf16[8,768,1536]{2,1,0:T(8,128)(2,1)} %bitcast.179, bf16[8,768,1536]{2,1,0:T(8,128)(2,1)} %bitcast.180), custom_call_target="tpu_custom_call" | custom-call | flops 4831838208 | bytes 3932160 | tf_op jit(solution)/shard_map/pallas_call | solution.py:100
  192.8 9.7 %shard_map.272 = (bf16[1,512,768]{2,1,0:T(8,128)(2,1)}, f32[1,6,2,512]{3,2,1,0:T(2,128)}, f32[1,6,2,2,512]{4,3,2,1,0:T(2,128)}) custom-call(s32[1]{0:T(128)} %get-tuple-element.370.idx, bf16[1,512,768]{2,1,0:T(8,128)(2,1)} %copy-done.12, bf16[8,768,1536]{2,1,0:T(8,128)(2,1)} %bitcast.181, bf16[8,768,1536]{2,1,0:T(8,128)(2,1)} %bitcast.182), custom_call_target="tpu_custom_call" | custom-call | flops 4831838208 | bytes 3932160 | tf_op jit(solution)/shard_map/pallas_call | solution.py:100
  213.8 15.8 %shard_map.274 = (bf16[2,512,768]{2,1,0:T(8,128)(2,1)}, f32[2,6,2,512]{3,2,1,0:T(2,128)}, f32[2,6,2,2,512]{4,3,2,1,0:T(2,128)}) custom-call(s32[2]{0:T(128)} %copy-done.90, bf16[2,512,768]{2,1,0:T(8,128)(2,1)} %bitcast.203, bf16[8,768,1536]{2,1,0:T(8,128)(2,1)} %bitcast.184, bf16[8,768,1536]{2,1,0:T(8,128)(2,1)} %bitcast.183), custom_call_target="tpu_custom_call" | custom-call | flops 9663676416 | bytes 7864320 | tf_op jit(solution)/shard_map/pallas_call | solution.py:100
  229.6 13.3 %collective-permute-done.14 = f32[1,6,2,512]{3,2,1,0:T(2,128)S(1)} collective-permute-done((f32[1,6,2,512]{3,2,1,0:T(2,128)}, f32[1,6,2,512]{3,2,1,0:T(2,128)S(1)}, u32[]{:S(2)}, u32[]{:S(2)}) %collective-permute-start.14) | collective-permute-done | bytes 24608 | tf_op jit(solution)/shard_map/ppermute | solution.py:722
  246.1 4.9 shard_map.275
  251.1 46.0 %shard_map.276 = (bf16[1024,768]{1,0:T(8,128)(2,1)}, f32[1024,768]{1,0:T(8,128)}, bf16[1024,768]{1,0:T(8,128)(2,1)}, f32[1,768]{1,0:T(1,128)}, bf16[768,6912]{1,0:T(8,128)(2,1)}) custom-call(f32[1024,768]{1,0:T(8,128)} %bitcast.199, bf16[1024,768]{1,0:T(8,128)(2,1)} %bitcast.232, bf16[1024,768]{1,0:T(8,128)(2,1)} %bitcast.231, ...), custom_call_target="tpu_custom_call" | custom-call | flops 32614907904 | bytes 32243712 | tf_op jit(solution)/shard_map/pallas_call | solution.py:492
  297.1 3.7 shard_map.277.stat_ref
  303.0 29.1 %shard_map.278 = (bf16[2,512,768]{2,1,0:T(8,128)(2,1)}, bf16[8,768,1536]{2,1,0:T(8,128)(2,1)}) custom-call(s32[2]{0:T(128)} %copy-done.90, bf16[2,512,768]{2,1,0:T(8,128)(2,1)} %bitcast.204, bf16[8,768,1536]{2,1,0:T(8,128)(2,1)} %bitcast.185, bf16[8,768,1536]{2,1,0:T(8,128)(2,1)} %bitcast.186, bf16[2,512,768]{2,1,0:T(8,128)(2,1)} %bitcast.218, ...), custom_call_target="tpu_custom_call" | custom-call | flops 24159191040 | bytes 14155776 | tf_op jit(solution)/shard_map/pallas_call | solution.py:170
  334.4 5.7 collective-permute-done.18
  341.9 28.7 %shard_map.279 = (bf16[2,512,768]{2,1,0:T(8,128)(2,1)}, bf16[8,768,1536]{2,1,0:T(8,128)(2,1)}) custom-call(s32[2]{0:T(128)} %iota_add_fusion.idx, bf16[2,512,768]{2,1,0:T(8,128)(2,1)} %collective-permute-done.2.q_ref, bf16[8,768,1536]{2,1,0:T(8,128)(2,1)} %bitcast.187, bf16[8,768,1536]{2,1,0:T(8,128)(2,1)} %bitcast.188, ...), custom_call_target="tpu_custom_call", output_to_operand_aliasing={{1}: (6, {})} | custom-call | flops 24159191040 | bytes 14155776 | tf_op jit(solution)/shard_map/pallas_call | solution.py:170
  373.3 16.0 %shard_map.280 = (bf16[1,512,768]{2,1,0:T(8,128)(2,1)}, bf16[8,768,1536]{2,1,0:T(8,128)(2,1)}) custom-call(s32[1]{0:T(128)} %get-tuple-element.371.idx, bf16[1,512,768]{2,1,0:T(8,128)(2,1)} %copy-done.13, bf16[8,768,1536]{2,1,0:T(8,128)(2,1)} %bitcast.189, bf16[8,768,1536]{2,1,0:T(8,128)(2,1)} %bitcast.190, ...), custom_call_target="tpu_custom_call", output_to_operand_aliasing={{1}: (6, {})} | custom-call | flops 12079595520 | bytes 7077888 | tf_op jit(solution)/shard_map/pallas_call | solution.py:170
  389.5 16.2 %shard_map.281 = (bf16[1,512,768]{2,1,0:T(8,128)(2,1)}, bf16[8,768,1536]{2,1,0:T(8,128)(2,1)}) custom-call(s32[1]{0:T(128)} %get-tuple-element.372.idx, bf16[1,512,768]{2,1,0:T(8,128)(2,1)} %collective-permute-done.1.q_ref, bf16[8,768,1536]{2,1,0:T(8,128)(2,1)} %bitcast.191, bf16[8,768,1536]{2,1,0:T(8,128)(2,1)} %bitcast.192, ...), custom_call_target="tpu_custom_call", output_to_operand_aliasing={{1}: (6, {})} | custom-call | flops 12079595520 | bytes 7077888 | tf_op jit(solution)/shard_map/pallas_call | solution.py:170
  409.4 16.1 %shard_map.282 = (bf16[1,512,768]{2,1,0:T(8,128)(2,1)}, bf16[8,768,1536]{2,1,0:T(8,128)(2,1)}) custom-call(s32[1]{0:T(128)} %get-tuple-element.370.idx, bf16[1,512,768]{2,1,0:T(8,128)(2,1)} %copy-done.12, bf16[8,768,1536]{2,1,0:T(8,128)(2,1)} %bitcast.193, bf16[8,768,1536]{2,1,0:T(8,128)(2,1)} %bitcast.194, ...), custom_call_target="tpu_custom_call", output_to_operand_aliasing={{1}: (6, {})} | custom-call | flops 12079595520 | bytes 7077888 | tf_op jit(solution)/shard_map/pallas_call | solution.py:170
  425.7 16.1 %shard_map.283 = (bf16[1,512,768]{2,1,0:T(8,128)(2,1)}, bf16[8,768,1536]{2,1,0:T(8,128)(2,1)}) custom-call(s32[1]{0:T(128)} %get-tuple-element.373.idx, bf16[1,512,768]{2,1,0:T(8,128)(2,1)} %collective-permute-done.q_ref, bf16[8,768,1536]{2,1,0:T(8,128)(2,1)} %bitcast.195, bf16[8,768,1536]{2,1,0:T(8,128)(2,1)} %bitcast.196, ...), custom_call_target="tpu_custom_call", output_to_operand_aliasing={{1}: (6, {})} | custom-call | flops 12079595520 | bytes 7077888 | tf_op jit(solution)/shard_map/pallas_call | solution.py:170
  444.4 21.2 %fusion.2 = bf16[768,1536]{1,0:T(8,128)(2,1)S(1)} fusion(bf16[6144,1536]{1,0:T(8,128)(2,1)} %bitcast.197, bf16[6144,768]{1,0:T(8,128)(2,1)} %bitcast.228), kind=kOutput, calls=%fused_computation.19 | convolution fusion | flops 14496694272 | bytes 30670848 | tf_op jit(solution)/shard_map/dot_general | solution.py:29
  469.6 4.6 multiply_reduce_fusion
  479.7 24.4 %shard_map.284 = bf16[2,512,2304]{2,1,0:T(8,128)(2,1)} custom-call(s32[2]{0:T(128)} %length_ref.3, bf16[2,512,2304]{2,1,0:T(8,128)(2,1)} %bitcast.239, bf16[2,512,2304]{2,1,0:T(8,128)(2,1)} %bitcast.240, bf16[2,512,2304]{2,1,0:T(8,128)(2,1)} %bitcast.241, bf16[2,512,768]{2,1,0:T(8,128)(2,1)} %bitcast.243, f32[2,6,2,512]{3,2,1,0:T(2,128)} %get-tuple-element.179.lse_ref), custom_call_target="tpu_custom_call" | custom-call | flops 16106127360 | bytes 12582912 | tf_op jit(solution)/shard_map/pallas_call | solution.py:300
  504.1 6.8 %bitcast_convert_fusion = bf16[768,2304]{1,0:T(8,128)(2,1)S(1)} fusion(bf16[2,512,768]{2,1,0:T(8,128)(2,1)S(1)} %copy-done.30, bf16[2,512,2304]{2,1,0:T(8,128)(2,1)} %shard_map.284), kind=kOutput, calls=%fused_computation.2 | convolution fusion | flops 3625648128 | bytes 9830400 | tf_op jit(solution)/shard_map/dot_general | solution.py:29
  514.9 4.3 multiply_reduce_fusion.1
  529.4 3.0 bitcast_convert_fusion.2
  543.6 3.0 collective-permute-done.33
  555.3 21.2 %fusion.56 = f32[6144,768]{1,0:T(8,128)} fusion(bf16[6144,1536]{1,0:T(8,128)(2,1)} %bitcast.198, bf16[768,1536]{1,0:T(8,128)(2,1)S(1)} %copy-done.95), kind=kOutput, calls=%fused_computation.187 | convolution fusion | flops 14495514624 | bytes 40108032 | tf_op jit(solution)/shard_map/dot_general | solution.py:29
  592.2 3.9 collective-permute-done.38
  596.2 3.6 collective-permute-done.39
  616.6 4.6 collective-permute-done.43
  (452 shorter events, 159.0 us)
Async XLA Ops:
  7.2 110.8 %all-gather.3.cloned.1.call-start = ((), (), s32[]{:S(2)}) async-start(), calls=%async_computation.1 | async-start | bytes 2433024 | tf_op jit(solution)/shard_map/all_gather | solution.py:737
  7.9 243.1 %all-gather.5.cloned.1.call-start = ((), (), s32[]{:S(2)}) async-start(), calls=%async_computation.2 | async-start | bytes 10948608 | tf_op jit(solution)/shard_map/all_gather | solution.py:771
  111.2 357.3 %reduce-scatter.2.cloned.1.call-start = ((), (), s32[]{:S(2)}) async-start(), calls=%async_computation.3 | async-start | bytes 10948608 | tf_op jit(solution)/shard_map/reduce_scatter | solution.py:816
  111.4 26.2 %collective-permute-start.2 = (bf16[2,512,768]{2,1,0:T(8,128)(2,1)}, bf16[2,512,768]{2,1,0:T(8,128)(2,1)}, u32[]{:S(2)}, u32[]{:S(2)}) collective-permute-start(bf16[2,512,768]{2,1,0:T(8,128)(2,1)} %bitcast.202), channel_id=1, source_target_pairs={{0,1},{1,0},{2,3},{3,2},{4,5},{5,4},{6,7},{7,6},{8,9},{9,8},{10,11... | collective-permute-start | bytes 4718600 | tf_op jit(solution)/shard_map/ppermute | solution.py:718
  114.5 38.8 %collective-permute-start.1 = (bf16[1,512,768]{2,1,0:T(8,128)(2,1)}, bf16[1,512,768]{2,1,0:T(8,128)(2,1)}, u32[]{:S(2)}, u32[]{:S(2)}) collective-permute-start(bf16[1,512,768]{2,1,0:T(8,128)(2,1)} %get-tuple-element.329), channel_id=1, source_target_pairs={{0,2},{1,3},{2,0},{3,1},{4,6},{5,7},{6,4},{7,5},{8,10},{9,11},{10,... | collective-permute-start | bytes 2359304 | tf_op jit(solution)/shard_map/ppermute | solution.py:722
  116.0 59.3 %collective-permute-start = (bf16[1,512,768]{2,1,0:T(8,128)(2,1)}, bf16[1,512,768]{2,1,0:T(8,128)(2,1)}, u32[]{:S(2)}, u32[]{:S(2)}) collective-permute-start(bf16[1,512,768]{2,1,0:T(8,128)(2,1)} %get-tuple-element.330), channel_id=1, source_target_pairs={{0,2},{1,3},{2,0},{3,1},{4,6},{5,7},{6,4},{7,5},{8,10},{9,11},{10,... | collective-permute-start | bytes 2359304 | tf_op jit(solution)/shard_map/ppermute | solution.py:722
  175.3 16.6 %collective-permute-start.4 = (bf16[1,512,768]{2,1,0:T(8,128)(2,1)}, bf16[1,512,768]{2,1,0:T(8,128)(2,1)S(1)}, u32[]{:S(2)}, u32[]{:S(2)}) collective-permute-start(bf16[1,512,768]{2,1,0:T(8,128)(2,1)} %collective-permute-done.q_ref), channel_id=1, source_target_pairs={{0,1},{1,0},{2,3},{3,2},{4,5},{5,4},{6,7},{7,6},{8,9},{9,8},{10,11... | collective-permute-start | bytes 2359304 | tf_op jit(solution)/shard_map/ppermute | solution.py:718
  175.6 27.5 %collective-permute-start.29 = (f32[8,2]{1,0:T(8,128)S(1)}, f32[8,2]{1,0:T(8,128)S(1)}, u32[]{:S(2)}, u32[]{:S(2)}) collective-permute-start(f32[8,2]{1,0:T(8,128)S(1)} %fusion.25), channel_id=1, source_target_pairs={{0,1},{1,2},{2,3},{3,0},{4,5},{5,6},{6,7},{7,4},{8,9},{9,10},{10,1... | collective-permute-start | bytes 200 | tf_op jit(solution)/shard_map/ppermute | solution.py:742
  176.0 27.2 %collective-permute-start.30 = (f32[8,2]{1,0:T(8,128)S(1)}, f32[8,2]{1,0:T(8,128)S(1)}, u32[]{:S(2)}, u32[]{:S(2)}) collective-permute-start(f32[8,2]{1,0:T(8,128)S(1)} %fusion.25), channel_id=1, source_target_pairs={{0,2},{1,3},{2,0},{3,1},{4,6},{5,7},{6,4},{7,5},{8,10},{9,11},{10,... | collective-permute-start | bytes 200 | tf_op jit(solution)/shard_map/ppermute | solution.py:742
  187.0 16.3 %collective-permute-start.31 = (f32[8,2]{1,0:T(8,128)S(1)}, f32[8,2]{1,0:T(8,128)S(1)}, u32[]{:S(2)}, u32[]{:S(2)}) collective-permute-start(f32[8,2]{1,0:T(8,128)S(1)} %fusion.25), channel_id=1, source_target_pairs={{0,3},{1,0},{2,1},{3,2},{4,7},{5,4},{6,5},{7,6},{8,11},{9,8},{10,9... | collective-permute-start | bytes 200 | tf_op jit(solution)/shard_map/ppermute | solution.py:742
  203.4 41.5 %collective-permute-start.9 = (bf16[2,512,768]{2,1,0:T(8,128)(2,1)}, bf16[2,512,768]{2,1,0:T(8,128)(2,1)S(1)}, u32[]{:S(2)}, u32[]{:S(2)}) collective-permute-start(bf16[2,512,768]{2,1,0:T(8,128)(2,1)} %get-tuple-element.122), channel_id=1, source_target_pairs={{0,1},{1,0},{2,3},{3,2},{4,5},{5,4},{6,7},{7,6},{8,9},{9,8},{10,11... | collective-permute-start | bytes 4718600 | tf_op jit(solution)/shard_map/ppermute | solution.py:718
  204.9 38.7 %collective-permute-start.10 = (bf16[1,512,768]{2,1,0:T(8,128)(2,1)}, bf16[1,512,768]{2,1,0:T(8,128)(2,1)S(1)}, u32[]{:S(2)}, u32[]{:S(2)}) collective-permute-start(bf16[1,512,768]{2,1,0:T(8,128)(2,1)} %get-tuple-element.137), channel_id=1, source_target_pairs={{0,2},{1,3},{2,0},{3,1},{4,6},{5,7},{6,4},{7,5},{8,10},{9,11},{10,... | collective-permute-start | bytes 2359304 | tf_op jit(solution)/shard_map/ppermute | solution.py:722
  205.9 23.7 %collective-permute-start.13 = (f32[1,6,2,512]{3,2,1,0:T(2,128)S(1)}, f32[1,6,2,512]{3,2,1,0:T(2,128)S(1)}, u32[]{:S(2)}, u32[]{:S(2)}) collective-permute-start(f32[1,6,2,512]{3,2,1,0:T(2,128)S(1)} %copy-done.99), channel_id=1, source_target_pairs={{0,2},{1,3},{2,0},{3,1},{4,6},{5,7},{6,4},{7,5},{8,10},{9,11},{10,... | collective-permute-start | bytes 73736 | tf_op jit(solution)/shard_map/ppermute | solution.py:722
  211.7 31.9 %collective-permute-start.11 = (bf16[1,512,768]{2,1,0:T(8,128)(2,1)}, bf16[1,512,768]{2,1,0:T(8,128)(2,1)S(1)}, u32[]{:S(2)}, u32[]{:S(2)}) collective-permute-start(bf16[1,512,768]{2,1,0:T(8,128)(2,1)} %get-tuple-element.141), channel_id=1, source_target_pairs={{0,2},{1,3},{2,0},{3,1},{4,6},{5,7},{6,4},{7,5},{8,10},{9,11},{10,... | collective-permute-start | bytes 2359304 | tf_op jit(solution)/shard_map/ppermute | solution.py:722
  212.7 30.3 %collective-permute-start.14 = (f32[1,6,2,512]{3,2,1,0:T(2,128)}, f32[1,6,2,512]{3,2,1,0:T(2,128)S(1)}, u32[]{:S(2)}, u32[]{:S(2)}) collective-permute-start(f32[1,6,2,512]{3,2,1,0:T(2,128)} %get-tuple-element.146), channel_id=1, source_target_pairs={{0,2},{1,3},{2,0},{3,1},{4,6},{5,7},{6,4},{7,5},{8,10},{9,11},{10,... | collective-permute-start | bytes 73736 | tf_op jit(solution)/shard_map/ppermute | solution.py:722
  229.6 15.4 %collective-permute-start.12 = (f32[2,6,2,512]{3,2,1,0:T(2,128)S(1)}, f32[2,6,2,512]{3,2,1,0:T(2,128)S(1)}, u32[]{:S(2)}, u32[]{:S(2)}) collective-permute-start(f32[2,6,2,512]{3,2,1,0:T(2,128)S(1)} %copy-done.59), channel_id=1, source_target_pairs={{0,1},{1,0},{2,3},{3,2},{4,5},{5,4},{6,7},{7,6},{8,9},{9,8},{10,11... | collective-permute-start | bytes 147464 | tf_op jit(solution)/shard_map/ppermute | solution.py:718
  300.9 32.7 %collective-permute-start.16 = (f32[2,6,4,512]{3,2,1,0:T(4,128)}, f32[2,6,4,512]{3,2,1,0:T(4,128)S(1)}, u32[]{:S(2)}, u32[]{:S(2)}) collective-permute-start(f32[2,6,4,512]{3,2,1,0:T(4,128)} %shard_map.277.stat_ref), channel_id=1, source_target_pairs={{0,1},{1,0},{2,3},{3,2},{4,5},{5,4},{6,7},{7,6},{8,9},{9,8},{10,11... | collective-permute-start | bytes 294920 | tf_op jit(solution)/shard_map/ppermute | solution.py:718
  300.9 33.4 %collective-permute-start.19 = (f32[2,6,4,512]{3,2,1,0:T(4,128)}, f32[2,6,4,512]{3,2,1,0:T(4,128)S(1)}, u32[]{:S(2)}, u32[]{:S(2)}) collective-permute-start(f32[2,6,4,512]{3,2,1,0:T(4,128)} %shard_map.277.stat_ref), channel_id=1, source_target_pairs={{0,2},{1,3},{2,0},{3,1},{4,6},{5,7},{6,4},{7,5},{8,10},{9,11},{10,... | collective-permute-start | bytes 294920 | tf_op jit(solution)/shard_map/ppermute | solution.py:722
  301.9 38.1 %collective-permute-start.18 = (bf16[2,512,768]{2,1,0:T(8,128)(2,1)S(1)}, bf16[2,512,768]{2,1,0:T(8,128)(2,1)S(1)}, u32[]{:S(2)}, u32[]{:S(2)}) collective-permute-start(bf16[2,512,768]{2,1,0:T(8,128)(2,1)S(1)} %bitcast.219), channel_id=1, source_target_pairs={{0,2},{1,3},{2,0},{3,1},{4,6},{5,7},{6,4},{7,5},{8,10},{9,11},{10,... | collective-permute-start | bytes 4718600 | tf_op jit(solution)/shard_map/ppermute | solution.py:722
  303.0 37.0 %collective-permute-start.15 = (bf16[2,512,768]{2,1,0:T(8,128)(2,1)S(1)}, bf16[2,512,768]{2,1,0:T(8,128)(2,1)S(1)}, u32[]{:S(2)}, u32[]{:S(2)}) collective-permute-start(bf16[2,512,768]{2,1,0:T(8,128)(2,1)S(1)} %bitcast.220), channel_id=1, source_target_pairs={{0,1},{1,0},{2,3},{3,2},{4,5},{5,4},{6,7},{7,6},{8,9},{9,8},{10,11... | collective-permute-start | bytes 4718600 | tf_op jit(solution)/shard_map/ppermute | solution.py:718
  340.1 31.6 %collective-permute-start.21 = (f32[2,6,4,512]{3,2,1,0:T(4,128)S(1)}, f32[2,6,4,512]{3,2,1,0:T(4,128)S(1)}, u32[]{:S(2)}, u32[]{:S(2)}) collective-permute-start(f32[2,6,4,512]{3,2,1,0:T(4,128)S(1)} %collective-permute-done.19), channel_id=1, source_target_pairs={{0,1},{1,0},{2,3},{3,2},{4,5},{5,4},{6,7},{7,6},{8,9},{9,8},{10,11... | collective-permute-start | bytes 294920 | tf_op jit(solution)/shard_map/ppermute | solution.py:718
  340.1 31.6 %collective-permute-start.20 = (bf16[2,512,768]{2,1,0:T(8,128)(2,1)S(1)}, bf16[2,512,768]{2,1,0:T(8,128)(2,1)S(1)}, u32[]{:S(2)}, u32[]{:S(2)}) collective-permute-start(bf16[2,512,768]{2,1,0:T(8,128)(2,1)S(1)} %collective-permute-done.18), channel_id=1, source_target_pairs={{0,1},{1,0},{2,3},{3,2},{4,5},{5,4},{6,7},{7,6},{8,9},{9,8},{10,11... | collective-permute-start | bytes 4718600 | tf_op jit(solution)/shard_map/ppermute | solution.py:718
  371.2 97.3 %collective-permute-start.17 = (bf16[2,512,768]{2,1,0:T(8,128)(2,1)}, bf16[2,512,768]{2,1,0:T(8,128)(2,1)}, u32[]{:S(2)}, u32[]{:S(2)}) collective-permute-start(bf16[2,512,768]{2,1,0:T(8,128)(2,1)} %get-tuple-element.160), channel_id=1, source_target_pairs={{0,1},{1,0},{2,3},{3,2},{4,5},{5,4},{6,7},{7,6},{8,9},{9,8},{10,11... | collective-permute-start | bytes 4718600 | tf_op jit(solution)/shard_map/ppermute | solution.py:718
  389.3 16.4 %collective-permute-start.22 = (bf16[1,512,768]{2,1,0:T(8,128)(2,1)}, bf16[1,512,768]{2,1,0:T(8,128)(2,1)S(1)}, u32[]{:S(2)}, u32[]{:S(2)}) collective-permute-start(bf16[1,512,768]{2,1,0:T(8,128)(2,1)} %get-tuple-element.168), channel_id=1, source_target_pairs={{0,1},{1,0},{2,3},{3,2},{4,5},{5,4},{6,7},{7,6},{8,9},{9,8},{10,11... | collective-permute-start | bytes 2359304 | tf_op jit(solution)/shard_map/ppermute | solution.py:718
  407.0 60.2 %collective-permute-start.23 = (bf16[1,512,768]{2,1,0:T(8,128)(2,1)S(1)}, bf16[1,512,768]{2,1,0:T(8,128)(2,1)S(1)}, u32[]{:S(2)}, u32[]{:S(2)}) collective-permute-start(bf16[1,512,768]{2,1,0:T(8,128)(2,1)S(1)} %add_convert_fusion.5), channel_id=1, source_target_pairs={{0,2},{1,3},{2,0},{3,1},{4,6},{5,7},{6,4},{7,5},{8,10},{9,11},{10,... | collective-permute-start | bytes 2359304 | tf_op jit(solution)/shard_map/ppermute | solution.py:722
  425.5 16.3 %collective-permute-start.24 = (bf16[1,512,768]{2,1,0:T(8,128)(2,1)}, bf16[1,512,768]{2,1,0:T(8,128)(2,1)S(1)}, u32[]{:S(2)}, u32[]{:S(2)}) collective-permute-start(bf16[1,512,768]{2,1,0:T(8,128)(2,1)} %get-tuple-element.174), channel_id=1, source_target_pairs={{0,1},{1,0},{2,3},{3,2},{4,5},{5,4},{6,7},{7,6},{8,9},{9,8},{10,11... | collective-permute-start | bytes 2359304 | tf_op jit(solution)/shard_map/ppermute | solution.py:718
  443.1 24.1 %collective-permute-start.25 = (bf16[1,512,768]{2,1,0:T(8,128)(2,1)S(1)}, bf16[1,512,768]{2,1,0:T(8,128)(2,1)S(1)}, u32[]{:S(2)}, u32[]{:S(2)}) collective-permute-start(bf16[1,512,768]{2,1,0:T(8,128)(2,1)S(1)} %add_convert_fusion.4), channel_id=1, source_target_pairs={{0,2},{1,3},{2,0},{3,1},{4,6},{5,7},{6,4},{7,5},{8,10},{9,11},{10,... | collective-permute-start | bytes 2359304 | tf_op jit(solution)/shard_map/ppermute | solution.py:722
  553.7 22.8 %collective-permute-start.35 = (bf16[2,2,2,24,1920]{4,3,2,1,0:T(8,128)(2,1)S(1)}, bf16[2,2,2,24,1920]{4,3,2,1,0:T(8,128)(2,1)S(1)}, u32[]{:S(2)}, u32[]{:S(2)}) collective-permute-start(bf16[2,2,2,24,1920]{4,3,2,1,0:T(8,128)(2,1)S(1)} %dynamic-slice_bitcast_fusion.1), channel_id=1, source_target_pairs={{0,2},{1,3},{2,0},{3,1},{4,6},{5,7},{6,4},{7,5},{8,10},{9,11},{10,... | collective-permute-start | bytes 2211848 | tf_op jit(solution)/shard_map/ppermute | solution.py:544
  554.6 21.9 %collective-permute-start.36 = (bf16[2,2,2,24,1920]{4,3,2,1,0:T(8,128)(2,1)S(1)}, bf16[2,2,2,24,1920]{4,3,2,1,0:T(8,128)(2,1)S(1)}, u32[]{:S(2)}, u32[]{:S(2)}) collective-permute-start(bf16[2,2,2,24,1920]{4,3,2,1,0:T(8,128)(2,1)S(1)} %dynamic-slice_bitcast_fusion), channel_id=1, source_target_pairs={{0,8},{4,12},{8,0},{12,4},{16,24},{20,28},{24,16},{28,20},{1,9},{5... | collective-permute-start | bytes 2211848 | tf_op jit(solution)/shard_map/ppermute | solution.py:544
  554.6 21.9 %collective-permute-start.34 = (bf16[2,2,2,24,1664]{4,3,2,1,0:T(8,128)(2,1)S(1)}, bf16[2,2,2,24,1664]{4,3,2,1,0:T(8,128)(2,1)S(1)}, u32[]{:S(2)}, u32[]{:S(2)}) collective-permute-start(bf16[2,2,2,24,1664]{4,3,2,1,0:T(8,128)(2,1)S(1)} %dynamic-slice_bitcast_fusion.2), channel_id=1, source_target_pairs={{0,4},{4,0},{8,12},{12,8},{16,20},{20,16},{24,28},{28,24},{1,5},{5... | collective-permute-start | bytes 1916936 | tf_op jit(solution)/shard_map/ppermute | solution.py:544
  579.7 16.5 %collective-permute-start.38 = (bf16[2,2,24,1920]{3,2,1,0:T(8,128)(2,1)S(1)}, bf16[2,2,24,1920]{3,2,1,0:T(8,128)(2,1)}, u32[]{:S(2)}, u32[]{:S(2)}) collective-permute-start(bf16[2,2,24,1920]{3,2,1,0:T(8,128)(2,1)S(1)} %dynamic-slice_bitcast_fusion.16), channel_id=1, source_target_pairs={{0,8},{4,12},{8,0},{12,4},{16,24},{20,28},{24,16},{28,20},{1,9},{5... | collective-permute-start | bytes 1105928 | tf_op jit(solution)/shard_map/ppermute | solution.py:544
  581.7 18.1 %collective-permute-start.39 = (bf16[2,2,24,1920]{3,2,1,0:T(8,128)(2,1)}, bf16[2,2,24,1920]{3,2,1,0:T(8,128)(2,1)}, u32[]{:S(2)}, u32[]{:S(2)}) collective-permute-start(bf16[2,2,24,1920]{3,2,1,0:T(8,128)(2,1)} %dynamic-slice_bitcast_fusion.15), channel_id=1, source_target_pairs={{0,16},{4,20},{8,24},{12,28},{16,0},{20,4},{24,8},{28,12},{1,17},{... | collective-permute-start | bytes 1105928 | tf_op jit(solution)/shard_map/ppermute | solution.py:544
  (119 other events, 1067.0 us)
Sparse Core Ops, SparseCore 0:
  10.9 77.2 all-gather.2
  111.3 90.2 all-gather.4
  297.2 154.2 reduce-scatter.1

commit v4 on v3

--- a/solution.py
+++ b/solution.py
@@ -429,6 +429,7 @@
     catt_ref,
     gain_grad_ref,
     w_grad_ref,
+    w_down_grad_ref,
     latter,
     normed,
     hidden,
@@ -459,7 +460,7 @@
     def _():
         more = dot(hidden[...], w_down_ref[...])
         total[...] = jnp.where(step == 1, more, total[...] + more)
-        w_grad_ref[...] = dot(hidden[...], cot_ref[...], TN).astype(BF)
+        w_down_grad_ref[...] = dot(hidden[...], cot_ref[...], TN).astype(BF)
 
     @pl.when(step == last)
     def _():
@@ -476,9 +477,9 @@
         w_grad_ref[...] = dot(att_ref[...], hidden[...], TN).astype(BF)
 
 
-def feed_forward(middle, att, cot, gain, weights):
+def feed_forward(middle, att, cot, gain, weights, w_down):
     tokens, width = middle.shape
-    chunks = (weights.shape[1] // width - 1) // 2
+    chunks = w_down.shape[0] // width
     steps = 2 * chunks + 1
 
     def whole(rows, columns):
@@ -497,30 +498,30 @@
             whole(1, width),
             whole(*square),
             pl.BlockSpec(square, lambda s: (0, 1 + chunk_of(s))),
-            pl.BlockSpec(square, lambda s: (0, 1 + chunks + chunk_of(s))),
+            pl.BlockSpec(square, lambda s: (chunk_of(s), 0)),
         ],
         out_specs=[whole(tokens, width)] * 3
         + [
             whole(1, width),
-            pl.BlockSpec(
-                square, lambda s: (0, jnp.where(s == steps - 1, 0, 1 + s // 2 + chunks * (s % 2)))
-            ),
+            pl.BlockSpec(square, lambda s: (0, jnp.where(s == steps - 1, 0, 1 + s // 2))),
+            pl.BlockSpec(square, lambda s: (chunk_of(s), 0)),
         ],
         out_shape=[
             jax.ShapeDtypeStruct((tokens, width), BF),
             jax.ShapeDtypeStruct((tokens, width), F32),
             jax.ShapeDtypeStruct((tokens, width), BF),
             jax.ShapeDtypeStruct((1, width), F32),
-            jax.ShapeDtypeStruct(weights.shape, BF),
+            jax.ShapeDtypeStruct((width, width + w_down.shape[0]), BF),
+            jax.ShapeDtypeStruct(w_down.shape, BF),
         ],
         scratch_shapes=wide,
         compiler_params=params(),
         cost_estimate=pl.CostEstimate(
             flops=2 * tokens * width * width * (6 * chunks + 3),
-            bytes_accessed=tokens * width * 14 + 4 * width * weights.shape[1],
+            bytes_accessed=tokens * width * 14 + 8 * width * weights.shape[1],
             transcendentals=tokens * width * chunks,
         ),
-    )(middle, att, cot, gain, weights, weights, weights)
+    )(middle, att, cot, gain, weights, weights, w_down)
 
 
 def bits_below(n):
@@ -538,12 +539,6 @@
     return ("psg", 1), xs, ys, zs, order
 
 
-def swap_bit(x, hop):
-    axis, bit = hop
-    n = lax.axis_size(axis)
-    return lax.ppermute(x, axis, [(p, p ^ bit) for p in range(n)])
-
-
 def my_bit(hop):
     return (lax.axis_index(hop[0]) // hop[1]) % 2
 
@@ -558,10 +553,11 @@
     return {axis: me + bit * (1 - 2 * ((me // bit) % 2))}
 
 
-def gather_body(*refs, columns, core, orders, order):
-    n, n_out = len(columns), 1 + max(c[0] for c in columns)
-    ins, outs = refs[:n], refs[n : n + n_out]
-    local, send, recv = refs[n + n_out :]
+def gather_body(*refs, columns, packing, core, orders, order):
+    n, n_out, n_more = len(columns), 1 + max(c[0] for c in columns), len(packing)
+    ins, more = refs[:n], refs[n : n + n_more]
+    outs, packed = refs[n + n_more : n + n_more + n_out], refs[n + n_more + n_out]
+    local, packs, send, recv = refs[n + n_more + n_out + 1 :]
     place = tuple(my_bit(h) for h in order)
 
     def block(k, have, flip=None):
@@ -586,6 +582,12 @@
     own = [pltpu.make_async_copy(ins[k], block(k, ()), local.at[k]) for k in range(n)]
     for c in own:
         c.start()
+    beside, start = [], 0
+    for k, width in enumerate(packing):
+        to = packed.at[:, pl.ds(start, width)]
+        beside.append(pltpu.make_async_copy(more[k], to, packs.at[k]))
+        beside[k].start()
+        start += width
     barrier = pltpu.get_barrier_semaphore()
     for hop in order:
         pl.semaphore_signal(
@@ -612,55 +614,125 @@
             c.wait_send()
         for c in near[k]:
             c.wait()
-
-
-def gather_rows(stripes, columns, widths):
+    for c in beside:
+        c.wait()
+
+
+def gather_rows(stripes, columns, widths, beside):
     core, xs, ys, zs, order = exchanges()
     orders = [zs + xs + ys, zs + ys + xs, xs + zs + ys, ys + zs + xs, xs + ys + zs]
     orders = [orders[k % len(orders)] for k in range(len(stripes))]
     rows, n = stripes[0].shape[0], len(stripes)
+    packing = [x.shape[1] for x in beside]
     outs = pl.pallas_call(
-        functools.partial(gather_body, columns=columns, core=core, orders=orders, order=order),
-        in_specs=[pl.BlockSpec(memory_space=pl.ANY)] * n,
-        out_specs=[pl.BlockSpec(memory_space=pl.ANY)] * len(widths),
+        functools.partial(
+            gather_body, columns=columns, packing=packing, core=core, orders=orders, order=order
+        ),
+        in_specs=[pl.BlockSpec(memory_space=pl.ANY)] * (n + len(beside)),
+        out_specs=[pl.BlockSpec(memory_space=pl.ANY)] * (len(widths) + 1),
         out_shape=[
             jax.ShapeDtypeStruct((2,) * len(order) + (rows, w), stripes[0].dtype) for w in widths
-        ],
+        ]
+        + [jax.ShapeDtypeStruct((rows, sum(packing)), beside[0].dtype)],
         scratch_shapes=[
             pltpu.SemaphoreType.DMA((n,)),
+            pltpu.SemaphoreType.DMA((len(beside),)),
             pltpu.SemaphoreType.DMA((n, 2 * len(order))),
             pltpu.SemaphoreType.DMA((n, 2 * len(order))),
         ],
         compiler_params=pltpu.CompilerParams(collective_id=0, has_side_effects=True),
-    )(*stripes)
-    return [o.reshape(rows << len(order), o.shape[-1]) for o in outs]
-
-
-def sum_rows(stripes, work):
+    )(*stripes, *beside)
+    return [o.reshape(rows << len(order), o.shape[-1]) for o in outs[:-1]] + [outs[-1]]
+
+
+def sum_body(*refs, n_in, columns, hops, order):
+    n, steps = len(columns), len(order)
+    n_out = 1 + max(c[3] for c in columns)
+    ins, outs = refs[:n_in], refs[n_in : n_in + n_out]
+    keeps = refs[n_in + n_out : n_in + n_out + n]
+    rest = refs[n_in + n_out + n :]
+    arrived, (local, send, recv) = rest[:-3], rest[-3:]
+    arrived = [arrived[steps * k : steps * (k + 1)] for k in range(n)]
+    held = [[[h for h in order if h not in hops[k][:t]] for t in range(steps + 1)] for k in range(n)]
+
+    def side(k, t, bit):
+        return tuple(bit if h == hops[k][t] else slice(None) for h in held[k][t])
+
+    def source(k, t, bit):
+        if t == 0:
+            given, start, width, _, _ = columns[k]
+            return ins[given].at[side(k, 0, bit) + (slice(None), pl.ds(start, width))]
+        return arrived[k][t - 1].at[side(k, t, bit)]
+
+    def move(k, t):
+        copy = pltpu.make_async_remote_copy(
+            src_ref=source(k, t, 1 - my_bit(hops[k][t])),
+            dst_ref=arrived[k][t],
+            send_sem=send.at[k, t],
+            recv_sem=recv.at[k, t],
+            device_id=partner(hops[k][t]),
+            device_id_type=pl.DeviceIdType.MESH,
+        )
+        copy.start()
+        return copy
+
+    own = [pltpu.make_async_copy(source(k, 0, my_bit(hops[k][0])), keeps[k], local.at[k]) for k in range(n)]
+    for c in own:
+        c.start()
+    barrier = pltpu.get_barrier_semaphore()
+    for hop in order:
+        pl.semaphore_signal(barrier, inc=1, device_id=partner(hop), device_id_type=pl.DeviceIdType.MESH)
+    pl.semaphore_wait(barrier, len(order))
+    moving = [[move(k, 0)] for k in range(n)]
+    for c in own:
+        c.wait()
+    for t in range(steps):
+        for k in range(n):
+            moving[k][t].wait_recv()
+            left = held[k][t + 1]
+            place = held[k][t].index(hops[k][t])
+            bit = my_bit(hops[k][t])
+
+            def add(i, carry, k=k, t=t, left=left, place=place, bit=bit):
+                at = tuple((i // 2 ** (len(left) - 1 - d)) % 2 for d in range(len(left)))
+                before = keeps[k][at] if t == 0 else arrived[k][t - 1][at[:place] + (bit,) + at[place:]]
+                total = before.astype(F32) + arrived[k][t][at].astype(F32)
+                if t + 1 < steps:
+                    arrived[k][t][at] = total.astype(BF)
+                else:
+                    _, _, width, out, start = columns[k]
+                    outs[out][:, start : start + width] = total
+                return carry
+
+            if left:
+                lax.fori_loop(0, 2 ** len(left), add, 0)
+            else:
+                add(0, 0)
+            if t + 1 < steps:
+                moving[k].append(move(k, t + 1))
+    for k in range(n):
+        for c in moving[k]:
+            c.wait_send()
+
+def sum_rows(arrays, columns, ordering, widths):
     core, xs, ys, zs, order = exchanges()
-    hops = [[core] + h for h in (xs + ys + zs, ys + zs + xs, zs + xs + ys)]
-    states = [[a.reshape((2,) * len(order) + (-1, a.shape[1])) for a in s] for s in stripes]
-    names = [order] * len(stripes)
-    made = []
-    for step in range(len(order)):
-        keep, send = [], []
-        for arrays, held, hop in zip(states, names, [h[step] for h in hops]):
-            at, bit = held.index(hop), my_bit(hop)
-            for side, b in ((keep, bit), (send, 1 - bit)):
-                side.append(
-                    jnp.concatenate(
-                        [lax.dynamic_index_in_dim(a, b, at, keepdims=False) for a in arrays], axis=-1
-                    )
-                )
-        send = lax.optimization_barrier(send)
-        got = [swap_bit(x, h[step]) for x, h in zip(send, hops)]
-        if step < len(work):
-            made.append(work[step](send))
-            got = after(got, made[-1])
-        got = lax.optimization_barrier(got)
-        states = [[(k.astype(F32) + g.astype(F32)).astype(BF)] for k, g in zip(keep, got)]
-        names = [[n for n in held if n != h[step]] for held, h in zip(names, hops)]
-    return [arrays[0] for arrays in states], made
+    axes = (xs + ys + zs, ys + zs + xs, zs + xs + ys)
+    hops = [[core] + axes[k] for k in ordering]
+    rows = arrays[0].shape[0] >> len(order)
+    n, steps = len(columns), len(order)
+    views = [a.reshape((2,) * steps + (rows, a.shape[1])) for a in arrays]
+    return pl.pallas_call(
+        functools.partial(sum_body, n_in=len(arrays), columns=columns, hops=hops, order=order),
+        in_specs=[pl.BlockSpec(memory_space=pl.ANY)] * len(arrays),
+        out_specs=[pl.BlockSpec(memory_space=pltpu.VMEM)] * len(widths),
+        out_shape=[jax.ShapeDtypeStruct((rows, w), F32) for w in widths],
+        scratch_shapes=[pltpu.VMEM((2,) * (steps - 1) + (rows, c[2]), BF) for c in columns]
+        + [pltpu.VMEM((2,) * (steps - 1 - t) + (rows, c[2]), BF) for c in columns for t in range(steps)]
+        + [pltpu.SemaphoreType.DMA((n,)), pltpu.SemaphoreType.DMA((n, steps)), pltpu.SemaphoreType.DMA((n, steps))],
+        compiler_params=pltpu.CompilerParams(
+            collective_id=1, has_side_effects=True, vmem_limit_bytes=VMEM_BYTES
+        ),
+    )(*views)
 
 
 def rms_parts(v):
@@ -727,11 +799,14 @@
     small = jnp.concatenate([norm_gains, task_table], axis=0).T
     small = jnp.pad(small, ((0, 0), (0, 128 - small.shape[1])))
     enc = encoder_out.reshape(group * keys, width)
-    w_self_in, w_out, w_rest = gather_rows(
+    fold = hidden_output_weight.shape[0] // shard
+    folded = hidden_output_weight.reshape(fold, shard, width)
+    w_self_in, w_out, w_rest, packed = gather_rows(
         [self_in[:, k * width : (k + 1) * width] for k in range(3)]
         + [self_out, jnp.concatenate([cross_query, small], axis=1)],
         [(0, 0, width), (0, width, width), (0, 2 * width, width), (1, 0, width), (2, 0, width + 128)],
         [3 * width, width, width + 128],
+        [cross_out, hidden_in] + [folded[k] for k in range(fold)],
     )
     w_self_out, w_cross_query, w_small = w_out, w_rest[:, :width], w_rest[:, width:]
     w_keyval = lax.all_gather(cross_keyval, ALL, axis=0, tiled=True)
@@ -758,22 +833,16 @@
     qkv = (mm(normed_one.reshape(flat), w_self_in) * scale).astype(BF)
     qkv = qkv.reshape(count, rows, 3 * width)
     self_att, self_lse = self_fwd(target_lengths, qkv)
+    second = lax.all_gather(packed, ALL, axis=0, tiled=True)
+    w_down = [
+        second[:, width * k : width * (k + 1)].reshape(width // shard, shard, width)
+        for k in range(1 + ff // width, 1 + ff // width + fold)
+    ]
+    w_down = jnp.concatenate(w_down, axis=1).reshape(ff, width)
     middle = stream + mm(self_att.reshape(flat), w_self_out).reshape(stream.shape)
     normed_two = (middle * rms_parts(middle) * gains[1]).astype(BF)
     own_q = (mm(normed_two.reshape(flat), w_cross_query) * QSCALE).astype(BF)
     own_q = own_q.reshape(count, rows, width)
-
-    n_dev = width // shard
-    fold = hidden_output_weight.shape[0] // shard
-    in_turn = after(hidden_in, own_q).reshape(shard, n_dev, fold, shard)
-    in_turn = in_turn.swapaxes(1, 2).reshape(shard, ff)
-    folded = [hidden_output_weight[shard * k : shard * (k + 1)] for k in range(fold)]
-    second = lax.all_gather(
-        jnp.concatenate([cross_out, in_turn] + folded, axis=1),
-        ALL,
-        axis=0,
-        tiled=True,
-    )
 
     near_ids = (ids_of(chip, core), ids_of(chip, 1 - core))
     far_ids, far_same_q = [], []
@@ -804,15 +873,21 @@
         far_back.append(back)
     own_part = cross_fwd(near_ids[0], after(own_q, latest), kv, npass)
     parts = [own_part[:2], core_swap(peer_part[:2])]
-    for back in far_back:
+    for back in after(far_back, w_down, own_part):
         parts.append(tuple(jnp.concatenate([b[k] for b in back], axis=0) for k in range(2)))
     cross_att, cross_lse, cross_sum = merge(parts, full=True)
 
-    output, grad_latter, grad_catt, gain_three, grad_second = feed_forward(
-        middle.reshape(flat), cross_att.reshape(flat), cotangent.reshape(flat), gains[2:3], second
+    output, grad_latter, grad_catt, gain_three, grad_second, grad_down = feed_forward(
+        middle.reshape(flat),
+        cross_att.reshape(flat),
+        cotangent.reshape(flat),
+        gains[2:3],
+        second,
+        w_down,
     )
     output, grad_latter = output.reshape(stream.shape), grad_latter.reshape(stream.shape)
     grad_catt, gain_three = grad_catt.reshape(stream.shape), gain_three[0]
+    sum_down = lax.psum_scatter(grad_down, ALL, scatter_dimension=0, tiled=True)
     sum_second = lax.psum_scatter(grad_second, ALL, scatter_dimension=0, tiled=True)
 
     own_sent = (grad_catt, row_stats(grad_catt, cross_sum, cross_lse))
@@ -839,10 +914,36 @@
             latest = joint
             back.append(chip_shift(joint, chips - step))
         dq_parts.append(jnp.concatenate(back, axis=0))
+    sets = [
+        (near_ids[0], *own_part[1:], own_sent[1]),
+        (near_ids[1], *peer_part[1:], peer_sent[1]),
+    ]
+    for step in range(1, chips):
+        for side in range(2):
+            lse, share = (
+                jnp.concatenate([lo[side][k] for lo in far_local[step - 1]], axis=0)
+                for k in range(2)
+            )
+            sets.append((far_ids[step - 1][side], lse, share, far_sent[step - 1][side][1]))
+    ids = jnp.concatenate([s[0] for s in sets])
+    masses = []
+    for _, lse, share, stats in sets:
+        weight = jnp.exp2(lse - stats[:, :, :2])
+        masses.append(jnp.sum(share * weight[:, :, :, None, :], axis=(1, 2, 4)) / (H * rows))
+    masses = jnp.concatenate(masses, axis=0)
+    place = ids[None, :] == jnp.arange(group, dtype=jnp.int32)[:, None]
+    mass = jnp.sum(jnp.where(place[:, :, None], masses[None], 0.0), axis=1)
+    query_grad = jnp.sum((retrieval - mass)[:, :, None] * embeds, axis=1)
+    hop = 1
+    while hop < psg:
+        perm = [(p, p ^ hop) for p in range(psg)]
+        query_grad = query_grad + lax.ppermute(query_grad, "psg", perm)
+        hop *= 2
+
     dkv_flat = after(dkv, joint).reshape(group * keys, 2 * width)
     grad_cross_keyval = mm(enc, dkv_flat, TN).astype(BF)
     total = dq_own.astype(F32) + dq_back.astype(F32)
-    for dq in after(dq_parts, grad_cross_keyval, sum_second):
+    for dq in after(dq_parts, grad_cross_keyval, sum_down, query_grad):
         total = total + dq.astype(F32)
     grad_cross_q = total.astype(BF).reshape(flat)
     grad_cross_query = mm(normed_two.reshape(flat), grad_cross_q, TN).astype(BF)
@@ -864,63 +965,41 @@
     tiny = jnp.pad(tiny, ((0, 0), (0, 128 - tiny.shape[1]))).astype(BF)
     grad_self_in = mm(normed_one.reshape(flat), grad_qkv, TN).astype(BF)
 
-    def distillation(sent):
-        sets = [
-            (near_ids[0], *own_part[1:], own_sent[1]),
-            (near_ids[1], *peer_part[1:], peer_sent[1]),
-        ]
-        for step in range(1, chips):
-            for side in range(2):
-                lse, share = (
-                    jnp.concatenate([lo[side][k] for lo in far_local[step - 1]], axis=0)
-                    for k in range(2)
-                )
-                sets.append((far_ids[step - 1][side], lse, share, far_sent[step - 1][side][1]))
-        ids = jnp.concatenate([s[0] for s in sets])
-        masses = []
-        for _, lse, share, stats in sets:
-            weight = jnp.exp2(lse - stats[:, :, :2])
-            masses.append(jnp.sum(share * weight[:, :, :, None, :], axis=(1, 2, 4)) / (H * rows))
-        masses = jnp.concatenate(masses, axis=0)
-        place = ids[None, :] == jnp.arange(group, dtype=jnp.int32)[:, None]
-        mass = jnp.sum(jnp.where(place[:, :, None], masses[None], 0.0), axis=1)
-        query_grad = jnp.sum((after(retrieval, sent) - mass)[:, :, None] * embeds, axis=1)
-        hop = 1
-        while hop < psg:
-            perm = [(p, p ^ hop) for p in range(psg)]
-            query_grad = query_grad + lax.ppermute(query_grad, "psg", perm)
-            hop *= 2
-        return query_grad
-
-    def encoder_part(sent):
-        return mm(after(dkv_flat, sent), w_keyval, NT).reshape(encoder_out.shape)
-
-    half = width // 2
-    summed, (query_grad, encoder_grad) = sum_rows(
+    given = [
+        after(grad_self_in, sum_second),
+        grad_self_out,
+        grad_cross_query,
+        grad_cross_keyval,
+        tiny,
+    ]
+    (summed,) = sum_rows(
+        given,
         [
-            [grad_self_in[:, :width], grad_cross_query, tiny],
-            [grad_self_in[:, width : 2 * width], grad_cross_keyval[:, :width], grad_self_out[:, :half]],
-            [grad_self_in[:, 2 * width :], grad_cross_keyval[:, width:], grad_self_out[:, half:]],
-        ],
-        [distillation, encoder_part],
+            (0, 0, width, 0, 0),
+            (0, width, width, 0, width),
+            (0, 2 * width, width, 0, 2 * width),
+            (1, 0, width, 0, 3 * width),
+            (2, 0, width, 0, 4 * width),
+            (3, 0, width, 0, 5 * width),
+            (3, width, width, 0, 6 * width),
+            (4, 0, tiny.shape[1], 0, 7 * width),
+        ],
+        [0, 1, 2, 0, 1, 2, 0, 1],
+        [7 * width + tiny.shape[1]],
     )
-    summed = [x.astype(F32) for x in summed]
-    small_sum = summed[0][:, 2 * width :].T
-    sum_in = sum_second[:, width : width + ff].reshape(shard, fold, n_dev, shard)
-    sum_in = sum_in.swapaxes(1, 2).reshape(shard, ff)
+    small_sum = summed[:, 7 * width :].T
+    encoder_grad = mm(dkv_flat, w_keyval, NT).reshape(encoder_out.shape)
     return (
         output,
         input_grad,
         encoder_grad,
-        jnp.concatenate([x[:, :width] for x in summed], axis=1),
-        jnp.concatenate([x[:, 2 * width :] for x in summed[1:]], axis=1),
-        summed[0][:, width : 2 * width],
-        jnp.concatenate([x[:, width : 2 * width] for x in summed[1:]], axis=1),
+        summed[:, : 3 * width],
+        summed[:, 3 * width : 4 * width],
+        summed[:, 4 * width : 5 * width],
+        summed[:, 5 * width : 7 * width],
         sum_second[:, :width].astype(F32),
-        sum_in.astype(F32),
-        jnp.concatenate(
-            [sum_second[:, width * k : width * (k + 1)] for k in range(1 + fold, 1 + 2 * fold)]
-        ).astype(F32),
+        sum_second[:, width:].astype(F32),
+        sum_down.astype(F32),
         small_sum[:3],
         small_sum[3 : 3 + n_tasks],
         query_grad,

time: 645 us -> 622 us (0.964)
  Pallas kernels: 366 us -> 415 us
  local copies, waits for them, and re-layouts: 62.3 us -> 32.9 us
  waiting for transfers between devices: 42.5 us -> 19.1 us
  starting transfers between devices: 34.2 us -> 17.4 us
  other arithmetic: 38.9 us -> 27.3 us
  matrix products: 76.1 us -> 85.9 us
    pallas_call x1 -> x2, Pallas kernels: 56.2 us -> 104 us  [the longest x1 56.5 us: gather_rows(): pl.pallas_call(functools.partial(gather_body, columns=columns, packing=pa...]
    ppermute x17 -> x2, waiting for transfers between devices: 22.3 us -> 1.77 us  [on_device(): query_grad = query_grad + lax.ppermute(query_grad, 'psg', perm)]
    ppermute x17 -> x2, starting transfers between devices: 17.3 us -> 1.36 us  [on_device(): query_grad = query_grad + lax.ppermute(query_grad, 'psg', perm)]
    unnamed x212 -> x130, local copies, waits for them, and re-layouts: 22.7 us -> 10.7 us
    dot_general x11, matrix products: 76.1 us -> 85.9 us  [mm(): return lax.dot_general(a, b, dims, preferred_element_type=F32)]
    squeeze x17 -> x0, local copies, waits for them, and re-layouts: 7.8 us -> none  [sum_rows(): lax.dynamic_index_in_dim(a, b, at, keepdims=False)]
    convert_element_type x17 -> x3, other arithmetic: 9.79 us -> 2.11 us  [the longest x1 0.73 us: on_device(): sum_down.astype(F32)]
  transfers between devices with their start and end apart: 49 -> 35, of which waited for: 10 -> 5; matrix products, arithmetic and copies ran while one was open for 16% -> 21% of each run, Pallas kernels for 47% -> 52%
where the time goes in v4:
time: 622 us; the launch traced here: 613 us
  Pallas kernels  415 us (67%)
  matrix products  85.9 us (14%)
  local copies, waits for them, and re-layouts  32.9 us (5%)
  other arithmetic  27.3 us (4%)
  waiting for transfers between devices  19.1 us (3%)
  starting transfers between devices  17.4 us (3%)
  between operations  14.9 us (2%)
    pallas_call x6, Pallas kernels, cross_bwd(): pl.pallas_call(functools.partial(cross_bwd_body, chunk=min(rows, 256)), g...  123 us
    dot_general x11, matrix products, mm(): return lax.dot_general(a, b, dims, preferred_element_type=F32)  85.9 us
    pallas_call x6, Pallas kernels, cross_fwd(): pl.pallas_call(functools.partial(cross_fwd_body, npass=npass), grid_spec=...  69.1 us
    pallas_call x1, Pallas kernels, gather_rows(): pl.pallas_call(functools.partial(gather_body, columns=columns, packing=pa...  56.5 us
    pallas_call x1, Pallas kernels, sum_rows(): pl.pallas_call(functools.partial(sum_body, n_in=len(arrays), columns=colu...  47.9 us
    pallas_call x1, Pallas kernels, feed_forward(): pl.pallas_call(feed_forward_body, grid=(steps,), in_specs=[whole(tokens,...  46.3 us
    pallas_call x1, Pallas kernels, self_bwd(): pl.pallas_call(functools.partial(self_bwd_body, chunk=min(rows, 256)), gr...  24.5 us
    pallas_call x1, Pallas kernels, keyval(): pl.pallas_call(keyval_body, grid=(n // block,), in_specs=[pl.BlockSpec((b...  19.8 us
  transfers between devices with their start and end apart: 35, of which 5 were waited for; matrix products, arithmetic and copies ran while one was open for 21% of the time, Pallas kernels for 52%

profile of v4, /device:TPU:0, one launch (start us, length us, event | category | flops | bytes accessed | tf_op | source)
XLA Modules:
  0.0 612.5 jit_solution(5583808170942197076)
XLA Ops:
  11.9 56.5 %shard_map.264 = (bf16[2,2,2,2,2,24,2304]{6,5,4,3,2,1,0:T(8,128)(2,1)}, bf16[2,2,2,2,2,24,768]{6,5,4,3,2,1,0:T(8,128)(2,1)}, bf16[2,2,2,2,2,24,896]{6,5,4,3,2,1,0:T(8,128)(2,1)}, bf16[24,6912]{1,0:T(8,128)(2,1)}) custom-call(bf16[24,768]{1,0:T(8,128)(2,1)} %get-tuple-element.276.refs_0_, bf16[24,768]{1,0:T(8,128)(2,1)} %get-tuple-element.275.refs_1_, ...), custom_call_target="tpu_custom_call" | custom-call | tf_op jit(solution)/shard_map/pallas_call | solution.py:627
  74.8 5.6 multiply_convert_fusion
  80.4 13.7 %shard_map.265 = (bf16[2,512,768]{2,1,0:T(8,128)(2,1)}, f32[2,6,2,512]{3,2,1,0:T(2,128)}) custom-call(s32[2]{0:T(128)} %length_ref.3, bf16[2,512,2304]{2,1,0:T(8,128)(2,1)} %bitcast.136, bf16[2,512,2304]{2,1,0:T(8,128)(2,1)} %bitcast.137, bf16[2,512,2304]{2,1,0:T(8,128)(2,1)} %bitcast.138), custom_call_target="tpu_custom_call" | custom-call | flops 6442450944 | bytes 6291456 | tf_op jit(solution)/shard_map/pallas_call | solution.py:226
  94.0 3.0 multiply_reduce_fusion.4
  107.6 19.8 %shard_map.266 = bf16[6144,1536]{1,0:T(8,128)(2,1)} custom-call(bf16[6144,768]{1,0:T(8,128)(2,1)} %bitcast.128, bf16[768,1536]{1,0:T(8,128)(2,1)} %all-gather.3.cloned.1.call-done.w_ref), custom_call_target="tpu_custom_call" | custom-call | flops 14495514624 | bytes 28311552 | tf_op jit(solution)/shard_map/pallas_call | solution.py:403
  127.4 15.9 %shard_map.267 = (bf16[2,512,768]{2,1,0:T(8,128)(2,1)}, f32[2,6,2,512]{3,2,1,0:T(2,128)}, f32[2,6,2,2,512]{4,3,2,1,0:T(2,128)}) custom-call(s32[2]{0:T(128)} %iota_add_fusion.idx, bf16[2,512,768]{2,1,0:T(8,128)(2,1)} %collective-permute-done.2.q_ref, bf16[8,768,1536]{2,1,0:T(8,128)(2,1)} %bitcast.79, bf16[8,768,1536]{2,1,0:T(8,128)(2,1)} %bitcast.80), custom_call_target="tpu_custom_call" | custom-call | flops 9663676416 | bytes 7864320 | tf_op jit(solution)/shard_map/pallas_call | solution.py:100
  144.7 9.2 %shard_map.268 = (bf16[1,512,768]{2,1,0:T(8,128)(2,1)}, f32[1,6,2,512]{3,2,1,0:T(2,128)}, f32[1,6,2,2,512]{4,3,2,1,0:T(2,128)}) custom-call(s32[1]{0:T(128)} %get-tuple-element.269.idx, bf16[1,512,768]{2,1,0:T(8,128)(2,1)} %collective-permute-done.1.q_ref, bf16[8,768,1536]{2,1,0:T(8,128)(2,1)} %bitcast.81, bf16[8,768,1536]{2,1,0:T(8,128)(2,1)} %bitcast.82), custom_call_target="tpu_custom_call" | custom-call | flops 4831838208 | bytes 3932160 | tf_op jit(solution)/shard_map/pallas_call | solution.py:100
  154.8 9.3 %shard_map.269 = (bf16[1,512,768]{2,1,0:T(8,128)(2,1)}, f32[1,6,2,512]{3,2,1,0:T(2,128)}, f32[1,6,2,2,512]{4,3,2,1,0:T(2,128)}) custom-call(s32[1]{0:T(128)} %get-tuple-element.268.idx, bf16[1,512,768]{2,1,0:T(8,128)(2,1)} %copy-done.10, bf16[8,768,1536]{2,1,0:T(8,128)(2,1)} %bitcast.83, bf16[8,768,1536]{2,1,0:T(8,128)(2,1)} %bitcast.84), custom_call_target="tpu_custom_call" | custom-call | flops 4831838208 | bytes 3932160 | tf_op jit(solution)/shard_map/pallas_call | solution.py:100
  165.3 9.4 %shard_map.270 = (bf16[1,512,768]{2,1,0:T(8,128)(2,1)}, f32[1,6,2,512]{3,2,1,0:T(2,128)}, f32[1,6,2,2,512]{4,3,2,1,0:T(2,128)}) custom-call(s32[1]{0:T(128)} %get-tuple-element.270.idx, bf16[1,512,768]{2,1,0:T(8,128)(2,1)} %collective-permute-done.q_ref, bf16[8,768,1536]{2,1,0:T(8,128)(2,1)} %bitcast.85, bf16[8,768,1536]{2,1,0:T(8,128)(2,1)} %bitcast.86), custom_call_target="tpu_custom_call" | custom-call | flops 4831838208 | bytes 3932160 | tf_op jit(solution)/shard_map/pallas_call | solution.py:100
  180.0 9.6 %shard_map.272 = (bf16[1,512,768]{2,1,0:T(8,128)(2,1)}, f32[1,6,2,512]{3,2,1,0:T(2,128)}, f32[1,6,2,2,512]{4,3,2,1,0:T(2,128)}) custom-call(s32[1]{0:T(128)} %get-tuple-element.267.idx, bf16[1,512,768]{2,1,0:T(8,128)(2,1)} %copy-done.9, bf16[8,768,1536]{2,1,0:T(8,128)(2,1)} %bitcast.87, bf16[8,768,1536]{2,1,0:T(8,128)(2,1)} %bitcast.88), custom_call_target="tpu_custom_call" | custom-call | flops 4831838208 | bytes 3932160 | tf_op jit(solution)/shard_map/pallas_call | solution.py:100
  193.3 2.9 shard_map.273
  198.3 15.8 %shard_map.274 = (bf16[2,512,768]{2,1,0:T(8,128)(2,1)}, f32[2,6,2,512]{3,2,1,0:T(2,128)}, f32[2,6,2,2,512]{4,3,2,1,0:T(2,128)}) custom-call(s32[2]{0:T(128)} %iota_add_fusion.3.idx, bf16[2,512,768]{2,1,0:T(8,128)(2,1)} %bitcast.10.q_ref, bf16[8,768,1536]{2,1,0:T(8,128)(2,1)} %bitcast.90, bf16[8,768,1536]{2,1,0:T(8,128)(2,1)} %bitcast.89), custom_call_target="tpu_custom_call" | custom-call | flops 9663676416 | bytes 7864320 | tf_op jit(solution)/shard_map/pallas_call | solution.py:100
  219.2 9.5 %collective-permute-done.13 = f32[1,6,2,512]{3,2,1,0:T(2,128)S(1)} collective-permute-done((f32[1,6,2,512]{3,2,1,0:T(2,128)}, f32[1,6,2,512]{3,2,1,0:T(2,128)S(1)}, u32[]{:S(2)}, u32[]{:S(2)}) %collective-permute-start.13) | collective-permute-done | bytes 24608 | tf_op jit(solution)/shard_map/ppermute | solution.py:794
  232.6 4.9 shard_map.275
  237.6 46.3 %shard_map.276 = (bf16[1024,768]{1,0:T(8,128)(2,1)}, f32[1024,768]{1,0:T(8,128)}, bf16[1024,768]{1,0:T(8,128)(2,1)}, f32[1,768]{1,0:T(1,128)}, bf16[768,3840]{1,0:T(8,128)(2,1)}, /*index=5*/bf16[3072,768]{1,0:T(8,128)(2,1)}) custom-call(f32[1024,768]{1,0:T(8,128)} %bitcast.105, bf16[1024,768]{1,0:T(8,128)(2,1)} %bitcast.133, bf16[1024,768]{1,0:T(8,128)(2,1)} %bitcast.132, ...), custom_call_target="tpu_custom_call" | custom-call | flops 32614907904 | bytes 53477376 | tf_op jit(solution)/shard_map/pallas_call | solution.py:493
  290.8 4.0 shard_map.277.stat_ref
  298.3 28.8 %shard_map.278 = (bf16[2,512,768]{2,1,0:T(8,128)(2,1)}, bf16[8,768,1536]{2,1,0:T(8,128)(2,1)}) custom-call(s32[2]{0:T(128)} %iota_add_fusion.3.idx, bf16[2,512,768]{2,1,0:T(8,128)(2,1)} %bitcast.10.q_ref, bf16[8,768,1536]{2,1,0:T(8,128)(2,1)} %bitcast.91, bf16[8,768,1536]{2,1,0:T(8,128)(2,1)} %bitcast.92, bf16[2,512,768]{2,1,0:T(8,128)(2,1)} %bitcast.119, ...), custom_call_target="tpu_custom_call" | custom-call | flops 24159191040 | bytes 14155776 | tf_op jit(solution)/shard_map/pallas_call | solution.py:170
  328.8 4.6 collective-permute-done.18
  334.2 29.0 %shard_map.279 = (bf16[2,512,768]{2,1,0:T(8,128)(2,1)}, bf16[8,768,1536]{2,1,0:T(8,128)(2,1)}) custom-call(s32[2]{0:T(128)} %iota_add_fusion.idx, bf16[2,512,768]{2,1,0:T(8,128)(2,1)} %collective-permute-done.2.q_ref, bf16[8,768,1536]{2,1,0:T(8,128)(2,1)} %bitcast.93, bf16[8,768,1536]{2,1,0:T(8,128)(2,1)} %bitcast.94, ...), custom_call_target="tpu_custom_call", output_to_operand_aliasing={{1}: (6, {})} | custom-call | flops 24159191040 | bytes 14155776 | tf_op jit(solution)/shard_map/pallas_call | solution.py:170
  371.4 16.2 %shard_map.280 = (bf16[1,512,768]{2,1,0:T(8,128)(2,1)}, bf16[8,768,1536]{2,1,0:T(8,128)(2,1)}) custom-call(s32[1]{0:T(128)} %get-tuple-element.268.idx, bf16[1,512,768]{2,1,0:T(8,128)(2,1)} %copy-done.10, bf16[8,768,1536]{2,1,0:T(8,128)(2,1)} %bitcast.95, bf16[8,768,1536]{2,1,0:T(8,128)(2,1)} %bitcast.96, ...), custom_call_target="tpu_custom_call", output_to_operand_aliasing={{1}: (6, {})} | custom-call | flops 12079595520 | bytes 7077888 | tf_op jit(solution)/shard_map/pallas_call | solution.py:170
  387.6 16.1 %shard_map.281 = (bf16[1,512,768]{2,1,0:T(8,128)(2,1)}, bf16[8,768,1536]{2,1,0:T(8,128)(2,1)}) custom-call(s32[1]{0:T(128)} %get-tuple-element.269.idx, bf16[1,512,768]{2,1,0:T(8,128)(2,1)} %collective-permute-done.1.q_ref, bf16[8,768,1536]{2,1,0:T(8,128)(2,1)} %bitcast.97, bf16[8,768,1536]{2,1,0:T(8,128)(2,1)} %bitcast.98, ...), custom_call_target="tpu_custom_call", output_to_operand_aliasing={{1}: (6, {})} | custom-call | flops 12079595520 | bytes 7077888 | tf_op jit(solution)/shard_map/pallas_call | solution.py:170
  408.0 16.1 %shard_map.282 = (bf16[1,512,768]{2,1,0:T(8,128)(2,1)}, bf16[8,768,1536]{2,1,0:T(8,128)(2,1)}) custom-call(s32[1]{0:T(128)} %get-tuple-element.267.idx, bf16[1,512,768]{2,1,0:T(8,128)(2,1)} %copy-done.9, bf16[8,768,1536]{2,1,0:T(8,128)(2,1)} %bitcast.99, bf16[8,768,1536]{2,1,0:T(8,128)(2,1)} %bitcast.100, ...), custom_call_target="tpu_custom_call", output_to_operand_aliasing={{1}: (6, {})} | custom-call | flops 12079595520 | bytes 7077888 | tf_op jit(solution)/shard_map/pallas_call | solution.py:170
  424.3 16.5 %shard_map.283 = (bf16[1,512,768]{2,1,0:T(8,128)(2,1)}, bf16[8,768,1536]{2,1,0:T(8,128)(2,1)}) custom-call(s32[1]{0:T(128)} %get-tuple-element.270.idx, bf16[1,512,768]{2,1,0:T(8,128)(2,1)} %collective-permute-done.q_ref, bf16[8,768,1536]{2,1,0:T(8,128)(2,1)} %bitcast.101, bf16[8,768,1536]{2,1,0:T(8,128)(2,1)} %bitcast.102, ...), custom_call_target="tpu_custom_call", output_to_operand_aliasing={{1}: (6, {})} | custom-call | flops 12079595520 | bytes 7077888 | tf_op jit(solution)/shard_map/pallas_call | solution.py:170
  443.1 22.7 %convolution_convert_fusion = bf16[1536,768]{0,1:T(8,128)(2,1)} fusion(bf16[6144,1536]{1,0:T(8,128)(2,1)} %bitcast.103, bf16[6144,768]{1,0:T(8,128)(2,1)} %bitcast.129), kind=kOutput, calls=%fused_computation.4 | convolution fusion | flops 14496694272 | bytes 30670848 | tf_op jit(solution)/shard_map/dot_general | solution.py:29
  465.8 21.2 %fusion.2 = f32[8,2,384,768]{3,2,1,0:T(8,128)} fusion(bf16[8,2,384,1536]{3,2,1,0:T(8,128)(2,1)} %bitcast.104, bf16[768,1536]{1,0:T(8,128)(2,1)S(1)} %copy-done.59), kind=kOutput, calls=%fused_computation.20 | convolution fusion | flops 14495514624 | bytes 40108032 | tf_op jit(solution)/shard_map/dot_general | solution.py:29
  488.4 4.7 multiply_reduce_fusion
  497.0 24.5 %shard_map.284 = bf16[2,512,2304]{2,1,0:T(8,128)(2,1)} custom-call(s32[2]{0:T(128)} %length_ref.3, bf16[2,512,2304]{2,1,0:T(8,128)(2,1)} %bitcast.139, bf16[2,512,2304]{2,1,0:T(8,128)(2,1)} %bitcast.140, bf16[2,512,2304]{2,1,0:T(8,128)(2,1)} %bitcast.141, bf16[2,512,768]{2,1,0:T(8,128)(2,1)} %bitcast.143, f32[2,6,2,512]{3,2,1,0:T(2,128)} %get-tuple-element.154.lse_ref), custom_call_target="tpu_custom_call" | custom-call | flops 16106127360 | bytes 12582912 | tf_op jit(solution)/shard_map/pallas_call | solution.py:300
  521.6 7.3 %multiply_reduce_fusion.1 = (bf16[768]{0:T(1024)(128)(2,1)S(1)}, f32[2,512]{1,0:T(2,128)S(1)}, f32[2,512,768]{2,1,0:T(8,128)S(1)}) fusion(bf16[2,512,768]{2,1,0:T(8,128)(2,1)S(1)} %copy-done.3, f32[2,512]{1,0:T(2,128)S(1)} %copy-done.38, f32[2,768]{1,0:T(2,128)S(1)} %copy-done.26, f32[768]{0:T(1024)S(1)} %copy-done.34, ...), kind=kOutput, calls=%fused_computation.6 | convolution fusion | flops 3630168320 | bytes 12995072 | tf_op jit(solution)/shard_map/dot_general | solution.py:29
  533.3 4.5 bitcast_convert_fusion.2
  537.8 4.1 bitcast_convert_fusion.1
  541.9 7.7 %bitcast_convert_fusion = bf16[768,2304]{1,0:T(8,128)(2,1)} fusion(bf16[2,512,768]{2,1,0:T(8,128)(2,1)S(1)} %copy-done.15, bf16[2,512,2304]{2,1,0:T(8,128)(2,1)} %shard_map.284), kind=kOutput, calls=%fused_computation.2 | convolution fusion | flops 3625648128 | bytes 9830400 | tf_op jit(solution)/shard_map/dot_general | solution.py:29
  549.6 47.9 %shard_map.285 = f32[24,5504]{1,0:T(8,128)} custom-call(bf16[2,2,2,2,2,24,2304]{6,5,4,3,2,1,0:T(8,128)(2,1)} %bitcast.113, bf16[2,2,2,2,2,24,768]{6,5,4,3,2,1,0:T(8,128)(2,1)} %bitcast.122, bf16[2,2,2,2,2,24,768]{6,5,4,3,2,1,0:T(8,128)(2,1)} %bitcast.112, bf16[2,2,2,2,2,24,1536]{6,5,4,3,2,1,0:T(8,128)(2,1)} %bitcast.115, ...), custom_call_target="tpu_custom_call" | custom-call | tf_op jit(solution)/shard_map/pallas_call | solution.py:724
  (295 shorter events, 90.6 us)
Async XLA Ops:
  7.2 100.4 %all-gather.3.cloned.1.call-start = ((), (), s32[]{:S(2)}) async-start(), calls=%async_computation.2 | async-start | bytes 2433024 | tf_op jit(solution)/shard_map/all_gather | solution.py:812
  7.9 206.2 %all-gather.5.cloned.1.call-start = ((), (), s32[]{:S(2)}) async-start(), calls=%async_computation.3 | async-start | bytes 10948608 | tf_op jit(solution)/shard_map/all_gather | solution.py:836
  68.4 419.9 %reduce-scatter.3.cloned.1.call-start = ((), (), s32[]{:S(2)}) async-start(), calls=%async_computation.4 | async-start | bytes 4866048 | tf_op jit(solution)/shard_map/reduce_scatter | solution.py:890
  102.0 25.4 %collective-permute-start.2 = (bf16[2,512,768]{2,1,0:T(8,128)(2,1)}, bf16[2,512,768]{2,1,0:T(8,128)(2,1)}, u32[]{:S(2)}, u32[]{:S(2)}) collective-permute-start(bf16[2,512,768]{2,1,0:T(8,128)(2,1)} %bitcast.10.q_ref), channel_id=1, source_target_pairs={{0,1},{1,0},{2,3},{3,2},{4,5},{5,4},{6,7},{7,6},{8,9},{9,8},{10,11... | collective-permute-start | bytes 4718600 | tf_op jit(solution)/shard_map/ppermute | solution.py:790
  105.1 38.2 %collective-permute-start.1 = (bf16[1,512,768]{2,1,0:T(8,128)(2,1)}, bf16[1,512,768]{2,1,0:T(8,128)(2,1)}, u32[]{:S(2)}, u32[]{:S(2)}) collective-permute-start(bf16[1,512,768]{2,1,0:T(8,128)(2,1)} %get-tuple-element.251), channel_id=1, source_target_pairs={{0,2},{1,3},{2,0},{3,1},{4,6},{5,7},{6,4},{7,5},{8,10},{9,11},{10,... | collective-permute-start | bytes 2359304 | tf_op jit(solution)/shard_map/ppermute | solution.py:794
  106.8 57.9 %collective-permute-start = (bf16[1,512,768]{2,1,0:T(8,128)(2,1)}, bf16[1,512,768]{2,1,0:T(8,128)(2,1)}, u32[]{:S(2)}, u32[]{:S(2)}) collective-permute-start(bf16[1,512,768]{2,1,0:T(8,128)(2,1)} %get-tuple-element.252), channel_id=1, source_target_pairs={{0,2},{1,3},{2,0},{3,1},{4,6},{5,7},{6,4},{7,5},{8,10},{9,11},{10,... | collective-permute-start | bytes 2359304 | tf_op jit(solution)/shard_map/ppermute | solution.py:794
  143.3 10.6 %collective-permute-start.3 = (bf16[1,512,768]{2,1,0:T(8,128)(2,1)}, bf16[1,512,768]{2,1,0:T(8,128)(2,1)S(1)}, u32[]{:S(2)}, u32[]{:S(2)}) collective-permute-start(bf16[1,512,768]{2,1,0:T(8,128)(2,1)} %collective-permute-done.1.q_ref), channel_id=1, source_target_pairs={{0,1},{1,0},{2,3},{3,2},{4,5},{5,4},{6,7},{7,6},{8,9},{9,8},{10,11... | collective-permute-start | bytes 2359304 | tf_op jit(solution)/shard_map/ppermute | solution.py:790
  164.1 10.5 %collective-permute-start.5 = (bf16[1,512,768]{2,1,0:T(8,128)(2,1)}, bf16[1,512,768]{2,1,0:T(8,128)(2,1)S(1)}, u32[]{:S(2)}, u32[]{:S(2)}) collective-permute-start(bf16[1,512,768]{2,1,0:T(8,128)(2,1)} %get-tuple-element.98), channel_id=1, source_target_pairs={{0,1},{1,0},{2,3},{3,2},{4,5},{5,4},{6,7},{7,6},{8,9},{9,8},{10,11... | collective-permute-start | bytes 2359304 | tf_op jit(solution)/shard_map/ppermute | solution.py:790
  164.8 14.3 %collective-permute-start.4 = (bf16[1,512,768]{2,1,0:T(8,128)(2,1)}, bf16[1,512,768]{2,1,0:T(8,128)(2,1)S(1)}, u32[]{:S(2)}, u32[]{:S(2)}) collective-permute-start(bf16[1,512,768]{2,1,0:T(8,128)(2,1)} %collective-permute-done.q_ref), channel_id=1, source_target_pairs={{0,1},{1,0},{2,3},{3,2},{4,5},{5,4},{6,7},{7,6},{8,9},{9,8},{10,11... | collective-permute-start | bytes 2359304 | tf_op jit(solution)/shard_map/ppermute | solution.py:790
  164.8 9.8 %collective-permute-start.6 = (f32[1,6,2,512]{3,2,1,0:T(2,128)}, f32[1,6,2,512]{3,2,1,0:T(2,128)S(1)}, u32[]{:S(2)}, u32[]{:S(2)}) collective-permute-start(f32[1,6,2,512]{3,2,1,0:T(2,128)} %get-tuple-element.99), channel_id=1, source_target_pairs={{0,1},{1,0},{2,3},{3,2},{4,5},{5,4},{6,7},{7,6},{8,9},{9,8},{10,11... | collective-permute-start | bytes 73736 | tf_op jit(solution)/shard_map/ppermute | solution.py:790
  189.6 3.1 collective-permute-start.7
  189.7 3.1 collective-permute-start.8
  190.6 41.4 %collective-permute-start.9 = (bf16[2,512,768]{2,1,0:T(8,128)(2,1)}, bf16[2,512,768]{2,1,0:T(8,128)(2,1)}, u32[]{:S(2)}, u32[]{:S(2)}) collective-permute-start(bf16[2,512,768]{2,1,0:T(8,128)(2,1)} %get-tuple-element.90), channel_id=1, source_target_pairs={{0,1},{1,0},{2,3},{3,2},{4,5},{5,4},{6,7},{7,6},{8,9},{9,8},{10,11... | collective-permute-start | bytes 4718600 | tf_op jit(solution)/shard_map/ppermute | solution.py:790
  190.7 28.5 %collective-permute-start.10 = (bf16[1,512,768]{2,1,0:T(8,128)(2,1)}, bf16[1,512,768]{2,1,0:T(8,128)(2,1)}, u32[]{:S(2)}, u32[]{:S(2)}) collective-permute-start(bf16[1,512,768]{2,1,0:T(8,128)(2,1)} %get-tuple-element.105), channel_id=1, source_target_pairs={{0,2},{1,3},{2,0},{3,1},{4,6},{5,7},{6,4},{7,5},{8,10},{9,11},{10,... | collective-permute-start | bytes 2359304 | tf_op jit(solution)/shard_map/ppermute | solution.py:794
  192.4 26.8 %collective-permute-start.11 = (f32[1,6,2,512]{3,2,1,0:T(2,128)S(1)}, f32[1,6,2,512]{3,2,1,0:T(2,128)S(1)}, u32[]{:S(2)}, u32[]{:S(2)}) collective-permute-start(f32[1,6,2,512]{3,2,1,0:T(2,128)S(1)} %copy-done.62), channel_id=1, source_target_pairs={{0,2},{1,3},{2,0},{3,1},{4,6},{5,7},{6,4},{7,5},{8,10},{9,11},{10,... | collective-permute-start | bytes 73736 | tf_op jit(solution)/shard_map/ppermute | solution.py:794
  196.3 32.4 %collective-permute-start.12 = (bf16[1,512,768]{2,1,0:T(8,128)(2,1)}, bf16[1,512,768]{2,1,0:T(8,128)(2,1)}, u32[]{:S(2)}, u32[]{:S(2)}) collective-permute-start(bf16[1,512,768]{2,1,0:T(8,128)(2,1)} %get-tuple-element.109), channel_id=1, source_target_pairs={{0,2},{1,3},{2,0},{3,1},{4,6},{5,7},{6,4},{7,5},{8,10},{9,11},{10,... | collective-permute-start | bytes 2359304 | tf_op jit(solution)/shard_map/ppermute | solution.py:794
  197.9 30.8 %collective-permute-start.13 = (f32[1,6,2,512]{3,2,1,0:T(2,128)}, f32[1,6,2,512]{3,2,1,0:T(2,128)S(1)}, u32[]{:S(2)}, u32[]{:S(2)}) collective-permute-start(f32[1,6,2,512]{3,2,1,0:T(2,128)} %get-tuple-element.113), channel_id=1, source_target_pairs={{0,2},{1,3},{2,0},{3,1},{4,6},{5,7},{6,4},{7,5},{8,10},{9,11},{10,... | collective-permute-start | bytes 73736 | tf_op jit(solution)/shard_map/ppermute | solution.py:794
  219.2 12.8 %collective-permute-start.14 = (f32[2,6,2,512]{3,2,1,0:T(2,128)S(1)}, f32[2,6,2,512]{3,2,1,0:T(2,128)S(1)}, u32[]{:S(2)}, u32[]{:S(2)}) collective-permute-start(f32[2,6,2,512]{3,2,1,0:T(2,128)S(1)} %copy-done.29), channel_id=1, source_target_pairs={{0,1},{1,0},{2,3},{3,2},{4,5},{5,4},{6,7},{7,6},{8,9},{9,8},{10,11... | collective-permute-start | bytes 147464 | tf_op jit(solution)/shard_map/ppermute | solution.py:790
  283.9 265.7 %reduce-scatter.5.cloned.1.call-start = ((), (), s32[]{:S(2)}) async-start(), calls=%async_computation.5 | async-start | bytes 6082560 | tf_op jit(solution)/shard_map/reduce_scatter | solution.py:891
  286.7 3.6 collective-permute-start.27
  294.8 34.0 %collective-permute-start.19 = (f32[2,6,4,512]{3,2,1,0:T(4,128)}, f32[2,6,4,512]{3,2,1,0:T(4,128)S(1)}, u32[]{:S(2)}, u32[]{:S(2)}) collective-permute-start(f32[2,6,4,512]{3,2,1,0:T(4,128)} %shard_map.277.stat_ref), channel_id=1, source_target_pairs={{0,2},{1,3},{2,0},{3,1},{4,6},{5,7},{6,4},{7,5},{8,10},{9,11},{10,... | collective-permute-start | bytes 294920 | tf_op jit(solution)/shard_map/ppermute | solution.py:794
  296.1 31.6 %collective-permute-start.16 = (f32[2,6,4,512]{3,2,1,0:T(4,128)}, f32[2,6,4,512]{3,2,1,0:T(4,128)}, u32[]{:S(2)}, u32[]{:S(2)}) collective-permute-start(f32[2,6,4,512]{3,2,1,0:T(4,128)} %shard_map.277.stat_ref), channel_id=1, source_target_pairs={{0,1},{1,0},{2,3},{3,2},{4,5},{5,4},{6,7},{7,6},{8,9},{9,8},{10,11... | collective-permute-start | bytes 294920 | tf_op jit(solution)/shard_map/ppermute | solution.py:790
  296.1 37.2 %collective-permute-start.18 = (bf16[2,512,768]{2,1,0:T(8,128)(2,1)S(1)}, bf16[2,512,768]{2,1,0:T(8,128)(2,1)S(1)}, u32[]{:S(2)}, u32[]{:S(2)}) collective-permute-start(bf16[2,512,768]{2,1,0:T(8,128)(2,1)S(1)} %bitcast.120), channel_id=1, source_target_pairs={{0,2},{1,3},{2,0},{3,1},{4,6},{5,7},{6,4},{7,5},{8,10},{9,11},{10,... | collective-permute-start | bytes 4718600 | tf_op jit(solution)/shard_map/ppermute | solution.py:794
  296.9 36.8 %collective-permute-start.15 = (bf16[2,512,768]{2,1,0:T(8,128)(2,1)S(1)}, bf16[2,512,768]{2,1,0:T(8,128)(2,1)}, u32[]{:S(2)}, u32[]{:S(2)}) collective-permute-start(bf16[2,512,768]{2,1,0:T(8,128)(2,1)S(1)} %bitcast.121), channel_id=1, source_target_pairs={{0,1},{1,0},{2,3},{3,2},{4,5},{5,4},{6,7},{7,6},{8,9},{9,8},{10,11... | collective-permute-start | bytes 4718600 | tf_op jit(solution)/shard_map/ppermute | solution.py:790
  333.4 29.8 %collective-permute-start.21 = (f32[2,6,4,512]{3,2,1,0:T(4,128)S(1)}, f32[2,6,4,512]{3,2,1,0:T(4,128)S(1)}, u32[]{:S(2)}, u32[]{:S(2)}) collective-permute-start(f32[2,6,4,512]{3,2,1,0:T(4,128)S(1)} %collective-permute-done.19), channel_id=1, source_target_pairs={{0,1},{1,0},{2,3},{3,2},{4,5},{5,4},{6,7},{7,6},{8,9},{9,8},{10,11... | collective-permute-start | bytes 294920 | tf_op jit(solution)/shard_map/ppermute | solution.py:790
  333.6 36.1 %collective-permute-start.20 = (bf16[2,512,768]{2,1,0:T(8,128)(2,1)S(1)}, bf16[2,512,768]{2,1,0:T(8,128)(2,1)S(1)}, u32[]{:S(2)}, u32[]{:S(2)}) collective-permute-start(bf16[2,512,768]{2,1,0:T(8,128)(2,1)S(1)} %collective-permute-done.18), channel_id=1, source_target_pairs={{0,1},{1,0},{2,3},{3,2},{4,5},{5,4},{6,7},{7,6},{8,9},{9,8},{10,11... | collective-permute-start | bytes 4718600 | tf_op jit(solution)/shard_map/ppermute | solution.py:790
  365.3 3.9 collective-permute-start.30
  367.2 121.1 %collective-permute-start.17 = (bf16[2,512,768]{2,1,0:T(8,128)(2,1)}, bf16[2,512,768]{2,1,0:T(8,128)(2,1)}, u32[]{:S(2)}, u32[]{:S(2)}) collective-permute-start(bf16[2,512,768]{2,1,0:T(8,128)(2,1)} %get-tuple-element.133), channel_id=1, source_target_pairs={{0,1},{1,0},{2,3},{3,2},{4,5},{5,4},{6,7},{7,6},{8,9},{9,8},{10,11... | collective-permute-start | bytes 4718600 | tf_op jit(solution)/shard_map/ppermute | solution.py:790
  387.5 16.1 %collective-permute-start.22 = (bf16[1,512,768]{2,1,0:T(8,128)(2,1)}, bf16[1,512,768]{2,1,0:T(8,128)(2,1)S(1)}, u32[]{:S(2)}, u32[]{:S(2)}) collective-permute-start(bf16[1,512,768]{2,1,0:T(8,128)(2,1)} %get-tuple-element.141), channel_id=1, source_target_pairs={{0,1},{1,0},{2,3},{3,2},{4,5},{5,4},{6,7},{7,6},{8,9},{9,8},{10,11... | collective-permute-start | bytes 2359304 | tf_op jit(solution)/shard_map/ppermute | solution.py:790
  405.0 82.0 %collective-permute-start.23 = (bf16[1,512,768]{2,1,0:T(8,128)(2,1)S(1)}, bf16[1,512,768]{2,1,0:T(8,128)(2,1)S(1)}, u32[]{:S(2)}, u32[]{:S(2)}) collective-permute-start(bf16[1,512,768]{2,1,0:T(8,128)(2,1)S(1)} %add_convert_fusion.2), channel_id=1, source_target_pairs={{0,2},{1,3},{2,0},{3,1},{4,6},{5,7},{6,4},{7,5},{8,10},{9,11},{10,... | collective-permute-start | bytes 2359304 | tf_op jit(solution)/shard_map/ppermute | solution.py:794
  424.1 16.7 %collective-permute-start.24 = (bf16[1,512,768]{2,1,0:T(8,128)(2,1)}, bf16[1,512,768]{2,1,0:T(8,128)(2,1)S(1)}, u32[]{:S(2)}, u32[]{:S(2)}) collective-permute-start(bf16[1,512,768]{2,1,0:T(8,128)(2,1)} %get-tuple-element.147), channel_id=1, source_target_pairs={{0,1},{1,0},{2,3},{3,2},{4,5},{5,4},{6,7},{7,6},{8,9},{9,8},{10,11... | collective-permute-start | bytes 2359304 | tf_op jit(solution)/shard_map/ppermute | solution.py:790
  442.2 44.9 %collective-permute-start.25 = (bf16[1,512,768]{2,1,0:T(8,128)(2,1)S(1)}, bf16[1,512,768]{2,1,0:T(8,128)(2,1)S(1)}, u32[]{:S(2)}, u32[]{:S(2)}) collective-permute-start(bf16[1,512,768]{2,1,0:T(8,128)(2,1)S(1)} %add_convert_fusion.1), channel_id=1, source_target_pairs={{0,2},{1,3},{2,0},{3,1},{4,6},{5,7},{6,4},{7,5},{8,10},{9,11},{10,... | collective-permute-start | bytes 2359304 | tf_op jit(solution)/shard_map/ppermute | solution.py:794
  (66 other events, 1115.6 us)
Sparse Core Ops, SparseCore 0:
  10.9 69.0 all-gather.2
  83.0 94.3 all-gather.4
  284.0 107.8 reduce-scatter.2
  398.4 121.0 reduce-scatter.4

commit v5 on v4

--- a/solution.py
+++ b/solution.py
@@ -972,19 +972,18 @@
         grad_cross_keyval,
         tiny,
     ]
+    half = width // 2
+    stripes = [
+        (array, half * k, half)
+        for array, halves in ((0, 6), (1, 2), (2, 2), (3, 4))
+        for k in range(halves)
+    ]
+    stripes = [(*stripe, 0, half * k) for k, stripe in enumerate(stripes)]
+    stripes.append((4, 0, tiny.shape[1], 0, 7 * width))
     (summed,) = sum_rows(
         given,
-        [
-            (0, 0, width, 0, 0),
-            (0, width, width, 0, width),
-            (0, 2 * width, width, 0, 2 * width),
-            (1, 0, width, 0, 3 * width),
-            (2, 0, width, 0, 4 * width),
-            (3, 0, width, 0, 5 * width),
-            (3, width, width, 0, 6 * width),
-            (4, 0, tiny.shape[1], 0, 7 * width),
-        ],
-        [0, 1, 2, 0, 1, 2, 0, 1],
+        stripes,
+        [(0, 1, 2, 0, 1)[k % 5] for k in range(len(stripes))],
         [7 * width + tiny.shape[1]],
     )
     small_sum = summed[:, 7 * width :].T

time: 622 us -> 618 us (level)
  no operation moved by 1% of the time
where the time goes in v5:
time: 618 us; the launch traced here: 609 us
  Pallas kernels  412 us (67%)
  matrix products  85.9 us (14%)
  local copies, waits for them, and re-layouts  32.9 us (5%)
  other arithmetic  27.3 us (4%)
  waiting for transfers between devices  19.1 us (3%)
  starting transfers between devices  17.4 us (3%)
  between operations  14.9 us (2%)
    pallas_call x6, Pallas kernels, cross_bwd(): pl.pallas_call(functools.partial(cross_bwd_body, chunk=min(rows, 256)), g...  123 us
    dot_general x11, matrix products, mm(): return lax.dot_general(a, b, dims, preferred_element_type=F32)  85.9 us
    pallas_call x6, Pallas kernels, cross_fwd(): pl.pallas_call(functools.partial(cross_fwd_body, npass=npass), grid_spec=...  69.1 us
    pallas_call x1, Pallas kernels, gather_rows(): pl.pallas_call(functools.partial(gather_body, columns=columns, packing=pa...  56.5 us
    pallas_call x1, Pallas kernels, feed_forward(): pl.pallas_call(feed_forward_body, grid=(steps,), in_specs=[whole(tokens,...  46.3 us
    pallas_call x1, Pallas kernels, sum_rows(): pl.pallas_call(functools.partial(sum_body, n_in=len(arrays), columns=colu...  44.6 us
    pallas_call x1, Pallas kernels, self_bwd(): pl.pallas_call(functools.partial(self_bwd_body, chunk=min(rows, 256)), gr...  24.5 us
    pallas_call x1, Pallas kernels, keyval(): pl.pallas_call(keyval_body, grid=(n // block,), in_specs=[pl.BlockSpec((b...  19.8 us
  transfers between devices with their start and end apart: 35, of which 5 were waited for; matrix products, arithmetic and copies ran while one was open for 21% of the time, Pallas kernels for 52%

profile of v5, /device:TPU:0, one launch (start us, length us, event | category | flops | bytes accessed | tf_op | source)
XLA Modules:
  0.0 609.3 jit_solution(15569825694944796843)
XLA Ops:
  11.9 56.5 %shard_map.264 = (bf16[2,2,2,2,2,24,2304]{6,5,4,3,2,1,0:T(8,128)(2,1)}, bf16[2,2,2,2,2,24,768]{6,5,4,3,2,1,0:T(8,128)(2,1)}, bf16[2,2,2,2,2,24,896]{6,5,4,3,2,1,0:T(8,128)(2,1)}, bf16[24,6912]{1,0:T(8,128)(2,1)}) custom-call(bf16[24,768]{1,0:T(8,128)(2,1)} %get-tuple-element.276.refs_0_, bf16[24,768]{1,0:T(8,128)(2,1)} %get-tuple-element.275.refs_1_, ...), custom_call_target="tpu_custom_call" | custom-call | tf_op jit(solution)/shard_map/pallas_call | solution.py:627
  74.8 5.6 multiply_convert_fusion
  80.4 13.7 %shard_map.265 = (bf16[2,512,768]{2,1,0:T(8,128)(2,1)}, f32[2,6,2,512]{3,2,1,0:T(2,128)}) custom-call(s32[2]{0:T(128)} %length_ref.3, bf16[2,512,2304]{2,1,0:T(8,128)(2,1)} %bitcast.136, bf16[2,512,2304]{2,1,0:T(8,128)(2,1)} %bitcast.137, bf16[2,512,2304]{2,1,0:T(8,128)(2,1)} %bitcast.138), custom_call_target="tpu_custom_call" | custom-call | flops 6442450944 | bytes 6291456 | tf_op jit(solution)/shard_map/pallas_call | solution.py:226
  94.0 3.0 multiply_reduce_fusion.4
  107.6 19.8 %shard_map.266 = bf16[6144,1536]{1,0:T(8,128)(2,1)} custom-call(bf16[6144,768]{1,0:T(8,128)(2,1)} %bitcast.128, bf16[768,1536]{1,0:T(8,128)(2,1)} %all-gather.3.cloned.1.call-done.w_ref), custom_call_target="tpu_custom_call" | custom-call | flops 14495514624 | bytes 28311552 | tf_op jit(solution)/shard_map/pallas_call | solution.py:403
  127.4 15.9 %shard_map.267 = (bf16[2,512,768]{2,1,0:T(8,128)(2,1)}, f32[2,6,2,512]{3,2,1,0:T(2,128)}, f32[2,6,2,2,512]{4,3,2,1,0:T(2,128)}) custom-call(s32[2]{0:T(128)} %iota_add_fusion.idx, bf16[2,512,768]{2,1,0:T(8,128)(2,1)} %collective-permute-done.2.q_ref, bf16[8,768,1536]{2,1,0:T(8,128)(2,1)} %bitcast.79, bf16[8,768,1536]{2,1,0:T(8,128)(2,1)} %bitcast.80), custom_call_target="tpu_custom_call" | custom-call | flops 9663676416 | bytes 7864320 | tf_op jit(solution)/shard_map/pallas_call | solution.py:100
  144.7 9.2 %shard_map.268 = (bf16[1,512,768]{2,1,0:T(8,128)(2,1)}, f32[1,6,2,512]{3,2,1,0:T(2,128)}, f32[1,6,2,2,512]{4,3,2,1,0:T(2,128)}) custom-call(s32[1]{0:T(128)} %get-tuple-element.269.idx, bf16[1,512,768]{2,1,0:T(8,128)(2,1)} %collective-permute-done.1.q_ref, bf16[8,768,1536]{2,1,0:T(8,128)(2,1)} %bitcast.81, bf16[8,768,1536]{2,1,0:T(8,128)(2,1)} %bitcast.82), custom_call_target="tpu_custom_call" | custom-call | flops 4831838208 | bytes 3932160 | tf_op jit(solution)/shard_map/pallas_call | solution.py:100
  154.8 9.3 %shard_map.269 = (bf16[1,512,768]{2,1,0:T(8,128)(2,1)}, f32[1,6,2,512]{3,2,1,0:T(2,128)}, f32[1,6,2,2,512]{4,3,2,1,0:T(2,128)}) custom-call(s32[1]{0:T(128)} %get-tuple-element.268.idx, bf16[1,512,768]{2,1,0:T(8,128)(2,1)} %copy-done.10, bf16[8,768,1536]{2,1,0:T(8,128)(2,1)} %bitcast.83, bf16[8,768,1536]{2,1,0:T(8,128)(2,1)} %bitcast.84), custom_call_target="tpu_custom_call" | custom-call | flops 4831838208 | bytes 3932160 | tf_op jit(solution)/shard_map/pallas_call | solution.py:100
  165.3 9.4 %shard_map.270 = (bf16[1,512,768]{2,1,0:T(8,128)(2,1)}, f32[1,6,2,512]{3,2,1,0:T(2,128)}, f32[1,6,2,2,512]{4,3,2,1,0:T(2,128)}) custom-call(s32[1]{0:T(128)} %get-tuple-element.270.idx, bf16[1,512,768]{2,1,0:T(8,128)(2,1)} %collective-permute-done.q_ref, bf16[8,768,1536]{2,1,0:T(8,128)(2,1)} %bitcast.85, bf16[8,768,1536]{2,1,0:T(8,128)(2,1)} %bitcast.86), custom_call_target="tpu_custom_call" | custom-call | flops 4831838208 | bytes 3932160 | tf_op jit(solution)/shard_map/pallas_call | solution.py:100
  180.0 9.6 %shard_map.272 = (bf16[1,512,768]{2,1,0:T(8,128)(2,1)}, f32[1,6,2,512]{3,2,1,0:T(2,128)}, f32[1,6,2,2,512]{4,3,2,1,0:T(2,128)}) custom-call(s32[1]{0:T(128)} %get-tuple-element.267.idx, bf16[1,512,768]{2,1,0:T(8,128)(2,1)} %copy-done.9, bf16[8,768,1536]{2,1,0:T(8,128)(2,1)} %bitcast.87, bf16[8,768,1536]{2,1,0:T(8,128)(2,1)} %bitcast.88), custom_call_target="tpu_custom_call" | custom-call | flops 4831838208 | bytes 3932160 | tf_op jit(solution)/shard_map/pallas_call | solution.py:100
  193.3 2.9 shard_map.273
  198.3 15.8 %shard_map.274 = (bf16[2,512,768]{2,1,0:T(8,128)(2,1)}, f32[2,6,2,512]{3,2,1,0:T(2,128)}, f32[2,6,2,2,512]{4,3,2,1,0:T(2,128)}) custom-call(s32[2]{0:T(128)} %iota_add_fusion.3.idx, bf16[2,512,768]{2,1,0:T(8,128)(2,1)} %bitcast.10.q_ref, bf16[8,768,1536]{2,1,0:T(8,128)(2,1)} %bitcast.90, bf16[8,768,1536]{2,1,0:T(8,128)(2,1)} %bitcast.89), custom_call_target="tpu_custom_call" | custom-call | flops 9663676416 | bytes 7864320 | tf_op jit(solution)/shard_map/pallas_call | solution.py:100
  219.2 9.5 %collective-permute-done.13 = f32[1,6,2,512]{3,2,1,0:T(2,128)S(1)} collective-permute-done((f32[1,6,2,512]{3,2,1,0:T(2,128)}, f32[1,6,2,512]{3,2,1,0:T(2,128)S(1)}, u32[]{:S(2)}, u32[]{:S(2)}) %collective-permute-start.13) | collective-permute-done | bytes 24608 | tf_op jit(solution)/shard_map/ppermute | solution.py:794
  232.6 4.9 shard_map.275
  237.6 46.3 %shard_map.276 = (bf16[1024,768]{1,0:T(8,128)(2,1)}, f32[1024,768]{1,0:T(8,128)}, bf16[1024,768]{1,0:T(8,128)(2,1)}, f32[1,768]{1,0:T(1,128)}, bf16[768,3840]{1,0:T(8,128)(2,1)}, /*index=5*/bf16[3072,768]{1,0:T(8,128)(2,1)}) custom-call(f32[1024,768]{1,0:T(8,128)} %bitcast.105, bf16[1024,768]{1,0:T(8,128)(2,1)} %bitcast.133, bf16[1024,768]{1,0:T(8,128)(2,1)} %bitcast.132, ...), custom_call_target="tpu_custom_call" | custom-call | flops 32614907904 | bytes 53477376 | tf_op jit(solution)/shard_map/pallas_call | solution.py:493
  290.8 4.0 shard_map.277.stat_ref
  298.3 28.8 %shard_map.278 = (bf16[2,512,768]{2,1,0:T(8,128)(2,1)}, bf16[8,768,1536]{2,1,0:T(8,128)(2,1)}) custom-call(s32[2]{0:T(128)} %iota_add_fusion.3.idx, bf16[2,512,768]{2,1,0:T(8,128)(2,1)} %bitcast.10.q_ref, bf16[8,768,1536]{2,1,0:T(8,128)(2,1)} %bitcast.91, bf16[8,768,1536]{2,1,0:T(8,128)(2,1)} %bitcast.92, bf16[2,512,768]{2,1,0:T(8,128)(2,1)} %bitcast.119, ...), custom_call_target="tpu_custom_call" | custom-call | flops 24159191040 | bytes 14155776 | tf_op jit(solution)/shard_map/pallas_call | solution.py:170
  328.8 4.6 collective-permute-done.18
  334.2 29.0 %shard_map.279 = (bf16[2,512,768]{2,1,0:T(8,128)(2,1)}, bf16[8,768,1536]{2,1,0:T(8,128)(2,1)}) custom-call(s32[2]{0:T(128)} %iota_add_fusion.idx, bf16[2,512,768]{2,1,0:T(8,128)(2,1)} %collective-permute-done.2.q_ref, bf16[8,768,1536]{2,1,0:T(8,128)(2,1)} %bitcast.93, bf16[8,768,1536]{2,1,0:T(8,128)(2,1)} %bitcast.94, ...), custom_call_target="tpu_custom_call", output_to_operand_aliasing={{1}: (6, {})} | custom-call | flops 24159191040 | bytes 14155776 | tf_op jit(solution)/shard_map/pallas_call | solution.py:170
  371.4 16.2 %shard_map.280 = (bf16[1,512,768]{2,1,0:T(8,128)(2,1)}, bf16[8,768,1536]{2,1,0:T(8,128)(2,1)}) custom-call(s32[1]{0:T(128)} %get-tuple-element.268.idx, bf16[1,512,768]{2,1,0:T(8,128)(2,1)} %copy-done.10, bf16[8,768,1536]{2,1,0:T(8,128)(2,1)} %bitcast.95, bf16[8,768,1536]{2,1,0:T(8,128)(2,1)} %bitcast.96, ...), custom_call_target="tpu_custom_call", output_to_operand_aliasing={{1}: (6, {})} | custom-call | flops 12079595520 | bytes 7077888 | tf_op jit(solution)/shard_map/pallas_call | solution.py:170
  387.6 16.1 %shard_map.281 = (bf16[1,512,768]{2,1,0:T(8,128)(2,1)}, bf16[8,768,1536]{2,1,0:T(8,128)(2,1)}) custom-call(s32[1]{0:T(128)} %get-tuple-element.269.idx, bf16[1,512,768]{2,1,0:T(8,128)(2,1)} %collective-permute-done.1.q_ref, bf16[8,768,1536]{2,1,0:T(8,128)(2,1)} %bitcast.97, bf16[8,768,1536]{2,1,0:T(8,128)(2,1)} %bitcast.98, ...), custom_call_target="tpu_custom_call", output_to_operand_aliasing={{1}: (6, {})} | custom-call | flops 12079595520 | bytes 7077888 | tf_op jit(solution)/shard_map/pallas_call | solution.py:170
  408.0 16.1 %shard_map.282 = (bf16[1,512,768]{2,1,0:T(8,128)(2,1)}, bf16[8,768,1536]{2,1,0:T(8,128)(2,1)}) custom-call(s32[1]{0:T(128)} %get-tuple-element.267.idx, bf16[1,512,768]{2,1,0:T(8,128)(2,1)} %copy-done.9, bf16[8,768,1536]{2,1,0:T(8,128)(2,1)} %bitcast.99, bf16[8,768,1536]{2,1,0:T(8,128)(2,1)} %bitcast.100, ...), custom_call_target="tpu_custom_call", output_to_operand_aliasing={{1}: (6, {})} | custom-call | flops 12079595520 | bytes 7077888 | tf_op jit(solution)/shard_map/pallas_call | solution.py:170
  424.3 16.5 %shard_map.283 = (bf16[1,512,768]{2,1,0:T(8,128)(2,1)}, bf16[8,768,1536]{2,1,0:T(8,128)(2,1)}) custom-call(s32[1]{0:T(128)} %get-tuple-element.270.idx, bf16[1,512,768]{2,1,0:T(8,128)(2,1)} %collective-permute-done.q_ref, bf16[8,768,1536]{2,1,0:T(8,128)(2,1)} %bitcast.101, bf16[8,768,1536]{2,1,0:T(8,128)(2,1)} %bitcast.102, ...), custom_call_target="tpu_custom_call", output_to_operand_aliasing={{1}: (6, {})} | custom-call | flops 12079595520 | bytes 7077888 | tf_op jit(solution)/shard_map/pallas_call | solution.py:170
  443.1 22.7 %convolution_convert_fusion = bf16[1536,768]{0,1:T(8,128)(2,1)} fusion(bf16[6144,1536]{1,0:T(8,128)(2,1)} %bitcast.103, bf16[6144,768]{1,0:T(8,128)(2,1)} %bitcast.129), kind=kOutput, calls=%fused_computation.4 | convolution fusion | flops 14496694272 | bytes 30670848 | tf_op jit(solution)/shard_map/dot_general | solution.py:29
  465.8 21.2 %fusion.2 = f32[8,2,384,768]{3,2,1,0:T(8,128)} fusion(bf16[8,2,384,1536]{3,2,1,0:T(8,128)(2,1)} %bitcast.104, bf16[768,1536]{1,0:T(8,128)(2,1)S(1)} %copy-done.59), kind=kOutput, calls=%fused_computation.20 | convolution fusion | flops 14495514624 | bytes 40108032 | tf_op jit(solution)/shard_map/dot_general | solution.py:29
  488.4 4.7 multiply_reduce_fusion
  497.0 24.5 %shard_map.284 = bf16[2,512,2304]{2,1,0:T(8,128)(2,1)} custom-call(s32[2]{0:T(128)} %length_ref.3, bf16[2,512,2304]{2,1,0:T(8,128)(2,1)} %bitcast.139, bf16[2,512,2304]{2,1,0:T(8,128)(2,1)} %bitcast.140, bf16[2,512,2304]{2,1,0:T(8,128)(2,1)} %bitcast.141, bf16[2,512,768]{2,1,0:T(8,128)(2,1)} %bitcast.143, f32[2,6,2,512]{3,2,1,0:T(2,128)} %get-tuple-element.154.lse_ref), custom_call_target="tpu_custom_call" | custom-call | flops 16106127360 | bytes 12582912 | tf_op jit(solution)/shard_map/pallas_call | solution.py:300
  521.6 7.3 %multiply_reduce_fusion.1 = (bf16[768]{0:T(1024)(128)(2,1)S(1)}, f32[2,512]{1,0:T(2,128)S(1)}, f32[2,512,768]{2,1,0:T(8,128)S(1)}) fusion(bf16[2,512,768]{2,1,0:T(8,128)(2,1)S(1)} %copy-done.3, f32[2,512]{1,0:T(2,128)S(1)} %copy-done.38, f32[2,768]{1,0:T(2,128)S(1)} %copy-done.26, f32[768]{0:T(1024)S(1)} %copy-done.34, ...), kind=kOutput, calls=%fused_computation.6 | convolution fusion | flops 3630168320 | bytes 12995072 | tf_op jit(solution)/shard_map/dot_general | solution.py:29
  533.3 4.5 bitcast_convert_fusion.2
  537.8 4.1 bitcast_convert_fusion.1
  541.9 7.7 %bitcast_convert_fusion = bf16[768,2304]{1,0:T(8,128)(2,1)} fusion(bf16[2,512,768]{2,1,0:T(8,128)(2,1)S(1)} %copy-done.15, bf16[2,512,2304]{2,1,0:T(8,128)(2,1)} %shard_map.284), kind=kOutput, calls=%fused_computation.2 | convolution fusion | flops 3625648128 | bytes 9830400 | tf_op jit(solution)/shard_map/dot_general | solution.py:29
  549.6 44.6 %shard_map.285 = f32[24,5504]{1,0:T(8,128)} custom-call(bf16[2,2,2,2,2,24,2304]{6,5,4,3,2,1,0:T(8,128)(2,1)} %bitcast.113, bf16[2,2,2,2,2,24,768]{6,5,4,3,2,1,0:T(8,128)(2,1)} %bitcast.122, bf16[2,2,2,2,2,24,768]{6,5,4,3,2,1,0:T(8,128)(2,1)} %bitcast.112, bf16[2,2,2,2,2,24,1536]{6,5,4,3,2,1,0:T(8,128)(2,1)} %bitcast.115, ...), custom_call_target="tpu_custom_call" | custom-call | tf_op jit(solution)/shard_map/pallas_call | solution.py:724
  (295 shorter events, 90.6 us)
Async XLA Ops:
  7.2 100.4 %all-gather.3.cloned.1.call-start = ((), (), s32[]{:S(2)}) async-start(), calls=%async_computation.2 | async-start | bytes 2433024 | tf_op jit(solution)/shard_map/all_gather | solution.py:812
  7.9 206.2 %all-gather.5.cloned.1.call-start = ((), (), s32[]{:S(2)}) async-start(), calls=%async_computation.3 | async-start | bytes 10948608 | tf_op jit(solution)/shard_map/all_gather | solution.py:836
  68.4 419.9 %reduce-scatter.3.cloned.1.call-start = ((), (), s32[]{:S(2)}) async-start(), calls=%async_computation.4 | async-start | bytes 4866048 | tf_op jit(solution)/shard_map/reduce_scatter | solution.py:890
  102.0 25.4 %collective-permute-start.2 = (bf16[2,512,768]{2,1,0:T(8,128)(2,1)}, bf16[2,512,768]{2,1,0:T(8,128)(2,1)}, u32[]{:S(2)}, u32[]{:S(2)}) collective-permute-start(bf16[2,512,768]{2,1,0:T(8,128)(2,1)} %bitcast.10.q_ref), channel_id=1, source_target_pairs={{0,1},{1,0},{2,3},{3,2},{4,5},{5,4},{6,7},{7,6},{8,9},{9,8},{10,11... | collective-permute-start | bytes 4718600 | tf_op jit(solution)/shard_map/ppermute | solution.py:790
  105.1 38.2 %collective-permute-start.1 = (bf16[1,512,768]{2,1,0:T(8,128)(2,1)}, bf16[1,512,768]{2,1,0:T(8,128)(2,1)}, u32[]{:S(2)}, u32[]{:S(2)}) collective-permute-start(bf16[1,512,768]{2,1,0:T(8,128)(2,1)} %get-tuple-element.251), channel_id=1, source_target_pairs={{0,2},{1,3},{2,0},{3,1},{4,6},{5,7},{6,4},{7,5},{8,10},{9,11},{10,... | collective-permute-start | bytes 2359304 | tf_op jit(solution)/shard_map/ppermute | solution.py:794
  106.8 57.9 %collective-permute-start = (bf16[1,512,768]{2,1,0:T(8,128)(2,1)}, bf16[1,512,768]{2,1,0:T(8,128)(2,1)}, u32[]{:S(2)}, u32[]{:S(2)}) collective-permute-start(bf16[1,512,768]{2,1,0:T(8,128)(2,1)} %get-tuple-element.252), channel_id=1, source_target_pairs={{0,2},{1,3},{2,0},{3,1},{4,6},{5,7},{6,4},{7,5},{8,10},{9,11},{10,... | collective-permute-start | bytes 2359304 | tf_op jit(solution)/shard_map/ppermute | solution.py:794
  143.3 10.6 %collective-permute-start.3 = (bf16[1,512,768]{2,1,0:T(8,128)(2,1)}, bf16[1,512,768]{2,1,0:T(8,128)(2,1)S(1)}, u32[]{:S(2)}, u32[]{:S(2)}) collective-permute-start(bf16[1,512,768]{2,1,0:T(8,128)(2,1)} %collective-permute-done.1.q_ref), channel_id=1, source_target_pairs={{0,1},{1,0},{2,3},{3,2},{4,5},{5,4},{6,7},{7,6},{8,9},{9,8},{10,11... | collective-permute-start | bytes 2359304 | tf_op jit(solution)/shard_map/ppermute | solution.py:790
  164.1 10.5 %collective-permute-start.5 = (bf16[1,512,768]{2,1,0:T(8,128)(2,1)}, bf16[1,512,768]{2,1,0:T(8,128)(2,1)S(1)}, u32[]{:S(2)}, u32[]{:S(2)}) collective-permute-start(bf16[1,512,768]{2,1,0:T(8,128)(2,1)} %get-tuple-element.98), channel_id=1, source_target_pairs={{0,1},{1,0},{2,3},{3,2},{4,5},{5,4},{6,7},{7,6},{8,9},{9,8},{10,11... | collective-permute-start | bytes 2359304 | tf_op jit(solution)/shard_map/ppermute | solution.py:790
  164.8 14.3 %collective-permute-start.4 = (bf16[1,512,768]{2,1,0:T(8,128)(2,1)}, bf16[1,512,768]{2,1,0:T(8,128)(2,1)S(1)}, u32[]{:S(2)}, u32[]{:S(2)}) collective-permute-start(bf16[1,512,768]{2,1,0:T(8,128)(2,1)} %collective-permute-done.q_ref), channel_id=1, source_target_pairs={{0,1},{1,0},{2,3},{3,2},{4,5},{5,4},{6,7},{7,6},{8,9},{9,8},{10,11... | collective-permute-start | bytes 2359304 | tf_op jit(solution)/shard_map/ppermute | solution.py:790
  164.8 9.8 %collective-permute-start.6 = (f32[1,6,2,512]{3,2,1,0:T(2,128)}, f32[1,6,2,512]{3,2,1,0:T(2,128)S(1)}, u32[]{:S(2)}, u32[]{:S(2)}) collective-permute-start(f32[1,6,2,512]{3,2,1,0:T(2,128)} %get-tuple-element.99), channel_id=1, source_target_pairs={{0,1},{1,0},{2,3},{3,2},{4,5},{5,4},{6,7},{7,6},{8,9},{9,8},{10,11... | collective-permute-start | bytes 73736 | tf_op jit(solution)/shard_map/ppermute | solution.py:790
  189.6 3.1 collective-permute-start.7
  189.7 3.1 collective-permute-start.8
  190.6 41.4 %collective-permute-start.9 = (bf16[2,512,768]{2,1,0:T(8,128)(2,1)}, bf16[2,512,768]{2,1,0:T(8,128)(2,1)}, u32[]{:S(2)}, u32[]{:S(2)}) collective-permute-start(bf16[2,512,768]{2,1,0:T(8,128)(2,1)} %get-tuple-element.90), channel_id=1, source_target_pairs={{0,1},{1,0},{2,3},{3,2},{4,5},{5,4},{6,7},{7,6},{8,9},{9,8},{10,11... | collective-permute-start | bytes 4718600 | tf_op jit(solution)/shard_map/ppermute | solution.py:790
  190.7 28.5 %collective-permute-start.10 = (bf16[1,512,768]{2,1,0:T(8,128)(2,1)}, bf16[1,512,768]{2,1,0:T(8,128)(2,1)}, u32[]{:S(2)}, u32[]{:S(2)}) collective-permute-start(bf16[1,512,768]{2,1,0:T(8,128)(2,1)} %get-tuple-element.105), channel_id=1, source_target_pairs={{0,2},{1,3},{2,0},{3,1},{4,6},{5,7},{6,4},{7,5},{8,10},{9,11},{10,... | collective-permute-start | bytes 2359304 | tf_op jit(solution)/shard_map/ppermute | solution.py:794
  192.4 26.8 %collective-permute-start.11 = (f32[1,6,2,512]{3,2,1,0:T(2,128)S(1)}, f32[1,6,2,512]{3,2,1,0:T(2,128)S(1)}, u32[]{:S(2)}, u32[]{:S(2)}) collective-permute-start(f32[1,6,2,512]{3,2,1,0:T(2,128)S(1)} %copy-done.62), channel_id=1, source_target_pairs={{0,2},{1,3},{2,0},{3,1},{4,6},{5,7},{6,4},{7,5},{8,10},{9,11},{10,... | collective-permute-start | bytes 73736 | tf_op jit(solution)/shard_map/ppermute | solution.py:794
  196.3 32.4 %collective-permute-start.12 = (bf16[1,512,768]{2,1,0:T(8,128)(2,1)}, bf16[1,512,768]{2,1,0:T(8,128)(2,1)}, u32[]{:S(2)}, u32[]{:S(2)}) collective-permute-start(bf16[1,512,768]{2,1,0:T(8,128)(2,1)} %get-tuple-element.109), channel_id=1, source_target_pairs={{0,2},{1,3},{2,0},{3,1},{4,6},{5,7},{6,4},{7,5},{8,10},{9,11},{10,... | collective-permute-start | bytes 2359304 | tf_op jit(solution)/shard_map/ppermute | solution.py:794
  197.9 30.8 %collective-permute-start.13 = (f32[1,6,2,512]{3,2,1,0:T(2,128)}, f32[1,6,2,512]{3,2,1,0:T(2,128)S(1)}, u32[]{:S(2)}, u32[]{:S(2)}) collective-permute-start(f32[1,6,2,512]{3,2,1,0:T(2,128)} %get-tuple-element.113), channel_id=1, source_target_pairs={{0,2},{1,3},{2,0},{3,1},{4,6},{5,7},{6,4},{7,5},{8,10},{9,11},{10,... | collective-permute-start | bytes 73736 | tf_op jit(solution)/shard_map/ppermute | solution.py:794
  219.2 12.8 %collective-permute-start.14 = (f32[2,6,2,512]{3,2,1,0:T(2,128)S(1)}, f32[2,6,2,512]{3,2,1,0:T(2,128)S(1)}, u32[]{:S(2)}, u32[]{:S(2)}) collective-permute-start(f32[2,6,2,512]{3,2,1,0:T(2,128)S(1)} %copy-done.29), channel_id=1, source_target_pairs={{0,1},{1,0},{2,3},{3,2},{4,5},{5,4},{6,7},{7,6},{8,9},{9,8},{10,11... | collective-permute-start | bytes 147464 | tf_op jit(solution)/shard_map/ppermute | solution.py:790
  283.9 265.7 %reduce-scatter.5.cloned.1.call-start = ((), (), s32[]{:S(2)}) async-start(), calls=%async_computation.5 | async-start | bytes 6082560 | tf_op jit(solution)/shard_map/reduce_scatter | solution.py:891
  286.7 3.6 collective-permute-start.27
  294.8 34.0 %collective-permute-start.19 = (f32[2,6,4,512]{3,2,1,0:T(4,128)}, f32[2,6,4,512]{3,2,1,0:T(4,128)S(1)}, u32[]{:S(2)}, u32[]{:S(2)}) collective-permute-start(f32[2,6,4,512]{3,2,1,0:T(4,128)} %shard_map.277.stat_ref), channel_id=1, source_target_pairs={{0,2},{1,3},{2,0},{3,1},{4,6},{5,7},{6,4},{7,5},{8,10},{9,11},{10,... | collective-permute-start | bytes 294920 | tf_op jit(solution)/shard_map/ppermute | solution.py:794
  296.1 31.6 %collective-permute-start.16 = (f32[2,6,4,512]{3,2,1,0:T(4,128)}, f32[2,6,4,512]{3,2,1,0:T(4,128)}, u32[]{:S(2)}, u32[]{:S(2)}) collective-permute-start(f32[2,6,4,512]{3,2,1,0:T(4,128)} %shard_map.277.stat_ref), channel_id=1, source_target_pairs={{0,1},{1,0},{2,3},{3,2},{4,5},{5,4},{6,7},{7,6},{8,9},{9,8},{10,11... | collective-permute-start | bytes 294920 | tf_op jit(solution)/shard_map/ppermute | solution.py:790
  296.1 37.2 %collective-permute-start.18 = (bf16[2,512,768]{2,1,0:T(8,128)(2,1)S(1)}, bf16[2,512,768]{2,1,0:T(8,128)(2,1)S(1)}, u32[]{:S(2)}, u32[]{:S(2)}) collective-permute-start(bf16[2,512,768]{2,1,0:T(8,128)(2,1)S(1)} %bitcast.120), channel_id=1, source_target_pairs={{0,2},{1,3},{2,0},{3,1},{4,6},{5,7},{6,4},{7,5},{8,10},{9,11},{10,... | collective-permute-start | bytes 4718600 | tf_op jit(solution)/shard_map/ppermute | solution.py:794
  296.9 36.8 %collective-permute-start.15 = (bf16[2,512,768]{2,1,0:T(8,128)(2,1)S(1)}, bf16[2,512,768]{2,1,0:T(8,128)(2,1)}, u32[]{:S(2)}, u32[]{:S(2)}) collective-permute-start(bf16[2,512,768]{2,1,0:T(8,128)(2,1)S(1)} %bitcast.121), channel_id=1, source_target_pairs={{0,1},{1,0},{2,3},{3,2},{4,5},{5,4},{6,7},{7,6},{8,9},{9,8},{10,11... | collective-permute-start | bytes 4718600 | tf_op jit(solution)/shard_map/ppermute | solution.py:790
  333.4 29.8 %collective-permute-start.21 = (f32[2,6,4,512]{3,2,1,0:T(4,128)S(1)}, f32[2,6,4,512]{3,2,1,0:T(4,128)S(1)}, u32[]{:S(2)}, u32[]{:S(2)}) collective-permute-start(f32[2,6,4,512]{3,2,1,0:T(4,128)S(1)} %collective-permute-done.19), channel_id=1, source_target_pairs={{0,1},{1,0},{2,3},{3,2},{4,5},{5,4},{6,7},{7,6},{8,9},{9,8},{10,11... | collective-permute-start | bytes 294920 | tf_op jit(solution)/shard_map/ppermute | solution.py:790
  333.6 36.1 %collective-permute-start.20 = (bf16[2,512,768]{2,1,0:T(8,128)(2,1)S(1)}, bf16[2,512,768]{2,1,0:T(8,128)(2,1)S(1)}, u32[]{:S(2)}, u32[]{:S(2)}) collective-permute-start(bf16[2,512,768]{2,1,0:T(8,128)(2,1)S(1)} %collective-permute-done.18), channel_id=1, source_target_pairs={{0,1},{1,0},{2,3},{3,2},{4,5},{5,4},{6,7},{7,6},{8,9},{9,8},{10,11... | collective-permute-start | bytes 4718600 | tf_op jit(solution)/shard_map/ppermute | solution.py:790
  365.3 3.9 collective-permute-start.30
  367.2 121.1 %collective-permute-start.17 = (bf16[2,512,768]{2,1,0:T(8,128)(2,1)}, bf16[2,512,768]{2,1,0:T(8,128)(2,1)}, u32[]{:S(2)}, u32[]{:S(2)}) collective-permute-start(bf16[2,512,768]{2,1,0:T(8,128)(2,1)} %get-tuple-element.133), channel_id=1, source_target_pairs={{0,1},{1,0},{2,3},{3,2},{4,5},{5,4},{6,7},{7,6},{8,9},{9,8},{10,11... | collective-permute-start | bytes 4718600 | tf_op jit(solution)/shard_map/ppermute | solution.py:790
  387.5 16.1 %collective-permute-start.22 = (bf16[1,512,768]{2,1,0:T(8,128)(2,1)}, bf16[1,512,768]{2,1,0:T(8,128)(2,1)S(1)}, u32[]{:S(2)}, u32[]{:S(2)}) collective-permute-start(bf16[1,512,768]{2,1,0:T(8,128)(2,1)} %get-tuple-element.141), channel_id=1, source_target_pairs={{0,1},{1,0},{2,3},{3,2},{4,5},{5,4},{6,7},{7,6},{8,9},{9,8},{10,11... | collective-permute-start | bytes 2359304 | tf_op jit(solution)/shard_map/ppermute | solution.py:790
  405.0 82.0 %collective-permute-start.23 = (bf16[1,512,768]{2,1,0:T(8,128)(2,1)S(1)}, bf16[1,512,768]{2,1,0:T(8,128)(2,1)S(1)}, u32[]{:S(2)}, u32[]{:S(2)}) collective-permute-start(bf16[1,512,768]{2,1,0:T(8,128)(2,1)S(1)} %add_convert_fusion.2), channel_id=1, source_target_pairs={{0,2},{1,3},{2,0},{3,1},{4,6},{5,7},{6,4},{7,5},{8,10},{9,11},{10,... | collective-permute-start | bytes 2359304 | tf_op jit(solution)/shard_map/ppermute | solution.py:794
  424.1 16.7 %collective-permute-start.24 = (bf16[1,512,768]{2,1,0:T(8,128)(2,1)}, bf16[1,512,768]{2,1,0:T(8,128)(2,1)S(1)}, u32[]{:S(2)}, u32[]{:S(2)}) collective-permute-start(bf16[1,512,768]{2,1,0:T(8,128)(2,1)} %get-tuple-element.147), channel_id=1, source_target_pairs={{0,1},{1,0},{2,3},{3,2},{4,5},{5,4},{6,7},{7,6},{8,9},{9,8},{10,11... | collective-permute-start | bytes 2359304 | tf_op jit(solution)/shard_map/ppermute | solution.py:790
  442.2 44.9 %collective-permute-start.25 = (bf16[1,512,768]{2,1,0:T(8,128)(2,1)S(1)}, bf16[1,512,768]{2,1,0:T(8,128)(2,1)S(1)}, u32[]{:S(2)}, u32[]{:S(2)}) collective-permute-start(bf16[1,512,768]{2,1,0:T(8,128)(2,1)S(1)} %add_convert_fusion.1), channel_id=1, source_target_pairs={{0,2},{1,3},{2,0},{3,1},{4,6},{5,7},{6,4},{7,5},{8,10},{9,11},{10,... | collective-permute-start | bytes 2359304 | tf_op jit(solution)/shard_map/ppermute | solution.py:794
  (66 other events, 1109.0 us)
Sparse Core Ops, SparseCore 0:
  10.9 69.0 all-gather.2
  83.0 94.3 all-gather.4
  284.0 107.8 reduce-scatter.2
  398.4 121.0 reduce-scatter.4
